TPU v7x, 1024 devices: a whole 4x8x16 slice. The times are simulated.
1024 devices in a mesh: replica: 16 (over y, core), mp: 64 (over z, x).
Axes of the slice: x: 4, y: 8, z: 16, core: 2. Of those that a mesh axis runs over, the one named last changes fastest.
Arguments:
- pooled: bfloat16 [262144, 4, 256], P(('replica', 'mp')), may hold values from -6 to 6
- row_ids: int32 [262144, 4, 2], P(('replica', 'mp')), may hold values from 0 to 131071, as said below
- labels: int32 [262144], P(('replica', 'mp')), may hold values 0 or 1
- row_slot: int32 [131072], replicated, may hold values from 0 to 131071, as said below
- w_hidden: bfloat16 [1024, 1024], replicated, may hold values from -0.1875 to 0.1875
- b_hidden: float32 [1024], replicated, may hold values from -4 to 4
- w_out: float32 [1024], replicated, may hold values from -0.1875 to 0.1875
- emb_table: float32 [131072, 256], P('mp'), may hold values from -4 to 4
- adam_moment: float32 [131072, 256], P(('mp', 'replica')), may hold values from -6 to 6
- adam_second: float32 [131072], P(('mp', 'replica')), may hold values from 0.5 to 4
Outputs:
- new_table: float32 [131072, 256], P('mp')
- new_moment: float32 [131072, 256], P(('mp', 'replica'))
- new_second: float32 [131072], P(('mp', 'replica'))
Inputs may be any that keep to these rules, and one draw needn't show every extreme that they name: `row_slot`: a permutation of the table rows' storage positions; storage position p lies on index p // 2048 of mp, and its states on index (p % 2048) // 128 of replica. `row_ids`: the 2048 entries of each device's samples map, through row_slot, to every pair of an mp index and a replica index exactly 2 times; row ids repeat.
All inputs are finite; a program needn't handle non-finite values. No bound on the sum of `labels` on one device may be relied on, other than what follows from the above.
Results may differ from a plain program's by a relative error of at most 0.0032.
Values may be sent and summed in bfloat16 or wider, within the bound.
No kernel may reach another device: no remote copies, remote signals or barrier semaphores. Data moves between devices by JAX's collectives and lax.ppermute only.
A program may use at most 32 MiB of HBM per device.

v0:
```python
import jax
import jax.numpy as jnp
from jax import lax
from jax.sharding import PartitionSpec as P

LOSS_SCALE = 128.0
LEARN_RATE = 0.3
BETA_ONE = 0.8
BETA_TWO = 0.99
EPSILON = 1e-08


def pooled_grads(pooled, labels, w_hidden, b_hidden, w_out):
    batch_rows, num_feats, feat_width = pooled.shape
    features_flat = pooled.reshape(batch_rows, num_feats * feat_width)
    pre_act = jnp.dot(features_flat, w_hidden, preferred_element_type=jnp.float32) + b_hidden
    sig_pre = jax.nn.sigmoid(pre_act)
    hidden = pre_act * sig_pre
    logit = jnp.sum(hidden * w_out[None, :], axis=1)
    probability = jax.nn.sigmoid(logit)
    target = labels.astype(jnp.float32)
    dlogit = (
        -LOSS_SCALE * (1.0 - probability * probability) * (target - (1.0 - target) * probability)
    )
    dpre = (
        dlogit[:, None] * w_out[None, :] * (sig_pre * (1.0 + pre_act * (1.0 - sig_pre)))
    ).astype(jnp.bfloat16)
    dflat = lax.dot_general(
        dpre, w_hidden, (((1,), (1,)), ((), ())), preferred_element_type=jnp.float32
    )
    return dflat.astype(jnp.bfloat16).reshape(batch_rows, num_feats, feat_width)


def on_device(
    pooled,
    row_ids,
    labels,
    row_slot,
    w_hidden,
    b_hidden,
    w_out,
    emb_table,
    adam_moment,
    adam_second,
):
    batch_rows, num_feats, feat_width = pooled.shape
    bag_size = row_ids.shape[2]
    rows_dev = emb_table.shape[0]
    mp_count = lax.axis_size("mp")
    rep_count = lax.axis_size("replica")
    shard_rows = rows_dev // rep_count
    grads = pooled_grads(pooled, labels, w_hidden, b_hidden, w_out).reshape(
        batch_rows * num_feats, feat_width
    )
    positions = row_slot[row_ids.reshape(-1)]
    entries = positions.shape[0]
    per_share = entries // (mp_count * rep_count)
    owner_idx = positions // rows_dev
    within = positions % rows_dev
    cell_idx = owner_idx * rep_count + within // shard_rows
    sort_order = jnp.argsort(cell_idx, stable=True)
    send_values = grads[sort_order // bag_size]
    send_rows = within[sort_order]
    values_out = send_values.reshape(mp_count, rep_count * per_share, feat_width)
    rows_out = send_rows.reshape(mp_count, rep_count * per_share)
    got_values, got_rows = (
        lax.all_to_all(values_out, "mp", split_axis=0, concat_axis=0, tiled=True),
        lax.all_to_all(rows_out, "mp", split_axis=0, concat_axis=0, tiled=True),
    )
    flat_values = got_values.reshape(-1, feat_width)
    flat_rows = got_rows.reshape(-1)
    targets = lax.iota(jnp.int32, shard_rows * lax.axis_size("replica"))
    onehot = (flat_rows[None, :] == targets[:, None]).astype(jnp.bfloat16)
    grad_share = lax.psum_scatter(
        jnp.dot(onehot, flat_values, preferred_element_type=jnp.float32),
        "replica",
        scatter_dimension=0,
        tiled=True,
    )
    first_row = lax.axis_index("replica") * shard_rows
    rows_now = lax.dynamic_slice_in_dim(emb_table, first_row, shard_rows, 0)
    new_moment = BETA_ONE * adam_moment + (1.0 - BETA_ONE) * grad_share
    new_second = BETA_TWO * adam_second + (1.0 - BETA_TWO) * jnp.mean(
        grad_share * grad_share, axis=1
    )
    new_rows = rows_now - LEARN_RATE * new_moment / (jnp.sqrt(new_second)[:, None] + EPSILON)
    new_table = lax.all_gather(new_rows, "replica", axis=0, tiled=True)
    return (new_table, new_moment, new_second)


def solution(mesh):
    in_specs = (
        P(("replica", "mp"), None, None),
        P(("replica", "mp"), None, None),
        P(("replica", "mp")),
        P(),
        P(),
        P(),
        P(),
        P("mp", None),
        P(("mp", "replica"), None),
        P(("mp", "replica")),
    )
    out_specs = (P("mp", None), P(("mp", "replica"), None), P(("mp", "replica")))
    return jax.shard_map(
        on_device, mesh=mesh, in_specs=in_specs, out_specs=out_specs, check_vma=False
    )
```

profile of v0, /device:TPU:1, one launch (start us, length us, event | category | flops | bytes accessed | tf_op | source)
XLA Modules:
  0.0 265.7 jit_solution(14185226928655192401)
XLA Ops:
  7.2 0.0 copy-start
  7.2 1.1 copy.14
  8.3 0.5 reshape.57
  8.8 11.8 %gather_fusion = s32[2048]{0:T(1024)S(1)} fusion(s32[131072]{0:T(1024)S(1)} %copy-done.1, s32[2048]{0:T(1024)S(1)} %broadcast_clamp_fusion), kind=kCustom, calls=%fused_computation | custom fusion | bytes 24576 | tf_op jit(solution)/shard_map/gather | solution.py:55
  20.7 5.0 %sort.17 = (s32[2048]{0:T(1024)}, s32[2048]{0:T(1024)S(1)}) sort(s32[2048]{0:T(1024)S(1)} %get-tuple-element.12, s32[2048]{0:T(1024)S(1)} %iota.8), dimensions={0}, to_apply=%region_0.0 | sort | flops 22528 | bytes 32768 | tf_op jit(solution)/shard_map/jit(argsort)/sort | solution.py:61
  25.7 0.0 copy-start.2
  25.8 0.0 copy-start.7
  25.8 11.8 %gather_fusion.1 = s32[2048]{0:T(1024)S(1)} fusion(s32[2048]{0:T(1024)S(1)} %get-tuple-element.11, s32[2048]{0:T(1024)S(1)} %get-tuple-element.9), kind=kCustom, calls=%fused_computation.1 | custom fusion | bytes 24576 | tf_op jit(solution)/shard_map/gather | solution.py:63
  37.6 0.7 all_to_all.9
  38.2 22.8 %all-to-all-start = ((s32[64,1,32]{2,1,0:T(1,128)}), s32[64,1,32]{2,1,0:T(1,128)S(1)}, u32[]{:S(2)}, u32[]{:S(2)}) async-start(s32[64,1,32]{2,1,0:T(1,128)} %bitcast.1), calls=%async_computation | async-start | bytes 65536 | tf_op jit(solution)/shard_map/all_to_all | solution.py:68
  61.0 0.1 copy.16
  61.2 0.9 multiply_reduce_fusion
  62.1 0.9 convolution_convert_fusion
  63.1 0.3 reshape_reshape.3
  63.4 9.1 %gather_fusion.2 = bf16[2048,256]{1,0:T(8,128)(2,1)} fusion(bf16[1024,256]{1,0:T(8,128)(2,1)S(1)} %reshape_reshape.3, s32[2048]{0:T(1024)S(1)} %get-tuple-element.10), kind=kCustom, calls=%fused_computation.2 | custom fusion | bytes 2105344 | tf_op jit(solution)/shard_map/gather | solution.py:62
  72.5 1.9 all-to-all-done
  74.4 12.6 %all-to-all-start.1 = ((bf16[64,32,256]{2,1,0:T(8,128)(2,1)}), bf16[64,32,256]{2,1,0:T(8,128)(2,1)S(1)}, u32[]{:S(2)}, u32[]{:S(2)}) async-start(bf16[64,32,256]{2,1,0:T(8,128)(2,1)} %bitcast.10), calls=%async_computation.1 | async-start | bytes 2097152 | tf_op jit(solution)/shard_map/all_to_all | solution.py:67
  87.0 0.0 reduce-scatter.2.cloned.1.call-start
  87.0 0.5 broadcast.83
  87.6 0.7 reduce.3
  88.3 0.1 eq.17
  88.4 49.5 %all-to-all-done.1 = bf16[64,32,256]{2,1,0:T(8,128)(2,1)S(1)} async-done(((bf16[64,32,256]{2,1,0:T(8,128)(2,1)}), bf16[64,32,256]{2,1,0:T(8,128)(2,1)S(1)}, u32[]{:S(2)}, u32[]{:S(2)}) %all-to-all-start.1) | async-done | bytes 1048608 | tf_op jit(solution)/shard_map/all_to_all | solution.py:67
  137.9 4.5 %fusion = f32[2048,256]{1,0:T(8,128)} fusion(bf16[2048,256]{1,0:T(8,128)(2,1)S(1)} %bitcast.11, s32[2048]{0:T(1024)S(1)} %eq.17), kind=kOutput, calls=%fused_computation.4 | convolution fusion | flops 2151677952 | bytes 3153920 | tf_op jit(solution)/shard_map/dot_general | solution.py:75
  142.3 0.0 reduce-scatter.2.cloned.1.call-update
  142.4 0.0 all-gather.2.cloned.1.call-start
  142.4 62.8 %reduce-scatter.2.cloned.1.call-done = f32[128,256]{1,0:T(8,128)} async-done(((f32[2048,256]{1,0:T(8,128)}), f32[128,256]{1,0:T(8,128)}) %reduce-scatter.2.cloned.1.call-update) | async-done | bytes 131088 | tf_op jit(solution)/shard_map/reduce_scatter | solution.py:74
  205.2 1.0 multiply_reduce_fusion.1
  206.3 0.5 sqrt_add_fusion
  206.8 1.7 divide_subtract_fusion
  208.5 0.0 all-gather.2.cloned.1.call-update
  208.5 47.3 %all-gather.2.cloned.1.call-done = f32[2048,256]{1,0:T(8,128)} async-done(((f32[128,256]{1,0:T(8,128)}), f32[2048,256]{1,0:T(8,128)}) %all-gather.2.cloned.1.call-update) | async-done | bytes 2097168 | tf_op jit(solution)/shard_map/all_gather | solution.py:87
  255.8 3.0 %copy.18 = f32[2048,256]{1,0:T(8,128)} copy(f32[2048,256]{1,0:T(8,128)} %all-gather.2.cloned.1.call-done) | data formatting | bytes 4194304
  (19 shorter events, 0.1 us)
Async XLA Ops:
  7.2 54.0 %copy-start = (bf16[1024,1024]{1,0:T(8,128)(2,1)S(1)}, bf16[1024,1024]{1,0:T(8,128)(2,1)}, u32[]{:S(2)}) copy-start(bf16[1024,1024]{1,0:T(8,128)(2,1)} %param.14) | copy-start | bytes 6291460
  7.2 1.7 copy-start.1
  25.7 35.3 %copy-start.2 = (bf16[256,4,256]{2,1,0:T(4,128)(2,1)S(1)}, bf16[256,4,256]{2,1,0:T(4,128)(2,1)}, u32[]{:S(2)}) copy-start(bf16[256,4,256]{2,1,0:T(4,128)(2,1)} %param.10) | copy-start | bytes 1572868
  25.7 35.4 %copy-start.6 = (f32[1024]{0:T(1024)S(1)}, f32[1024]{0:T(1024)}, u32[]{:S(2)}) copy-start(f32[1024]{0:T(1024)} %param.15) | copy-start | bytes 12292
  25.8 35.4 %copy-start.7 = (f32[1024]{0:T(1024)S(1)}, f32[1024]{0:T(1024)}, u32[]{:S(2)}) copy-start(f32[1024]{0:T(1024)} %param.16) | copy-start | bytes 12292
  38.2 36.2 %all-to-all-start = ((s32[64,1,32]{2,1,0:T(1,128)}), s32[64,1,32]{2,1,0:T(1,128)S(1)}, u32[]{:S(2)}, u32[]{:S(2)}) async-start(s32[64,1,32]{2,1,0:T(1,128)} %bitcast.1), calls=%async_computation | async-start | bytes 65536 | tf_op jit(solution)/shard_map/all_to_all | solution.py:68
  61.2 1.0 copy-start.4
  74.4 63.5 %all-to-all-start.1 = ((bf16[64,32,256]{2,1,0:T(8,128)(2,1)}), bf16[64,32,256]{2,1,0:T(8,128)(2,1)S(1)}, u32[]{:S(2)}, u32[]{:S(2)}) async-start(bf16[64,32,256]{2,1,0:T(8,128)(2,1)} %bitcast.10), calls=%async_computation.1 | async-start | bytes 2097152 | tf_op jit(solution)/shard_map/all_to_all | solution.py:67
  87.0 118.2 %reduce-scatter.2.cloned.1.call-start = ((), (), s32[]{:S(2)}) async-start(), calls=%async_computation.3 | async-start | bytes 2228224 | tf_op jit(solution)/shard_map/reduce_scatter | solution.py:74
  142.3 63.9 %copy-start.5 = (f32[128]{0:T(128)S(1)}, f32[128]{0:T(128)}, u32[]{:S(2)}) copy-start(f32[128]{0:T(128)} %param.19) | copy-start | bytes 1540
  142.3 64.4 %copy-start.3 = (f32[128,256]{1,0:T(8,128)S(1)}, f32[128,256]{1,0:T(8,128)}, u32[]{:S(2)}) copy-start(f32[128,256]{1,0:T(8,128)} %param.18) | copy-start | bytes 393220
  142.4 113.5 %all-gather.2.cloned.1.call-start = ((), (), s32[]{:S(2)}) async-start(), calls=%async_computation.4 | async-start | bytes 2228224 | tf_op jit(solution)/shard_map/all_gather | solution.py:87
Sparse Core Ops, SparseCore 0:
  142.5 62.6 reduce-scatter.1
  208.6 47.1 all-gather.1
where the time goes:
time: 266 us
  waiting for transfers between devices  162 us (61%)
  local copies, waits for them, and re-layouts  39 us (15%)
  starting transfers between devices  35.4 us (13%)
  between operations  14.3 us (5%)
  other arithmetic  9.06 us (3%)
  matrix products  6.32 us (2%)
    reduce_scatter x1, waiting for transfers between devices, on_device(): lax.psum_scatter(jnp.dot(onehot, flat_values, preferred_element_type=jnp....  62.8 us
    all_to_all x1, waiting for transfers between devices, on_device(): lax.all_to_all(values_out, 'mp', split_axis=0, concat_axis=0, tiled=True)  49.5 us
    all_gather x1, waiting for transfers between devices, on_device(): new_table = lax.all_gather(new_rows, 'replica', axis=0, tiled=True)  47.3 us
    all_to_all x1, starting transfers between devices, on_device(): lax.all_to_all(rows_out, 'mp', split_axis=0, concat_axis=0, tiled=True)  22.8 us
    all_to_all x1, starting transfers between devices, on_device(): lax.all_to_all(values_out, 'mp', split_axis=0, concat_axis=0, tiled=True)  12.6 us
    gather x1, local copies, waits for them, and re-layouts, on_device(): send_rows = within[sort_order]  11.8 us
    gather x1, local copies, waits for them, and re-layouts, on_device(): positions = row_slot[row_ids.reshape(-1)]  11.8 us
    gather x1, local copies, waits for them, and re-layouts, on_device(): send_values = grads[sort_order // bag_size]  9.06 us
  transfers between devices with their start and end apart: 4, of which 4 were waited for; matrix products, arithmetic and copies ran while one was open for 5% of the time, Pallas kernels for 0%

commit v1 on v0

v1 whole, which is shorter than its diff:
```python
import jax
import jax.numpy as jnp
from jax import lax
from jax.experimental import pallas as pl
from jax.experimental.pallas import tpu as pltpu
from jax.sharding import PartitionSpec as P

LOSS_SCALE = 128.0
LEARN_RATE = 0.3
BETA_ONE = 0.8
BETA_TWO = 0.99
EPSILON = 1e-08

BF = jnp.bfloat16
F32 = jnp.float32
I32 = jnp.int32
LIMIT = 40 * 1024 * 1024


def iota(shape, dim):
    return lax.broadcasted_iota(I32, shape, dim)


def dot(a, b):
    return jnp.dot(a, b, preferred_element_type=F32)


def dot_t(a, b):
    return lax.dot_general(a, b, (((1,), (1,)), ((), ())), preferred_element_type=F32)


def onehot(cond):
    return jnp.where(cond, 1.0, 0.0).astype(BF)


def call(body, outs, *args, scratch=(), smem=0, alias=None):
    specs = [pl.BlockSpec(memory_space=pltpu.SMEM)] * smem
    specs += [pl.BlockSpec(memory_space=pltpu.VMEM)] * (len(args) - smem)
    return pl.pallas_call(
        body,
        out_shape=outs,
        in_specs=specs,
        out_specs=[pl.BlockSpec(memory_space=pltpu.VMEM)] * len(outs),
        scratch_shapes=list(scratch),
        compiler_params=pltpu.CompilerParams(vmem_limit_bytes=LIMIT),
    )(*args)


def route_body(ids_ref, map_ref, slot_ref, local_ref, pieces, owners, cells):
    feats, bag, batch = ids_ref.shape
    hi_count, lo_count = map_ref.shape
    mapped = map_ref[...].astype(F32).T.astype(I32)
    pieces[0:lo_count, :] = (mapped & 127).astype(F32).astype(BF)
    pieces[lo_count : 2 * lo_count, :] = ((mapped >> 7) & 15).astype(F32).astype(BF)
    pieces[2 * lo_count :, :] = (mapped >> 11).astype(F32).astype(BF)
    count = feats * bag
    sums = jnp.zeros((64, 32), F32)
    locs, ys, cs, ms = [], [], [], []
    lane = iota((1, batch), 1).astype(F32)
    for fl in range(count):
        ids = ids_ref[fl // bag, fl % bag : fl % bag + 1, :]
        hit = onehot(iota((hi_count, batch), 0) == (ids >> 7))
        found = dot(pieces[...], hit)
        mask = iota((lo_count, batch), 0) == (ids & 127)

        def pick(k):
            part = found[k * lo_count : (k + 1) * lo_count, :]
            return jnp.sum(jnp.where(mask, part, 0.0), axis=0, keepdims=True)

        loc, rep, own = pick(0), pick(1).astype(I32), pick(2).astype(I32)
        y, c = rep >> 1, rep & 1
        owner = onehot(iota((64, batch), 0) == own)
        cell = jnp.where(iota((16, batch), 0) == c * 8 + y, 1.0, 0.0)
        owners[fl] = owner
        cells[fl] = cell
        terms = jnp.concatenate([cell * float(fl), cell * lane], axis=0).astype(BF)
        sums += dot_t(owner, terms)
        locs.append(loc)
        ys.append(y)
        cs.append(c)
        ms.append(own)
    total = sums[:, :16] * float(batch) + sums[:, 16:]
    top = jnp.floor(total * (1.0 / 64.0))
    halves = jnp.concatenate([top, total - 64.0 * top], axis=1).T.astype(BF)
    local = jnp.zeros((64, 32), F32)
    for fl in range(count):
        seen = dot(halves, owners[fl])
        pair = jnp.sum(cells[fl] * (64.0 * seen[:16] + seen[16:]), axis=0, keepdims=True)
        rank = (pair < 2.0 * (lane + float(fl * batch))).astype(I32)
        lead = cs[fl] * 2 + rank
        slot_ref[fl : fl + 1, :] = (ys[fl] * 64 + ms[fl]) * 4 + lead
        spread = jnp.where(iota((32, batch), 0) == lead * 8 + ys[fl], locs[fl], 0.0)
        local += dot_t(owners[fl], spread.astype(BF))
    local_ref[...] = local


def pack_body(slot_ref, grads_ref, send_ref):
    batch, wide = grads_ref.shape
    width = 256
    step = 512
    for chunk in range(2048 // step):
        rows = iota((step, batch), 0) + chunk * step
        acc = jnp.zeros((step, width), F32)
        for f in range(wide // width):
            a = slot_ref[2 * f : 2 * f + 1, :]
            b = slot_ref[2 * f + 1 : 2 * f + 2, :]
            take = onehot((rows == a) | (rows == b))
            acc += dot(take, grads_ref[:, f * width : (f + 1) * width])
        left = acc[:, :128].reshape(step // 8, 8, 128)
        right = acc[:, 128:].reshape(step // 8, 8, 128)
        low = iota((step // 8, 8, 128), 1) < 4
        first = jnp.where(low, left, pltpu.roll(right, 4, axis=1))
        second = jnp.where(low, pltpu.roll(left, 4, axis=1), right)
        both = jnp.concatenate([first[:, None], second[:, None]], axis=1)
        send_ref[chunk * 2 * step : (chunk + 1) * 2 * step, :] = both.reshape(2 * step, 128).astype(BF)


def total_body(core_ref, local_ref, got_ref, own_ref, sib_ref):
    core = core_ref[0]
    n = iota((256, 512), 1)
    order = onehot(iota((256, 512), 0) == (n & 3) * 64 + (n >> 3))
    spot = dot(local_ref[...].astype(BF), order).astype(I32)
    n = iota((8, 512), 1)
    spot = spot + ((n >> 2) & 1) * 256 + (((n >> 1) & 1) ^ core) * 128
    acc = jnp.zeros((512, 128), F32)
    for y in range(8):
        hit = onehot(iota((512, 512), 0) == spot[y : y + 1, :])
        acc += dot(hit, got_ref[y * 512 : (y + 1) * 512, :])
    own_ref[:, :128] = acc[0:128]
    own_ref[:, 128:] = acc[256:384]
    sib_ref[:, :128] = acc[128:256]
    sib_ref[:, 128:] = acc[384:512]


def adam_body(own_ref, sib_ref, moment_ref, second_ref, new_moment_ref, new_second_ref, step_ref):
    grad = own_ref[...] + sib_ref[...]
    moment = BETA_ONE * moment_ref[...] + (1.0 - BETA_ONE) * grad
    mean = jnp.sum(grad * grad, axis=1, keepdims=True) * (1.0 / grad.shape[1])
    rows = grad.shape[0]
    eye = iota((rows, rows), 0) == iota((rows, rows), 1)
    old = jnp.sum(jnp.where(eye, second_ref[...], 0.0), axis=1, keepdims=True)
    second = BETA_TWO * old + (1.0 - BETA_TWO) * mean
    new_moment_ref[...] = moment
    new_second_ref[...] = jnp.sum(jnp.where(eye, second, 0.0), axis=0, keepdims=True)
    step_ref[...] = (LEARN_RATE * moment / (jnp.sqrt(second) + EPSILON)).astype(BF)


def pooled_grads(pooled, labels, w_hidden, b_hidden, w_out):
    batch_rows, num_feats, feat_width = pooled.shape
    features_flat = pooled.reshape(batch_rows, num_feats * feat_width)
    pre_act = jnp.dot(features_flat, w_hidden, preferred_element_type=F32) + b_hidden
    sig_pre = jax.nn.sigmoid(pre_act)
    hidden = pre_act * sig_pre
    logit = jnp.sum(hidden * w_out[None, :], axis=1)
    probability = jax.nn.sigmoid(logit)
    target = labels.astype(F32)
    dlogit = (
        -LOSS_SCALE * (1.0 - probability * probability) * (target - (1.0 - target) * probability)
    )
    dpre = (
        dlogit[:, None] * w_out[None, :] * (sig_pre * (1.0 + pre_act * (1.0 - sig_pre)))
    ).astype(BF)
    dflat = lax.dot_general(
        dpre, w_hidden, (((1,), (1,)), ((), ())), preferred_element_type=F32
    )
    return dflat.astype(BF)


def on_device(
    pooled,
    row_ids,
    labels,
    row_slot,
    w_hidden,
    b_hidden,
    w_out,
    emb_table,
    adam_moment,
    adam_second,
):
    shape = jax.ShapeDtypeStruct
    rep, mp = "replica", "mp"
    same_core = [[2 * y + c for y in range(8)] for c in range(2)]
    planes = [[r * 64 + m for r in group for m in range(64)] for group in same_core]
    other_core = [(i, i ^ 1) for i in range(16)]
    core = lax.axis_index(rep) % 2

    slots, local = call(
        route_body,
        [shape((8, 256), I32), shape((64, 32), F32)],
        row_ids.transpose(1, 2, 0),
        row_slot.reshape(1024, 128),
        scratch=[
            pltpu.VMEM((384, 1024), BF),
            pltpu.VMEM((8, 64, 256), BF),
            pltpu.VMEM((8, 16, 256), F32),
        ],
    )
    local = lax.all_to_all(
        local.reshape(64, 1, 32), mp, split_axis=0, concat_axis=0, tiled=True
    )
    grads = pooled_grads(pooled, labels, w_hidden, b_hidden, w_out)
    (send,) = call(pack_body, [shape((4096, 128), BF)], slots, grads)
    got = lax.all_to_all(
        send.reshape(512, 8, 128),
        (rep, mp),
        split_axis=0,
        concat_axis=0,
        tiled=True,
        axis_index_groups=planes,
    )
    local = local.reshape(64, 4, 8).transpose(2, 1, 0).reshape(8, 1, 256)
    local = lax.all_to_all(
        local, rep, split_axis=0, concat_axis=0, tiled=True, axis_index_groups=same_core
    )
    own, sib = call(
        total_body,
        [shape((128, 256), F32), shape((128, 256), F32)],
        core.reshape(1).astype(I32),
        local.reshape(8, 256),
        got.reshape(4096, 128),
        smem=1,
    )
    sib = lax.ppermute(sib, rep, other_core)
    new_moment, new_second, step = call(
        adam_body,
        [shape((128, 256), F32), shape((1, 128), F32), shape((128, 256), BF)],
        own,
        sib,
        adam_moment,
        adam_second.reshape(1, 128),
    )
    mine = lax.all_gather(step, rep, axis=0, tiled=False, axis_index_groups=same_core)
    others = lax.ppermute(mine, rep, other_core)
    even = jnp.where(core == 0, mine, others)
    odd = jnp.where(core == 0, others, mine)
    steps = jnp.stack([even, odd], axis=1).reshape(2048, 256)
    new_table = emb_table - steps.astype(F32)
    return (new_table, new_moment, new_second.reshape(128))


def solution(mesh):
    in_specs = (
        P(("replica", "mp"), None, None),
        P(("replica", "mp"), None, None),
        P(("replica", "mp")),
        P(),
        P(),
        P(),
        P(),
        P("mp", None),
        P(("mp", "replica"), None),
        P(("mp", "replica")),
    )
    out_specs = (P("mp", None), P(("mp", "replica"), None), P(("mp", "replica")))
    return jax.shard_map(
        on_device, mesh=mesh, in_specs=in_specs, out_specs=out_specs, check_vma=False
    )
```

time: 266 us -> 167 us (0.63)
  waiting for transfers between devices: 162 us -> 63.4 us
  local copies, waits for them, and re-layouts: 39 us -> 5.4 us
  starting transfers between devices: 35.4 us -> 63.2 us
  blocking collectives: 0 us -> 19.3 us
  between operations: 14.3 us -> 0.82 us
  Pallas kernels: 0 us -> 9.86 us
  other arithmetic: 9.06 us -> 1.81 us
  matrix products: 6.32 us -> 2.57 us
    reduce_scatter x1 -> x0, waiting for transfers between devices: 62.8 us -> none  [on_device(): lax.psum_scatter(jnp.dot(onehot, flat_values, preferred_element_type=jnp....]
    all_gather x1 -> x0, waiting for transfers between devices: 47.3 us -> none  [on_device(): new_table = lax.all_gather(new_rows, 'replica', axis=0, tiled=True)]
    gather x3 -> x0, local copies, waits for them, and re-layouts: 32.6 us -> none  [the longest x1 11.8 us: on_device(): send_rows = within[sort_order]]
    all_gather x0 -> x1, blocking collectives: none -> 19.3 us  [on_device(): lax.all_gather(step, rep, axis=0, tiled=False, axis_index_groups=same_core)]
    ppermute x0 -> x2, starting transfers between devices: none -> 18.3 us  [the longest x1 9.83 us: on_device(): sib = lax.ppermute(sib, rep, other_core)]
    pallas_call x0 -> x4, Pallas kernels: none -> 9.86 us  [call(): pl.pallas_call(body, out_shape=outs, in_specs=specs, out_specs=[pl.BlockS...]
    all_to_all x2 -> x3, starting transfers between devices: 35.4 us -> 44.9 us  [the longest x1 22.8 us: on_device(): lax.all_to_all(local.reshape(64, 1, 32), mp, split_axis=0, concat_axis=0,...]
    all_to_all x2 -> x3, waiting for transfers between devices: 51.5 us -> 60.9 us  [the longest x1 47.5 us: on_device(): lax.all_to_all(send.reshape(512, 8, 128), (rep, mp), split_axis=0, concat...]
  transfers between devices with their start and end apart: 4 -> 5, of which waited for: 4 -> 5; matrix products, arithmetic and copies ran while one was open for 5% -> 2% of each run, Pallas kernels for 0% -> 2%
where the time goes in v1:
time: 167 us; the launch traced here: 166 us
  waiting for transfers between devices  63.4 us (38%)
  starting transfers between devices  63.2 us (38%)
  blocking collectives  19.3 us (12%)
  Pallas kernels  9.86 us (6%)
  local copies, waits for them, and re-layouts  5.4 us (3%)
  matrix products  2.57 us (2%)
  other arithmetic  1.81 us (1%)
    all_to_all x1, waiting for transfers between devices, on_device(): lax.all_to_all(send.reshape(512, 8, 128), (rep, mp), split_axis=0, concat...  47.5 us
    all_to_all x1, starting transfers between devices, on_device(): lax.all_to_all(local.reshape(64, 1, 32), mp, split_axis=0, concat_axis=0,...  22.8 us
    all_gather x1, blocking collectives, on_device(): lax.all_gather(step, rep, axis=0, tiled=False, axis_index_groups=same_core)  19.3 us
    all_to_all x1, starting transfers between devices, on_device(): lax.all_to_all(send.reshape(512, 8, 128), (rep, mp), split_axis=0, concat...  15.3 us
    all_to_all x1, waiting for transfers between devices, on_device(): lax.all_to_all(local.reshape(64, 1, 32), mp, split_axis=0, concat_axis=0,...  10.5 us
    pallas_call x4, Pallas kernels, call(): pl.pallas_call(body, out_shape=outs, in_specs=specs, out_specs=[pl.BlockS...  9.86 us
    ppermute x1, starting transfers between devices, on_device(): sib = lax.ppermute(sib, rep, other_core)  9.83 us
    ppermute x1, starting transfers between devices, on_device(): others = lax.ppermute(mine, rep, other_core)  8.51 us
  transfers between devices with their start and end apart: 5, of which 5 were waited for; matrix products, arithmetic and copies ran while one was open for 2% of the time, Pallas kernels for 2%

profile of v1, /device:TPU:1, one launch (start us, length us, event | category | flops | bytes accessed | tf_op | source)
XLA Modules:
  0.0 166.4 jit_solution(13376390891225426500)
XLA Ops:
  0.6 0.0 copy-start
  0.7 1.2 copy-done.1
  1.8 0.7 copy-done.3
  2.5 5.0 %shard_map.121 = (s32[8,256]{1,0:T(8,128)S(1)}, f32[64,32]{1,0:T(8,128)}) custom-call(s32[4,2,256]{2,1,0:T(2,128)S(1)} %bitcast.31, s32[1024,128]{1,0:T(8,128)S(1)} %bitcast.29), custom_call_target="tpu_custom_call" | custom-call | tf_op jit(solution)/shard_map/pallas_call | solution.py:39
  7.6 22.8 %all-to-all-start = ((f32[64,1,32]{2,1,0:T(1,128)}), f32[64,1,32]{2,1,0:T(1,128)S(1)}, u32[]{:S(2)}, u32[]{:S(2)}) async-start(f32[64,1,32]{2,1,0:T(1,128)} %bitcast.4), calls=%async_computation | async-start | bytes 65536 | tf_op jit(solution)/shard_map/all_to_all | solution.py:199
  30.4 1.1 copy.27
  31.5 0.0 copy-start.6
  31.5 0.0 copy-start.7
  31.5 1.7 %multiply_reduce_fusion = (f32[256]{0:T(256)S(1)}, f32[256,1024]{1,0:T(8,128)S(1)}) fusion(f32[1024]{0:T(1024)} %param.16, f32[1024]{0:T(1024)} %param.15, bf16[256,1024]{1,0:T(8,128)(2,1)S(1)} %bitcast.36, bf16[1024,1024]{1,0:T(8,128)(2,1)S(1)} %copy-done), kind=kOutput, calls=%fused_computation.5 | convolution fusion | flops 538705664 | bytes 3679232 | tf_op jit(solution)/shard_map/dot_general | solution.py:151
  33.3 10.5 %all-to-all-done = f32[64,1,32]{2,1,0:T(1,128)S(1)} async-done(((f32[64,1,32]{2,1,0:T(1,128)}), f32[64,1,32]{2,1,0:T(1,128)S(1)}, u32[]{:S(2)}, u32[]{:S(2)}) %all-to-all-start) | async-done | bytes 8224 | tf_op jit(solution)/shard_map/all_to_all | solution.py:199
  43.7 0.1 copy.22
  43.8 0.7 reshape.58
  44.5 6.8 %all-to-all-start.1 = ((f32[8,1,256]{2,1,0:T(1,128)}), f32[8,1,256]{2,1,0:T(1,128)S(1)}, u32[]{:S(2)}, u32[]{:S(2)}) async-start(f32[8,1,256]{2,1,0:T(1,128)} %reshape.58), calls=%async_computation.1 | async-start | bytes 16384 | tf_op jit(solution)/shard_map/all_to_all | solution.py:213
  51.3 0.9 convolution_convert_fusion.grads_ref
  52.2 0.0 copy-start.2
  52.3 0.0 copy-start.4
  52.3 2.7 %shard_map.122 = bf16[4096,128]{1,0:T(8,128)(2,1)} custom-call(s32[8,256]{1,0:T(8,128)S(1)} %get-tuple-element.11.slot_ref, bf16[256,1024]{1,0:T(8,128)(2,1)S(1)} %convolution_convert_fusion.grads_ref), custom_call_target="tpu_custom_call" | custom-call | tf_op jit(solution)/shard_map/pallas_call | solution.py:39
  55.0 2.9 %all-to-all-done.1 = f32[8,1,256]{2,1,0:T(1,128)S(1)} async-done(((f32[8,1,256]{2,1,0:T(1,128)}), f32[8,1,256]{2,1,0:T(1,128)S(1)}, u32[]{:S(2)}, u32[]{:S(2)}) %all-to-all-start.1) | async-done | bytes 8224 | tf_op jit(solution)/shard_map/all_to_all | solution.py:213
  57.9 15.3 %all-to-all-start.2 = ((bf16[512,8,128]{2,1,0:T(8,128)(2,1)}), bf16[512,8,128]{2,1,0:T(8,128)(2,1)S(1)}, u32[]{:S(2)}, u32[]{:S(2)}) async-start(bf16[512,8,128]{2,1,0:T(8,128)(2,1)} %bitcast.7), calls=%async_computation.2 | async-start | bytes 2097152 | tf_op jit(solution)/shard_map/all_to_all | solution.py:204
  73.2 47.5 %all-to-all-done.2 = bf16[512,8,128]{2,1,0:T(8,128)(2,1)S(1)} async-done(((bf16[512,8,128]{2,1,0:T(8,128)(2,1)}), bf16[512,8,128]{2,1,0:T(8,128)(2,1)S(1)}, u32[]{:S(2)}, u32[]{:S(2)}) %all-to-all-start.2) | async-done | bytes 1048608 | tf_op jit(solution)/shard_map/all_to_all | solution.py:204
  120.7 1.4 shard_map.123
  122.1 9.8 %collective-permute-start = (f32[128,256]{1,0:T(8,128)S(1)}, f32[128,256]{1,0:T(8,128)S(1)}, u32[]{:S(2)}, u32[]{:S(2)}) collective-permute-start(f32[128,256]{1,0:T(8,128)S(1)} %get-tuple-element.13), channel_id=1, source_target_pairs={{0,64},{64,0},{128,192},{192,128},{256,320},{320,256},{384,448},{4... | collective-permute-start | bytes 393224 | tf_op jit(solution)/shard_map/ppermute | solution.py:224
  132.0 1.0 collective-permute-done.sib_ref
  132.9 0.7 shard_map.124
  133.6 19.3 %all-gather = bf16[1024,256]{1,0:T(8,128)(2,1)S(1)} all-gather(bf16[128,256]{1,0:T(8,128)(2,1)S(1)} %get-tuple-element.14), channel_id=2, replica_groups={{0,128,256,384,512,640,768,896},{64,192,320,448,576,704,832,960},{1,129..., dimensions={0}, use_global_device_ids=true | all-gather | bytes 589824 | tf_op jit(solution)/shard_map/all_gather | solution.py:233
  152.9 8.5 %collective-permute-start.1 = (bf16[8,128,256]{2,1,0:T(8,128)(2,1)S(1)}, bf16[8,128,256]{2,1,0:T(8,128)(2,1)S(1)}, u32[]{:S(2)}, u32[]{:S(2)}) collective-permute-start(bf16[8,128,256]{2,1,0:T(8,128)(2,1)S(1)} %bitcast.33), channel_id=1, source_target_pairs={{0,64},{64,0},{128,192},{192,128},{256,320},{320,256},{384,448},{4... | collective-permute-start | bytes 1572872 | tf_op jit(solution)/shard_map/ppermute | solution.py:234
  161.5 1.5 collective-permute-done.1
  163.0 0.1 select_bitcast_fusion.1
  163.0 0.1 maximum_convert_fusion
  163.2 0.1 copy.25
  163.3 1.4 copy-done.5
  164.8 1.6 bitcast_subtract_fusion
  (11 shorter events, 0.0 us)
Async XLA Ops:
  0.6 30.9 %copy-start = (bf16[1024,1024]{1,0:T(8,128)(2,1)S(1)}, bf16[1024,1024]{1,0:T(8,128)(2,1)}, u32[]{:S(2)}) copy-start(bf16[1024,1024]{1,0:T(8,128)(2,1)} %param.14) | copy-start | bytes 6291460
  0.6 1.2 copy-start.1
  1.8 0.7 copy-start.3
  7.6 36.2 %all-to-all-start = ((f32[64,1,32]{2,1,0:T(1,128)}), f32[64,1,32]{2,1,0:T(1,128)S(1)}, u32[]{:S(2)}, u32[]{:S(2)}) async-start(f32[64,1,32]{2,1,0:T(1,128)} %bitcast.4), calls=%async_computation | async-start | bytes 65536 | tf_op jit(solution)/shard_map/all_to_all | solution.py:199
  31.5 1.7 %copy-start.6 = (s32[256]{0:T(256)S(1)}, s32[256]{0:T(256)}, u32[]{:S(2)}) copy-start(s32[256]{0:T(256)} %param.12) | copy-start | bytes 3076
  31.5 19.8 %copy-start.7 = (f32[1024]{0:T(1024)S(1)}, f32[1024]{0:T(1024)}, u32[]{:S(2)}) copy-start(f32[1024]{0:T(1024)} %param.16) | copy-start | bytes 12292
  44.5 13.4 %all-to-all-start.1 = ((f32[8,1,256]{2,1,0:T(1,128)}), f32[8,1,256]{2,1,0:T(1,128)S(1)}, u32[]{:S(2)}, u32[]{:S(2)}) async-start(f32[8,1,256]{2,1,0:T(1,128)} %reshape.58), calls=%async_computation.1 | async-start | bytes 16384 | tf_op jit(solution)/shard_map/all_to_all | solution.py:213
  52.2 80.7 %copy-start.2 = (f32[128,256]{1,0:T(8,128)S(1)}, f32[128,256]{1,0:T(8,128)}, u32[]{:S(2)}) copy-start(f32[128,256]{1,0:T(8,128)} %moment_ref.1) | copy-start | bytes 393220
  52.3 80.7 %copy-start.4 = (f32[128]{0:T(128)S(1)}, f32[128]{0:T(128)}, u32[]{:S(2)}) copy-start(f32[128]{0:T(128)} %param.19) | copy-start | bytes 1540
  57.9 62.8 %all-to-all-start.2 = ((bf16[512,8,128]{2,1,0:T(8,128)(2,1)}), bf16[512,8,128]{2,1,0:T(8,128)(2,1)S(1)}, u32[]{:S(2)}, u32[]{:S(2)}) async-start(bf16[512,8,128]{2,1,0:T(8,128)(2,1)} %bitcast.7), calls=%async_computation.2 | async-start | bytes 2097152 | tf_op jit(solution)/shard_map/all_to_all | solution.py:204
  122.1 10.8 %collective-permute-start = (f32[128,256]{1,0:T(8,128)S(1)}, f32[128,256]{1,0:T(8,128)S(1)}, u32[]{:S(2)}, u32[]{:S(2)}) collective-permute-start(f32[128,256]{1,0:T(8,128)S(1)} %get-tuple-element.13), channel_id=1, source_target_pairs={{0,64},{64,0},{128,192},{192,128},{256,320},{320,256},{384,448},{4... | collective-permute-start | bytes 393224 | tf_op jit(solution)/shard_map/ppermute | solution.py:224
  152.9 10.0 %collective-permute-start.1 = (bf16[8,128,256]{2,1,0:T(8,128)(2,1)S(1)}, bf16[8,128,256]{2,1,0:T(8,128)(2,1)S(1)}, u32[]{:S(2)}, u32[]{:S(2)}) collective-permute-start(bf16[8,128,256]{2,1,0:T(8,128)(2,1)S(1)} %bitcast.33), channel_id=1, source_target_pairs={{0,64},{64,0},{128,192},{192,128},{256,320},{320,256},{384,448},{4... | collective-permute-start | bytes 1572872 | tf_op jit(solution)/shard_map/ppermute | solution.py:234
  163.2 1.6 copy-start.5

commit v2 on v1

--- a/solution.py
+++ b/solution.py
@@ -91,7 +91,8 @@
         slot_ref[fl : fl + 1, :] = (ys[fl] * 64 + ms[fl]) * 4 + lead
         spread = jnp.where(iota((32, batch), 0) == lead * 8 + ys[fl], locs[fl], 0.0)
         local += dot_t(owners[fl], spread.astype(BF))
-    local_ref[...] = local
+    turned = local.T
+    local_ref[...] = jnp.concatenate([turned[:16], turned[16:]], axis=1).astype(BF)
 
 
 def pack_body(slot_ref, grads_ref, send_ref):
@@ -115,13 +116,21 @@
         send_ref[chunk * 2 * step : (chunk + 1) * 2 * step, :] = both.reshape(2 * step, 128).astype(BF)
 
 
-def total_body(core_ref, local_ref, got_ref, own_ref, sib_ref):
-    core = core_ref[0]
-    n = iota((256, 512), 1)
-    order = onehot(iota((256, 512), 0) == (n & 3) * 64 + (n >> 3))
-    spot = dot(local_ref[...].astype(BF), order).astype(I32)
+def select_body(place_ref, all_ref, mine_ref):
+    rows, lanes = iota((8, 128), 0), iota((8, 128), 1)
+    take = onehot(lanes == rows * 64 + place_ref[0])
+    mine_ref[...] = dot_t(take, all_ref[...])[:2]
+
+
+def total_body(place_ref, local_ref, got_ref, own_ref, sib_ref):
+    y_here, core = place_ref[1], place_ref[2]
+    n = iota((1024, 512), 1)
+    order = onehot(iota((1024, 512), 0) == (n >> 3) * 16 + (n & 1) * 8 + y_here)
+    found = dot(local_ref[...].astype(BF), order).reshape(8, 2, 512)
     n = iota((8, 512), 1)
-    spot = spot + ((n >> 2) & 1) * 256 + (((n >> 1) & 1) ^ core) * 128
+    side = (n >> 1) & 1
+    spot = jnp.where(side == 0, found[:, 0, :], found[:, 1, :]).astype(I32)
+    spot = spot + ((n >> 2) & 1) * 256 + (side ^ core) * 128
     acc = jnp.zeros((512, 128), F32)
     for y in range(8):
         hit = onehot(iota((512, 512), 0) == spot[y : y + 1, :])
@@ -143,6 +152,13 @@
     new_moment_ref[...] = moment
     new_second_ref[...] = jnp.sum(jnp.where(eye, second, 0.0), axis=0, keepdims=True)
     step_ref[...] = (LEARN_RATE * moment / (jnp.sqrt(second) + EPSILON)).astype(BF)
+
+
+def table_body(place_ref, mine_ref, others_ref, table_ref, out_ref):
+    core = place_ref[2]
+    for steps, side in ((mine_ref, core), (others_ref, 1 - core)):
+        rows = pl.ds(pl.multiple_of(side * 128, 128), 128)
+        out_ref[rows, :] = table_ref[rows, :] - steps[0].astype(F32)
 
 
 def pooled_grads(pooled, labels, w_hidden, b_hidden, w_out):
@@ -183,11 +199,12 @@
     same_core = [[2 * y + c for y in range(8)] for c in range(2)]
     planes = [[r * 64 + m for r in group for m in range(64)] for group in same_core]
     other_core = [(i, i ^ 1) for i in range(16)]
-    core = lax.axis_index(rep) % 2
+    core = lax.axis_index(rep) & 1
+    place = jnp.stack([lax.axis_index(mp), lax.axis_index(rep) >> 1, core]).astype(I32)
 
     slots, local = call(
         route_body,
-        [shape((8, 256), I32), shape((64, 32), F32)],
+        [shape((8, 256), I32), shape((16, 128), BF)],
         row_ids.transpose(1, 2, 0),
         row_slot.reshape(1024, 128),
         scratch=[
@@ -196,11 +213,9 @@
             pltpu.VMEM((8, 16, 256), F32),
         ],
     )
-    local = lax.all_to_all(
-        local.reshape(64, 1, 32), mp, split_axis=0, concat_axis=0, tiled=True
-    )
     grads = pooled_grads(pooled, labels, w_hidden, b_hidden, w_out)
     (send,) = call(pack_body, [shape((4096, 128), BF)], slots, grads)
+    send, local = lax.optimization_barrier((send, local))
     got = lax.all_to_all(
         send.reshape(512, 8, 128),
         (rep, mp),
@@ -209,15 +224,14 @@
         tiled=True,
         axis_index_groups=planes,
     )
-    local = local.reshape(64, 4, 8).transpose(2, 1, 0).reshape(8, 1, 256)
-    local = lax.all_to_all(
-        local, rep, split_axis=0, concat_axis=0, tiled=True, axis_index_groups=same_core
-    )
+    local = lax.all_gather(local, mp, axis=0, tiled=True)
+    (local,) = call(select_body, [shape((2, 1024), F32)], place, local, smem=1)
+    local = lax.all_gather(local, rep, axis=0, tiled=True, axis_index_groups=same_core)
     own, sib = call(
         total_body,
         [shape((128, 256), F32), shape((128, 256), F32)],
-        core.reshape(1).astype(I32),
-        local.reshape(8, 256),
+        place,
+        local,
         got.reshape(4096, 128),
         smem=1,
     )
@@ -232,10 +246,18 @@
     )
     mine = lax.all_gather(step, rep, axis=0, tiled=False, axis_index_groups=same_core)
     others = lax.ppermute(mine, rep, other_core)
-    even = jnp.where(core == 0, mine, others)
-    odd = jnp.where(core == 0, others, mine)
-    steps = jnp.stack([even, odd], axis=1).reshape(2048, 256)
-    new_table = emb_table - steps.astype(F32)
+    new_table = pl.pallas_call(
+        table_body,
+        grid=(8,),
+        out_shape=shape((2048, 256), F32),
+        in_specs=[
+            pl.BlockSpec(memory_space=pltpu.SMEM),
+            pl.BlockSpec((1, 128, 256), lambda i: (i, 0, 0)),
+            pl.BlockSpec((1, 128, 256), lambda i: (i, 0, 0)),
+            pl.BlockSpec((256, 256), lambda i: (i, 0)),
+        ],
+        out_specs=pl.BlockSpec((256, 256), lambda i: (i, 0)),
+    )(place, mine, others, emb_table)
     return (new_table, new_moment, new_second.reshape(128))
 
 

time: 167 us -> 237 us (1.42)
  blocking collectives: 19.3 us -> 140 us
  waiting for transfers between devices: 63.4 us -> 2.48 us
  starting transfers between devices: 63.2 us -> 69.8 us
  Pallas kernels: 9.86 us -> 15.7 us
    all_gather x0 -> x2, blocking collectives: none -> 120 us  [the longest x1 99.3 us: on_device(): local = lax.all_gather(local, mp, axis=0, tiled=True)]
    all_to_all x1, waiting for transfers between devices: 47.5 us -> 0.01 us  [on_device(): lax.all_to_all(send.reshape(512, 8, 128), (rep, mp), split_axis=0, concat...]
    all_to_all x2 -> x0, starting transfers between devices: 29.6 us -> none  [the longest x1 22.8 us: on_device(): lax.all_to_all(local.reshape(64, 1, 32), mp, split_axis=0, concat_axis=0,...]
    all_to_all x1, starting transfers between devices: 15.3 us -> 36.5 us  [on_device(): lax.all_to_all(send.reshape(512, 8, 128), (rep, mp), split_axis=0, concat...]
    ppermute x1, starting transfers between devices: 9.83 us -> 25.6 us  [on_device(): sib = lax.ppermute(sib, rep, other_core)]
    all_to_all x2 -> x0, waiting for transfers between devices: 13.4 us -> none  [the longest x1 10.5 us: on_device(): lax.all_to_all(local.reshape(64, 1, 32), mp, split_axis=0, concat_axis=0,...]
    pallas_call x0 -> x1, Pallas kernels: none -> 6.01 us  [on_device(): pl.pallas_call(table_body, grid=(8,), out_shape=shape((2048, 256), F32),...]
    unnamed x18 -> x24, local copies, waits for them, and re-layouts: 4.49 us -> 4.86 us
  transfers between devices with their start and end apart: 5 -> 3, of which waited for: 5 -> 2; matrix products, arithmetic and copies ran while one was open for 2% -> 0% of each run, Pallas kernels for 2% -> 0%
where the time goes in v2:
time: 237 us; the launch traced here: 236 us
  blocking collectives  140 us (59%)
  starting transfers between devices  69.8 us (29%)
  Pallas kernels  15.7 us (7%)
  local copies, waits for them, and re-layouts  4.86 us (2%)
  matrix products  2.58 us (1%)
  waiting for transfers between devices  2.48 us (1%)
    all_gather x1, blocking collectives, on_device(): local = lax.all_gather(local, mp, axis=0, tiled=True)  99.3 us
    all_to_all x1, starting transfers between devices, on_device(): lax.all_to_all(send.reshape(512, 8, 128), (rep, mp), split_axis=0, concat...  36.5 us
    ppermute x1, starting transfers between devices, on_device(): sib = lax.ppermute(sib, rep, other_core)  25.6 us
    all_gather x1, blocking collectives, on_device(): lax.all_gather(local, rep, axis=0, tiled=True, axis_index_groups=same_core)  20.6 us
    all_gather x1, blocking collectives, on_device(): lax.all_gather(step, rep, axis=0, tiled=False, axis_index_groups=same_core)  19.8 us
    pallas_call x5, Pallas kernels, call(): pl.pallas_call(body, out_shape=outs, in_specs=specs, out_specs=[pl.BlockS...  9.71 us
    ppermute x1, starting transfers between devices, on_device(): others = lax.ppermute(mine, rep, other_core)  7.7 us
    pallas_call x1, Pallas kernels, on_device(): pl.pallas_call(table_body, grid=(8,), out_shape=shape((2048, 256), F32),...  6.01 us
  transfers between devices with their start and end apart: 3, of which 2 were waited for; matrix products, arithmetic and copies ran while one was open for 0% of the time, Pallas kernels for 0%

profile of v2, /device:TPU:1, one launch (start us, length us, event | category | flops | bytes accessed | tf_op | source)
XLA Modules:
  0.0 236.0 jit_solution(8539342430433852184)
XLA Ops:
  0.6 0.0 copy-start
  0.6 1.3 copy.13
  1.9 0.0 copy-start.2
  1.9 1.0 copy-done.2
  3.0 0.7 copy-done.4
  3.7 4.5 %shard_map.121 = (s32[8,256]{1,0:T(8,128)S(1)}, bf16[16,128]{1,0:T(8,128)(2,1)S(1)}) custom-call(s32[4,2,256]{2,1,0:T(2,128)S(1)} %bitcast.20, s32[1024,128]{1,0:T(8,128)S(1)} %bitcast.18), custom_call_target="tpu_custom_call" | custom-call | tf_op jit(solution)/shard_map/pallas_call | solution.py:39
  8.2 0.0 copy-done
  8.2 1.7 multiply_reduce_fusion
  9.9 0.0 copy-done.9
  10.0 0.0 copy-done.10
  10.0 0.9 convolution_convert_fusion.grads_ref
  10.9 1.8 shard_map.122
  12.7 0.0 copy-start.1
  12.7 1.0 copy-done.1
  13.6 36.5 %all-to-all-start = ((bf16[512,8,128]{2,1,0:T(8,128)(2,1)}), bf16[512,8,128]{2,1,0:T(8,128)(2,1)S(1)}, u32[]{:S(2)}, u32[]{:S(2)}) async-start(bf16[512,8,128]{2,1,0:T(8,128)(2,1)} %bitcast.17), calls=%async_computation | async-start | bytes 2097152 | tf_op jit(solution)/shard_map/all_to_all | solution.py:219
  50.1 99.3 %all_gather.12.all_ref = bf16[1024,128]{1,0:T(8,128)(2,1)S(1)} all-gather(bf16[16,128]{1,0:T(8,128)(2,1)S(1)} %get-tuple-element.14), channel_id=1, replica_groups=mesh['replica'=16,'mp'=64] {'mp'}, dimensions={0}, use_global_device_ids=true | all-gather | bytes 266240 | tf_op jit(solution)/shard_map/all_gather | solution.py:227
  149.5 0.1 pad_add_fusion.place_ref
  149.5 0.7 shard_map.123
  150.2 20.6 %all-gather.1 = f32[8,2,1024]{2,1,0:T(2,128)S(1)} all-gather(f32[1,2,1024]{2,1,0:T(2,128)S(1)} %bitcast.19), channel_id=1, replica_groups={{0,128,256,384,512,640,768,896},{64,192,320,448,576,704,832,960},{1,129..., dimensions={0}, use_global_device_ids=true | all-gather | bytes 73728 | tf_op jit(solution)/shard_map/all_gather | solution.py:229
  170.8 0.0 all-to-all-done
  170.9 2.0 shard_map.124
  172.9 25.6 %collective-permute-start = (f32[128,256]{1,0:T(8,128)S(1)}, f32[128,256]{1,0:T(8,128)S(1)}, u32[]{:S(2)}, u32[]{:S(2)}) collective-permute-start(f32[128,256]{1,0:T(8,128)S(1)} %get-tuple-element.17), channel_id=1, source_target_pairs={{0,64},{64,0},{128,192},{192,128},{256,320},{320,256},{384,448},{4... | collective-permute-start | bytes 393224 | tf_op jit(solution)/shard_map/ppermute | solution.py:238
  198.5 1.0 collective-permute-done.sib_ref
  199.5 0.0 copy-done.3
  199.5 0.0 copy-done.6
  199.5 0.7 shard_map.125
  200.2 19.8 %all-gather = bf16[1024,256]{1,0:T(8,128)(2,1)S(1)} all-gather(bf16[128,256]{1,0:T(8,128)(2,1)S(1)} %get-tuple-element.18), channel_id=2, replica_groups={{0,128,256,384,512,640,768,896},{64,192,320,448,576,704,832,960},{1,129..., dimensions={0}, use_global_device_ids=true | all-gather | bytes 589824 | tf_op jit(solution)/shard_map/all_gather | solution.py:247
  220.0 7.7 %collective-permute-start.1 = (bf16[8,128,256]{2,1,0:T(8,128)(2,1)S(1)}, bf16[8,128,256]{2,1,0:T(8,128)(2,1)S(1)}, u32[]{:S(2)}, u32[]{:S(2)}) collective-permute-start(bf16[8,128,256]{2,1,0:T(8,128)(2,1)S(1)} %bitcast.22), channel_id=1, source_target_pairs={{0,64},{64,0},{128,192},{192,128},{256,320},{320,256},{384,448},{4... | collective-permute-start | bytes 1572872 | tf_op jit(solution)/shard_map/ppermute | solution.py:248
  227.7 1.5 collective-permute-done.1.others_ref
  229.2 0.0 copy-done.7
  229.2 0.8 copy-done.8
  230.0 6.0 %shard_map.126 = f32[2048,256]{1,0:T(8,128)} custom-call(s32[3]{0:T(128)} %copy-done.5, bf16[8,128,256]{2,1,0:T(8,128)(2,1)} %bitcast.23, bf16[8,128,256]{2,1,0:T(8,128)(2,1)} %copy-done.8, f32[2048,256]{1,0:T(8,128)} %table_ref.1), custom_call_target="tpu_custom_call" | custom-call | tf_op jit(solution)/shard_map/pallas_call | solution.py:249
  (11 shorter events, 0.1 us)
Async XLA Ops:
  0.6 7.6 %copy-start = (bf16[1024,1024]{1,0:T(8,128)(2,1)S(1)}, bf16[1024,1024]{1,0:T(8,128)(2,1)}, u32[]{:S(2)}) copy-start(bf16[1024,1024]{1,0:T(8,128)(2,1)} %param.14) | copy-start | bytes 6291460
  1.9 1.0 copy-start.2
  3.0 0.7 copy-start.4
  8.2 1.8 copy-start.9
  8.2 1.8 copy-start.10
  12.7 1.0 copy-start.1
  13.6 185.8 %copy-start.3 = (f32[128,256]{1,0:T(8,128)S(1)}, f32[128,256]{1,0:T(8,128)}, u32[]{:S(2)}) copy-start(f32[128,256]{1,0:T(8,128)} %moment_ref.1) | copy-start | bytes 393220
  13.6 185.8 %copy-start.6 = (f32[128]{0:T(128)S(1)}, f32[128]{0:T(128)}, u32[]{:S(2)}) copy-start(f32[128]{0:T(128)} %param.19) | copy-start | bytes 1540
  13.6 157.2 %all-to-all-start = ((bf16[512,8,128]{2,1,0:T(8,128)(2,1)}), bf16[512,8,128]{2,1,0:T(8,128)(2,1)S(1)}, u32[]{:S(2)}, u32[]{:S(2)}) async-start(bf16[512,8,128]{2,1,0:T(8,128)(2,1)} %bitcast.17), calls=%async_computation | async-start | bytes 2097152 | tf_op jit(solution)/shard_map/all_to_all | solution.py:219
  149.5 79.7 %copy-start.5 = (s32[3]{0:T(128)}, s32[3]{0:T(128)S(1)}, u32[]{:S(2)}) copy-start(s32[3]{0:T(128)S(1)} %pad_add_fusion.place_ref) | copy-start | bytes 40
  172.9 26.6 %collective-permute-start = (f32[128,256]{1,0:T(8,128)S(1)}, f32[128,256]{1,0:T(8,128)S(1)}, u32[]{:S(2)}, u32[]{:S(2)}) collective-permute-start(f32[128,256]{1,0:T(8,128)S(1)} %get-tuple-element.17), channel_id=1, source_target_pairs={{0,64},{64,0},{128,192},{192,128},{256,320},{320,256},{384,448},{4... | collective-permute-start | bytes 393224 | tf_op jit(solution)/shard_map/ppermute | solution.py:238
  220.0 9.2 %copy-start.7 = (bf16[1024,256]{1,0:T(8,128)(2,1)}, bf16[1024,256]{1,0:T(8,128)(2,1)S(1)}, u32[]{:S(2)}) copy-start(bf16[1024,256]{1,0:T(8,128)(2,1)S(1)} %all-gather) | copy-start | bytes 1572868
  220.0 9.2 %collective-permute-start.1 = (bf16[8,128,256]{2,1,0:T(8,128)(2,1)S(1)}, bf16[8,128,256]{2,1,0:T(8,128)(2,1)S(1)}, u32[]{:S(2)}, u32[]{:S(2)}) collective-permute-start(bf16[8,128,256]{2,1,0:T(8,128)(2,1)S(1)} %bitcast.22), channel_id=1, source_target_pairs={{0,64},{64,0},{128,192},{192,128},{256,320},{320,256},{384,448},{4... | collective-permute-start | bytes 1572872 | tf_op jit(solution)/shard_map/ppermute | solution.py:248
  229.2 0.8 copy-start.8

commit v3 on v1

--- a/solution.py
+++ b/solution.py
@@ -115,16 +115,18 @@
         send_ref[chunk * 2 * step : (chunk + 1) * 2 * step, :] = both.reshape(2 * step, 128).astype(BF)
 
 
-def total_body(core_ref, local_ref, got_ref, own_ref, sib_ref):
-    core = core_ref[0]
-    n = iota((256, 512), 1)
-    order = onehot(iota((256, 512), 0) == (n & 3) * 64 + (n >> 3))
-    spot = dot(local_ref[...].astype(BF), order).astype(I32)
-    n = iota((8, 512), 1)
-    spot = spot + ((n >> 2) & 1) * 256 + (((n >> 1) & 1) ^ core) * 128
+def total_body(place_ref, local_ref, got_ref, own_ref, sib_ref):
+    y_here, core = place_ref[0], place_ref[1]
+    n = iota((32, 512), 1)
+    pick = onehot(iota((32, 512), 0) == (n & 3) * 8 + y_here)
+    near = iota((64, 512), 0) == iota((64, 512), 1) >> 3
+    n = iota((1, 512), 1)
+    shift = ((n >> 2) & 1) * 256 + (((n >> 1) & 1) ^ core) * 128
     acc = jnp.zeros((512, 128), F32)
     for y in range(8):
-        hit = onehot(iota((512, 512), 0) == spot[y : y + 1, :])
+        found = dot(local_ref[y].astype(BF), pick)
+        spot = jnp.sum(jnp.where(near, found, 0.0), axis=0, keepdims=True).astype(I32) + shift
+        hit = onehot(iota((512, 512), 0) == spot)
         acc += dot(hit, got_ref[y * 512 : (y + 1) * 512, :])
     own_ref[:, :128] = acc[0:128]
     own_ref[:, 128:] = acc[256:384]
@@ -183,7 +185,8 @@
     same_core = [[2 * y + c for y in range(8)] for c in range(2)]
     planes = [[r * 64 + m for r in group for m in range(64)] for group in same_core]
     other_core = [(i, i ^ 1) for i in range(16)]
-    core = lax.axis_index(rep) % 2
+    core = lax.axis_index(rep) & 1
+    place = jnp.stack([lax.axis_index(rep) >> 1, core]).astype(I32)
 
     slots, local = call(
         route_body,
@@ -201,6 +204,7 @@
     )
     grads = pooled_grads(pooled, labels, w_hidden, b_hidden, w_out)
     (send,) = call(pack_body, [shape((4096, 128), BF)], slots, grads)
+    send, local = lax.optimization_barrier((send, local))
     got = lax.all_to_all(
         send.reshape(512, 8, 128),
         (rep, mp),
@@ -209,15 +213,14 @@
         tiled=True,
         axis_index_groups=planes,
     )
-    local = local.reshape(64, 4, 8).transpose(2, 1, 0).reshape(8, 1, 256)
-    local = lax.all_to_all(
-        local, rep, split_axis=0, concat_axis=0, tiled=True, axis_index_groups=same_core
+    local = lax.all_gather(
+        local.reshape(64, 32), rep, axis=0, tiled=False, axis_index_groups=same_core
     )
     own, sib = call(
         total_body,
         [shape((128, 256), F32), shape((128, 256), F32)],
-        core.reshape(1).astype(I32),
-        local.reshape(8, 256),
+        place,
+        local,
         got.reshape(4096, 128),
         smem=1,
     )

time: 167 us -> 161 us (0.964)
  waiting for transfers between devices: 63.4 us -> 37 us
  blocking collectives: 19.3 us -> 41 us
  starting transfers between devices: 63.2 us -> 60.3 us
  Pallas kernels: 9.86 us -> 11.8 us
    all_gather x0 -> x1, blocking collectives: none -> 21.7 us  [on_device(): lax.all_gather(local.reshape(64, 32), rep, axis=0, tiled=False, axis_inde...]
    all_to_all x1, waiting for transfers between devices: 47.5 us -> 27.7 us  [on_device(): lax.all_to_all(send.reshape(512, 8, 128), (rep, mp), split_axis=0, concat...]
    all_to_all x1 -> x0, starting transfers between devices: 6.83 us -> none  [on_device(): lax.all_to_all(local, rep, split_axis=0, concat_axis=0, tiled=True, axis_...]
    all_to_all x1, starting transfers between devices: 15.3 us -> 21.3 us  [on_device(): lax.all_to_all(send.reshape(512, 8, 128), (rep, mp), split_axis=0, concat...]
    all_to_all x1, waiting for transfers between devices: 10.5 us -> 6.84 us  [on_device(): lax.all_to_all(local.reshape(64, 1, 32), mp, split_axis=0, concat_axis=0,...]
    all_to_all x1 -> x0, waiting for transfers between devices: 2.9 us -> none  [on_device(): lax.all_to_all(local, rep, split_axis=0, concat_axis=0, tiled=True, axis_...]
    ppermute x1, starting transfers between devices: 9.83 us -> 7.82 us  [on_device(): sib = lax.ppermute(sib, rep, other_core)]
    pallas_call x4, Pallas kernels: 9.86 us -> 11.8 us  [call(): pl.pallas_call(body, out_shape=outs, in_specs=specs, out_specs=[pl.BlockS...]
  transfers between devices with their start and end apart: 5 -> 4, of which waited for: 5 -> 4; matrix products, arithmetic and copies ran while one was open for 2% -> 2% of each run, Pallas kernels for 2% -> 2%
where the time goes in v3:
time: 161 us
  starting transfers between devices  60.3 us (37%)
  blocking collectives  41 us (25%)
  waiting for transfers between devices  37 us (23%)
  Pallas kernels  11.8 us (7%)
  local copies, waits for them, and re-layouts  5.23 us (3%)
  matrix products  2.57 us (2%)
  other arithmetic  1.88 us (1%)
    all_to_all x1, waiting for transfers between devices, on_device(): lax.all_to_all(send.reshape(512, 8, 128), (rep, mp), split_axis=0, concat...  27.7 us
    all_to_all x1, starting transfers between devices, on_device(): lax.all_to_all(local.reshape(64, 1, 32), mp, split_axis=0, concat_axis=0,...  22.8 us
    all_gather x1, blocking collectives, on_device(): lax.all_gather(local.reshape(64, 32), rep, axis=0, tiled=False, axis_inde...  21.7 us
    all_to_all x1, starting transfers between devices, on_device(): lax.all_to_all(send.reshape(512, 8, 128), (rep, mp), split_axis=0, concat...  21.3 us
    all_gather x1, blocking collectives, on_device(): lax.all_gather(step, rep, axis=0, tiled=False, axis_index_groups=same_core)  19.3 us
    pallas_call x4, Pallas kernels, call(): pl.pallas_call(body, out_shape=outs, in_specs=specs, out_specs=[pl.BlockS...  11.8 us
    ppermute x1, starting transfers between devices, on_device(): others = lax.ppermute(mine, rep, other_core)  8.45 us
    ppermute x1, starting transfers between devices, on_device(): sib = lax.ppermute(sib, rep, other_core)  7.82 us
  transfers between devices with their start and end apart: 4, of which 4 were waited for; matrix products, arithmetic and copies ran while one was open for 2% of the time, Pallas kernels for 2%

profile of v3, /device:TPU:1, one launch (start us, length us, event | category | flops | bytes accessed | tf_op | source)
XLA Modules:
  0.0 160.6 jit_solution(5258116225967544315)
XLA Ops:
  0.6 0.0 copy-start
  0.6 0.0 copy-start.1
  0.7 1.2 copy-done.1
  1.8 0.7 copy-done.3
  2.5 5.0 %shard_map.121 = (s32[8,256]{1,0:T(8,128)S(1)}, f32[64,32]{1,0:T(8,128)}) custom-call(s32[4,2,256]{2,1,0:T(2,128)S(1)} %bitcast.27, s32[1024,128]{1,0:T(8,128)S(1)} %bitcast.26), custom_call_target="tpu_custom_call" | custom-call | tf_op jit(solution)/shard_map/pallas_call | solution.py:39
  7.6 22.8 %all-to-all-start = ((f32[64,1,32]{2,1,0:T(1,128)}), f32[64,1,32]{2,1,0:T(1,128)S(1)}, u32[]{:S(2)}, u32[]{:S(2)}) async-start(f32[64,1,32]{2,1,0:T(1,128)} %bitcast.5), calls=%async_computation | async-start | bytes 65536 | tf_op jit(solution)/shard_map/all_to_all | solution.py:202
  30.4 1.1 copy.18
  31.5 0.0 copy-start.7
  31.5 0.0 copy-start.8
  31.5 1.7 %multiply_reduce_fusion = (f32[256]{0:T(256)S(1)}, f32[256,1024]{1,0:T(8,128)S(1)}) fusion(f32[1024]{0:T(1024)} %param.16, f32[1024]{0:T(1024)} %param.15, bf16[256,1024]{1,0:T(8,128)(2,1)S(1)} %bitcast.32, bf16[1024,1024]{1,0:T(8,128)(2,1)S(1)} %copy-done), kind=kOutput, calls=%fused_computation.5 | convolution fusion | flops 538705664 | bytes 3679232 | tf_op jit(solution)/shard_map/dot_general | solution.py:153
  33.3 0.9 convolution_convert_fusion.grads_ref
  34.2 2.7 %shard_map.122 = bf16[4096,128]{1,0:T(8,128)(2,1)} custom-call(s32[8,256]{1,0:T(8,128)S(1)} %get-tuple-element.12.slot_ref, bf16[256,1024]{1,0:T(8,128)(2,1)S(1)} %convolution_convert_fusion.grads_ref), custom_call_target="tpu_custom_call" | custom-call | tf_op jit(solution)/shard_map/pallas_call | solution.py:39
  36.9 6.8 %all-to-all-done = f32[64,1,32]{2,1,0:T(1,128)S(1)} async-done(((f32[64,1,32]{2,1,0:T(1,128)}), f32[64,1,32]{2,1,0:T(1,128)S(1)}, u32[]{:S(2)}, u32[]{:S(2)}) %all-to-all-start) | async-done | bytes 8224 | tf_op jit(solution)/shard_map/all_to_all | solution.py:202
  43.7 0.6 copy-done.6
  44.4 21.3 %all-to-all-start.1 = ((bf16[512,8,128]{2,1,0:T(8,128)(2,1)}), bf16[512,8,128]{2,1,0:T(8,128)(2,1)S(1)}, u32[]{:S(2)}, u32[]{:S(2)}) async-start(bf16[512,8,128]{2,1,0:T(8,128)(2,1)} %bitcast.7), calls=%async_computation.1 | async-start | bytes 2097152 | tf_op jit(solution)/shard_map/all_to_all | solution.py:208
  65.6 0.1 pad_add_fusion.place_ref
  65.7 21.7 %all-gather = f32[512,1,32]{2,1,0:T(1,128)S(1)} all-gather(f32[64,1,32]{2,1,0:T(1,128)} %copy-done.6), channel_id=2, replica_groups={{0,128,256,384,512,640,768,896},{64,192,320,448,576,704,832,960},{1,129..., dimensions={0}, use_global_device_ids=true | all-gather | bytes 73728 | tf_op jit(solution)/shard_map/all_gather | solution.py:216
  87.4 27.7 %all-to-all-done.1 = bf16[512,8,128]{2,1,0:T(8,128)(2,1)S(1)} async-done(((bf16[512,8,128]{2,1,0:T(8,128)(2,1)}), bf16[512,8,128]{2,1,0:T(8,128)(2,1)S(1)}, u32[]{:S(2)}, u32[]{:S(2)}) %all-to-all-start.1) | async-done | bytes 1048608 | tf_op jit(solution)/shard_map/all_to_all | solution.py:208
  115.2 3.3 %shard_map.123 = (f32[128,256]{1,0:T(8,128)S(1)}, f32[128,256]{1,0:T(8,128)S(1)}) custom-call(s32[2]{0:T(128)S(1)} %pad_add_fusion.place_ref, f32[8,64,32]{2,1,0:T(8,128)S(1)} %bitcast.25, bf16[4096,128]{1,0:T(8,128)(2,1)S(1)} %bitcast.24), custom_call_target="tpu_custom_call" | custom-call | tf_op jit(solution)/shard_map/pallas_call | solution.py:39
  118.4 7.8 %collective-permute-start = (f32[128,256]{1,0:T(8,128)S(1)}, f32[128,256]{1,0:T(8,128)S(1)}, u32[]{:S(2)}, u32[]{:S(2)}) collective-permute-start(f32[128,256]{1,0:T(8,128)S(1)} %get-tuple-element.17), channel_id=1, source_target_pairs={{0,64},{64,0},{128,192},{192,128},{256,320},{320,256},{384,448},{4... | collective-permute-start | bytes 393224 | tf_op jit(solution)/shard_map/ppermute | solution.py:227
  126.3 1.0 collective-permute-done.sib_ref
  127.2 0.0 copy-done.2
  127.2 0.7 shard_map.124
  127.9 19.3 %all-gather.1 = bf16[1024,256]{1,0:T(8,128)(2,1)S(1)} all-gather(bf16[128,256]{1,0:T(8,128)(2,1)S(1)} %get-tuple-element.18), channel_id=3, replica_groups={{0,128,256,384,512,640,768,896},{64,192,320,448,576,704,832,960},{1,129..., dimensions={0}, use_global_device_ids=true | all-gather | bytes 589824 | tf_op jit(solution)/shard_map/all_gather | solution.py:236
  147.3 8.4 %collective-permute-start.1 = (bf16[8,128,256]{2,1,0:T(8,128)(2,1)S(1)}, bf16[8,128,256]{2,1,0:T(8,128)(2,1)S(1)}, u32[]{:S(2)}, u32[]{:S(2)}) collective-permute-start(bf16[8,128,256]{2,1,0:T(8,128)(2,1)S(1)} %bitcast.29), channel_id=1, source_target_pairs={{0,64},{64,0},{128,192},{192,128},{256,320},{320,256},{384,448},{4... | collective-permute-start | bytes 1572872 | tf_op jit(solution)/shard_map/ppermute | solution.py:237
  155.7 1.5 collective-permute-done.1
  157.2 0.1 select_bitcast_fusion.1
  157.3 0.1 maximum_convert_fusion
  157.4 0.0 copy-start.5
  157.5 0.1 copy.17
  157.6 1.4 copy-done.5
  159.0 1.6 bitcast_subtract_fusion
  (9 shorter events, 0.0 us)
Async XLA Ops:
  0.6 30.9 %copy-start = (bf16[1024,1024]{1,0:T(8,128)(2,1)S(1)}, bf16[1024,1024]{1,0:T(8,128)(2,1)}, u32[]{:S(2)}) copy-start(bf16[1024,1024]{1,0:T(8,128)(2,1)} %param.14) | copy-start | bytes 6291460
  0.6 1.2 copy-start.1
  1.8 0.7 copy-start.3
  7.6 36.2 %all-to-all-start = ((f32[64,1,32]{2,1,0:T(1,128)}), f32[64,1,32]{2,1,0:T(1,128)S(1)}, u32[]{:S(2)}, u32[]{:S(2)}) async-start(f32[64,1,32]{2,1,0:T(1,128)} %bitcast.5), calls=%async_computation | async-start | bytes 65536 | tf_op jit(solution)/shard_map/all_to_all | solution.py:202
  31.5 1.7 %copy-start.7 = (s32[256]{0:T(256)S(1)}, s32[256]{0:T(256)}, u32[]{:S(2)}) copy-start(s32[256]{0:T(256)} %param.12) | copy-start | bytes 3076
  31.5 1.7 %copy-start.8 = (f32[1024]{0:T(1024)S(1)}, f32[1024]{0:T(1024)}, u32[]{:S(2)}) copy-start(f32[1024]{0:T(1024)} %param.16) | copy-start | bytes 12292
  36.9 90.3 %copy-start.2 = (f32[128,256]{1,0:T(8,128)S(1)}, f32[128,256]{1,0:T(8,128)}, u32[]{:S(2)}) copy-start(f32[128,256]{1,0:T(8,128)} %moment_ref.1) | copy-start | bytes 393220
  36.9 90.3 %copy-start.4 = (f32[128]{0:T(128)S(1)}, f32[128]{0:T(128)}, u32[]{:S(2)}) copy-start(f32[128]{0:T(128)} %param.19) | copy-start | bytes 1540
  43.7 0.6 copy-start.6
  44.4 70.8 %all-to-all-start.1 = ((bf16[512,8,128]{2,1,0:T(8,128)(2,1)}), bf16[512,8,128]{2,1,0:T(8,128)(2,1)S(1)}, u32[]{:S(2)}, u32[]{:S(2)}) async-start(bf16[512,8,128]{2,1,0:T(8,128)(2,1)} %bitcast.7), calls=%async_computation.1 | async-start | bytes 2097152 | tf_op jit(solution)/shard_map/all_to_all | solution.py:208
  118.4 8.8 %collective-permute-start = (f32[128,256]{1,0:T(8,128)S(1)}, f32[128,256]{1,0:T(8,128)S(1)}, u32[]{:S(2)}, u32[]{:S(2)}) collective-permute-start(f32[128,256]{1,0:T(8,128)S(1)} %get-tuple-element.17), channel_id=1, source_target_pairs={{0,64},{64,0},{128,192},{192,128},{256,320},{320,256},{384,448},{4... | collective-permute-start | bytes 393224 | tf_op jit(solution)/shard_map/ppermute | solution.py:227
  147.3 10.0 %collective-permute-start.1 = (bf16[8,128,256]{2,1,0:T(8,128)(2,1)S(1)}, bf16[8,128,256]{2,1,0:T(8,128)(2,1)S(1)}, u32[]{:S(2)}, u32[]{:S(2)}) collective-permute-start(bf16[8,128,256]{2,1,0:T(8,128)(2,1)S(1)} %bitcast.29), channel_id=1, source_target_pairs={{0,64},{64,0},{128,192},{192,128},{256,320},{320,256},{384,448},{4... | collective-permute-start | bytes 1572872 | tf_op jit(solution)/shard_map/ppermute | solution.py:237
  157.4 1.6 copy-start.5

commit v4 on v3

--- a/solution.py
+++ b/solution.py
@@ -14,7 +14,8 @@
 BF = jnp.bfloat16
 F32 = jnp.float32
 I32 = jnp.int32
-LIMIT = 40 * 1024 * 1024
+LIMIT = 32 * 1024 * 1024
+HEAD = 112
 
 
 def iota(shape, dim):
@@ -49,10 +50,10 @@
 def route_body(ids_ref, map_ref, slot_ref, local_ref, pieces, owners, cells):
     feats, bag, batch = ids_ref.shape
     hi_count, lo_count = map_ref.shape
-    mapped = map_ref[...].astype(F32).T.astype(I32)
-    pieces[0:lo_count, :] = (mapped & 127).astype(F32).astype(BF)
-    pieces[lo_count : 2 * lo_count, :] = ((mapped >> 7) & 15).astype(F32).astype(BF)
-    pieces[2 * lo_count :, :] = (mapped >> 11).astype(F32).astype(BF)
+    mapped = map_ref[...].astype(F32).T
+    high = jnp.floor(mapped * (1.0 / 256.0))
+    pieces[0:lo_count, :] = (mapped - 256.0 * high).astype(BF)
+    pieces[lo_count:, :] = (high - 256.0).astype(BF)
     count = feats * bag
     sums = jnp.zeros((64, 32), F32)
     locs, ys, cs, ms = [], [], [], []
@@ -67,8 +68,9 @@
             part = found[k * lo_count : (k + 1) * lo_count, :]
             return jnp.sum(jnp.where(mask, part, 0.0), axis=0, keepdims=True)
 
-        loc, rep, own = pick(0), pick(1).astype(I32), pick(2).astype(I32)
-        y, c = rep >> 1, rep & 1
+        low, high = pick(0).astype(I32), pick(1).astype(I32) + 256
+        loc = (low & 127).astype(F32)
+        own, y, c = high >> 3, high & 7, low >> 7
         owner = onehot(iota((64, batch), 0) == own)
         cell = jnp.where(iota((16, batch), 0) == c * 8 + y, 1.0, 0.0)
         owners[fl] = owner
@@ -115,18 +117,23 @@
         send_ref[chunk * 2 * step : (chunk + 1) * 2 * step, :] = both.reshape(2 * step, 128).astype(BF)
 
 
-def total_body(place_ref, local_ref, got_ref, own_ref, sib_ref):
+def spots_body(place_ref, local_ref, spots_ref):
     y_here, core = place_ref[0], place_ref[1]
     n = iota((32, 512), 1)
     pick = onehot(iota((32, 512), 0) == (n & 3) * 8 + y_here)
     near = iota((64, 512), 0) == iota((64, 512), 1) >> 3
     n = iota((1, 512), 1)
     shift = ((n >> 2) & 1) * 256 + (((n >> 1) & 1) ^ core) * 128
+    for y in range(8):
+        found = dot(local_ref[y].astype(BF), pick)
+        spot = jnp.sum(jnp.where(near, found, 0.0), axis=0, keepdims=True).astype(I32)
+        spots_ref[y : y + 1, :] = spot + shift
+
+
+def total_body(spots_ref, got_ref, own_ref, sib_ref):
     acc = jnp.zeros((512, 128), F32)
     for y in range(8):
-        found = dot(local_ref[y].astype(BF), pick)
-        spot = jnp.sum(jnp.where(near, found, 0.0), axis=0, keepdims=True).astype(I32) + shift
-        hit = onehot(iota((512, 512), 0) == spot)
+        hit = onehot(iota((512, 512), 0) == spots_ref[y : y + 1, :])
         acc += dot(hit, got_ref[y * 512 : (y + 1) * 512, :])
     own_ref[:, :128] = acc[0:128]
     own_ref[:, 128:] = acc[256:384]
@@ -134,7 +141,7 @@
     sib_ref[:, 128:] = acc[384:512]
 
 
-def adam_body(own_ref, sib_ref, moment_ref, second_ref, new_moment_ref, new_second_ref, step_ref):
+def adam_body(own_ref, sib_ref, moment_ref, second_ref, new_moment_ref, new_second_ref, head_ref, tail_ref):
     grad = own_ref[...] + sib_ref[...]
     moment = BETA_ONE * moment_ref[...] + (1.0 - BETA_ONE) * grad
     mean = jnp.sum(grad * grad, axis=1, keepdims=True) * (1.0 / grad.shape[1])
@@ -144,7 +151,37 @@
     second = BETA_TWO * old + (1.0 - BETA_TWO) * mean
     new_moment_ref[...] = moment
     new_second_ref[...] = jnp.sum(jnp.where(eye, second, 0.0), axis=0, keepdims=True)
-    step_ref[...] = (LEARN_RATE * moment / (jnp.sqrt(second) + EPSILON)).astype(BF)
+    step = (LEARN_RATE * moment / (jnp.sqrt(second) + EPSILON)).astype(BF)
+    head_ref[...] = step[:HEAD]
+    tail_ref[...] = jnp.broadcast_to(step[HEAD:][None], tail_ref.shape)
+
+
+def table_body(head_ref, tail_ref, table_ref, out_ref, rows_ref, in_sems, out_sems):
+    parts = in_sems.shape[0]
+    size = rows_ref.shape[0] // parts
+
+    def span(i):
+        return pl.ds(i * size, size)
+
+    loads = [
+        pltpu.make_async_copy(table_ref.at[span(i)], rows_ref.at[span(i)], in_sems.at[i])
+        for i in range(parts)
+    ]
+    stores = [
+        pltpu.make_async_copy(rows_ref.at[span(i)], out_ref.at[span(i)], out_sems.at[i])
+        for i in range(parts)
+    ]
+    for load in loads:
+        load.start()
+    for i in range(parts):
+        loads[i].wait()
+        for r in range(i * size // 128, (i + 1) * size // 128):
+            mid = r * 128 + HEAD
+            rows_ref[r * 128 : mid, :] -= head_ref[r].astype(F32)
+            rows_ref[mid : (r + 1) * 128, :] -= tail_ref[r].astype(F32)
+        stores[i].start()
+    for store in stores:
+        store.wait()
 
 
 def pooled_grads(pooled, labels, w_hidden, b_hidden, w_out):
@@ -194,7 +231,7 @@
         row_ids.transpose(1, 2, 0),
         row_slot.reshape(1024, 128),
         scratch=[
-            pltpu.VMEM((384, 1024), BF),
+            pltpu.VMEM((256, 1024), BF),
             pltpu.VMEM((8, 64, 256), BF),
             pltpu.VMEM((8, 16, 256), F32),
         ],
@@ -216,29 +253,42 @@
     local = lax.all_gather(
         local.reshape(64, 32), rep, axis=0, tiled=False, axis_index_groups=same_core
     )
+    (spots,) = call(spots_body, [shape((8, 512), I32)], place, local, smem=1)
     own, sib = call(
         total_body,
         [shape((128, 256), F32), shape((128, 256), F32)],
-        place,
-        local,
+        spots,
         got.reshape(4096, 128),
-        smem=1,
     )
     sib = lax.ppermute(sib, rep, other_core)
-    new_moment, new_second, step = call(
+    new_moment, new_second, head, tail = call(
         adam_body,
-        [shape((128, 256), F32), shape((1, 128), F32), shape((128, 256), BF)],
+        [
+            shape((128, 256), F32),
+            shape((1, 128), F32),
+            shape((HEAD, 256), BF),
+            shape((16, 128 - HEAD, 256), BF),
+        ],
         own,
         sib,
         adam_moment,
         adam_second.reshape(1, 128),
     )
-    mine = lax.all_gather(step, rep, axis=0, tiled=False, axis_index_groups=same_core)
-    others = lax.ppermute(mine, rep, other_core)
-    even = jnp.where(core == 0, mine, others)
-    odd = jnp.where(core == 0, others, mine)
-    steps = jnp.stack([even, odd], axis=1).reshape(2048, 256)
-    new_table = emb_table - steps.astype(F32)
+    tails = lax.all_to_all(tail, rep, split_axis=0, concat_axis=0, tiled=True)
+    heads = lax.all_gather(head, rep, axis=0, tiled=False)
+    vmem, hbm = pl.BlockSpec(memory_space=pltpu.VMEM), pl.BlockSpec(memory_space=pltpu.HBM)
+    new_table = pl.pallas_call(
+        table_body,
+        out_shape=shape((2048, 256), F32),
+        in_specs=[vmem, vmem, hbm],
+        out_specs=hbm,
+        scratch_shapes=[
+            pltpu.VMEM((2048, 256), F32),
+            pltpu.SemaphoreType.DMA((4,)),
+            pltpu.SemaphoreType.DMA((4,)),
+        ],
+        compiler_params=pltpu.CompilerParams(vmem_limit_bytes=51 * 1024 * 1024),
+    )(heads, tails, emb_table)
     return (new_table, new_moment, new_second.reshape(128))
 
 

time: 161 us -> 152 us (0.944)
  starting transfers between devices: 60.3 us -> 56.2 us
  waiting for transfers between devices: 37 us -> 34.8 us
  local copies, waits for them, and re-layouts: 5.23 us -> 3.04 us
  other arithmetic: 1.88 us -> 0.09 us
    ppermute x1 -> x0, starting transfers between devices: 8.45 us -> none  [on_device(): others = lax.ppermute(mine, rep, other_core)]
    all_to_all x0 -> x1, starting transfers between devices: none -> 4.12 us  [on_device(): tails = lax.all_to_all(tail, rep, split_axis=0, concat_axis=0, tiled=True)]
    pallas_call x0 -> x1, Pallas kernels: none -> 2.46 us  [on_device(): pl.pallas_call(table_body, out_shape=shape((2048, 256), F32), in_specs=[v...]
    unnamed x19 -> x15, local copies, waits for them, and re-layouts: 5.1 us -> 3.04 us
    pallas_call x4 -> x5, Pallas kernels: 11.8 us -> 10.1 us  [call(): pl.pallas_call(body, out_shape=outs, in_specs=specs, out_specs=[pl.BlockS...]
  transfers between devices with their start and end apart: 4 -> 4, of which waited for: 4 -> 3; matrix products, arithmetic and copies ran while one was open for 2% -> 3% of each run, Pallas kernels for 2% -> 2%
where the time goes in v4:
time: 152 us
  starting transfers between devices  56.2 us (37%)
  blocking collectives  41.8 us (28%)
  waiting for transfers between devices  34.8 us (23%)
  Pallas kernels  12.6 us (8%)
  local copies, waits for them, and re-layouts  3.04 us (2%)
  matrix products  2.6 us (2%)
    all_to_all x1, waiting for transfers between devices, on_device(): lax.all_to_all(send.reshape(512, 8, 128), (rep, mp), split_axis=0, concat...  27 us
    all_to_all x1, starting transfers between devices, on_device(): lax.all_to_all(local.reshape(64, 1, 32), mp, split_axis=0, concat_axis=0,...  22.8 us
    all_gather x1, blocking collectives, on_device(): lax.all_gather(local.reshape(64, 32), rep, axis=0, tiled=False, axis_inde...  21.6 us
    all_to_all x1, starting transfers between devices, on_device(): lax.all_to_all(send.reshape(512, 8, 128), (rep, mp), split_axis=0, concat...  21.4 us
    all_gather x1, blocking collectives, on_device(): heads = lax.all_gather(head, rep, axis=0, tiled=False)  20.2 us
    pallas_call x5, Pallas kernels, call(): pl.pallas_call(body, out_shape=outs, in_specs=specs, out_specs=[pl.BlockS...  10.1 us
    ppermute x1, starting transfers between devices, on_device(): sib = lax.ppermute(sib, rep, other_core)  7.82 us
    all_to_all x1, waiting for transfers between devices, on_device(): lax.all_to_all(local.reshape(64, 1, 32), mp, split_axis=0, concat_axis=0,...  6.81 us
  transfers between devices with their start and end apart: 4, of which 3 were waited for; matrix products, arithmetic and copies ran while one was open for 3% of the time, Pallas kernels for 2%

profile of v4, /device:TPU:1, one launch (start us, length us, event | category | flops | bytes accessed | tf_op | source)
XLA Modules:
  0.0 152.0 jit_solution(5859573069793637999)
XLA Ops:
  0.6 0.0 copy-start
  0.6 0.0 copy-start.1
  0.7 1.2 copy-done.1
  1.8 0.0 copy-start.3
  1.8 0.7 copy-done.3
  2.5 4.5 %shard_map.121 = (s32[8,256]{1,0:T(8,128)S(1)}, f32[64,32]{1,0:T(8,128)}) custom-call(s32[4,2,256]{2,1,0:T(2,128)S(1)} %bitcast.22, s32[1024,128]{1,0:T(8,128)S(1)} %bitcast.21), custom_call_target="tpu_custom_call" | custom-call | tf_op jit(solution)/shard_map/pallas_call | solution.py:40
  7.0 22.8 %all-to-all-start = ((f32[64,1,32]{2,1,0:T(1,128)}), f32[64,1,32]{2,1,0:T(1,128)S(1)}, u32[]{:S(2)}, u32[]{:S(2)}) async-start(f32[64,1,32]{2,1,0:T(1,128)} %bitcast.5), calls=%async_computation | async-start | bytes 65536 | tf_op jit(solution)/shard_map/all_to_all | solution.py:239
  29.8 1.1 copy.15
  31.0 0.0 copy-done
  31.0 0.0 copy-start.5
  31.0 0.0 copy-start.6
  31.0 1.7 %multiply_reduce_fusion = (f32[256]{0:T(256)S(1)}, f32[256,1024]{1,0:T(8,128)S(1)}) fusion(f32[1024]{0:T(1024)} %param.16, f32[1024]{0:T(1024)} %param.15, bf16[256,1024]{1,0:T(8,128)(2,1)S(1)} %bitcast.25, bf16[1024,1024]{1,0:T(8,128)(2,1)S(1)} %copy-done), kind=kOutput, calls=%fused_computation.3 | convolution fusion | flops 538705664 | bytes 3679232 | tf_op jit(solution)/shard_map/dot_general | solution.py:190
  32.7 0.0 copy-done.5
  32.7 0.0 copy-done.6
  32.7 0.9 convolution_convert_fusion.grads_ref
  33.7 2.7 %shard_map.122 = bf16[4096,128]{1,0:T(8,128)(2,1)} custom-call(s32[8,256]{1,0:T(8,128)S(1)} %get-tuple-element.13.slot_ref, bf16[256,1024]{1,0:T(8,128)(2,1)S(1)} %convolution_convert_fusion.grads_ref), custom_call_target="tpu_custom_call" | custom-call | tf_op jit(solution)/shard_map/pallas_call | solution.py:40
  36.4 6.8 %all-to-all-done = f32[64,1,32]{2,1,0:T(1,128)S(1)} async-done(((f32[64,1,32]{2,1,0:T(1,128)}), f32[64,1,32]{2,1,0:T(1,128)S(1)}, u32[]{:S(2)}, u32[]{:S(2)}) %all-to-all-start) | async-done | bytes 8224 | tf_op jit(solution)/shard_map/all_to_all | solution.py:239
  43.2 21.4 %all-to-all-start.1 = ((bf16[512,8,128]{2,1,0:T(8,128)(2,1)}), bf16[512,8,128]{2,1,0:T(8,128)(2,1)S(1)}, u32[]{:S(2)}, u32[]{:S(2)}) async-start(bf16[512,8,128]{2,1,0:T(8,128)(2,1)} %bitcast.7), calls=%async_computation.1 | async-start | bytes 2097152 | tf_op jit(solution)/shard_map/all_to_all | solution.py:245
  64.7 0.1 pad_add_fusion.place_ref
  64.7 21.6 %all-gather = f32[512,1,32]{2,1,0:T(1,128)S(1)} all-gather(f32[64,1,32]{2,1,0:T(1,128)S(1)} %all-to-all-done), channel_id=2, replica_groups={{0,128,256,384,512,640,768,896},{64,192,320,448,576,704,832,960},{1,129..., dimensions={0}, use_global_device_ids=true | all-gather | bytes 73728 | tf_op jit(solution)/shard_map/all_gather | solution.py:253
  86.3 0.8 shard_map.123.spots_ref
  87.2 27.0 %all-to-all-done.1 = bf16[512,8,128]{2,1,0:T(8,128)(2,1)S(1)} async-done(((bf16[512,8,128]{2,1,0:T(8,128)(2,1)}), bf16[512,8,128]{2,1,0:T(8,128)(2,1)S(1)}, u32[]{:S(2)}, u32[]{:S(2)}) %all-to-all-start.1) | async-done | bytes 1048608 | tf_op jit(solution)/shard_map/all_to_all | solution.py:245
  114.2 1.2 shard_map.124
  115.4 7.8 %collective-permute-start = (f32[128,256]{1,0:T(8,128)S(1)}, f32[128,256]{1,0:T(8,128)S(1)}, u32[]{:S(2)}, u32[]{:S(2)}) collective-permute-start(f32[128,256]{1,0:T(8,128)S(1)} %get-tuple-element.18), channel_id=1, source_target_pairs={{0,64},{64,0},{128,192},{192,128},{256,320},{320,256},{384,448},{4... | collective-permute-start | bytes 393224 | tf_op jit(solution)/shard_map/ppermute | solution.py:263
  123.2 1.0 collective-permute-done.sib_ref
  124.2 0.0 copy-done.2
  124.2 0.0 copy-done.4
  124.2 0.8 shard_map.125
  125.0 4.1 %all-to-all-start.2 = ((bf16[16,16,256]{2,1,0:T(8,128)(2,1)}), bf16[16,16,256]{2,1,0:T(8,128)(2,1)S(1)}, u32[]{:S(2)}, u32[]{:S(2)}) async-start(bf16[16,16,256]{2,1,0:T(8,128)(2,1)} %get-tuple-element.20), calls=%async_computation.2 | async-start | bytes 262144 | tf_op jit(solution)/shard_map/all_to_all | solution.py:277
  129.1 20.2 %all-gather.1 = bf16[1792,256]{1,0:T(8,128)(2,1)S(1)} all-gather(bf16[112,256]{1,0:T(8,128)(2,1)S(1)} %get-tuple-element.19), channel_id=3, replica_groups=mesh['replica'=16,'mp'=64] {'replica'}, dimensions={0}, use_global_device_ids=true | all-gather | bytes 974848 | tf_op jit(solution)/shard_map/all_gather | solution.py:278
  149.3 0.0 all-to-all-done.2.tail_ref
  149.3 2.5 %shard_map.126 = f32[2048,256]{1,0:T(8,128)} custom-call(bf16[16,112,256]{2,1,0:T(8,128)(2,1)S(1)} %bitcast.19, bf16[16,16,256]{2,1,0:T(8,128)(2,1)S(1)} %all-to-all-done.2.tail_ref, f32[2048,256]{1,0:T(8,128)} %table_ref.1), custom_call_target="tpu_custom_call" | custom-call | tf_op jit(solution)/shard_map/pallas_call | solution.py:280
  (3 shorter events, 0.0 us)
Async XLA Ops:
  0.6 30.3 %copy-start = (bf16[1024,1024]{1,0:T(8,128)(2,1)S(1)}, bf16[1024,1024]{1,0:T(8,128)(2,1)}, u32[]{:S(2)}) copy-start(bf16[1024,1024]{1,0:T(8,128)(2,1)} %param.14) | copy-start | bytes 6291460
  0.6 1.2 copy-start.1
  1.8 0.7 copy-start.3
  7.0 36.2 %all-to-all-start = ((f32[64,1,32]{2,1,0:T(1,128)}), f32[64,1,32]{2,1,0:T(1,128)S(1)}, u32[]{:S(2)}, u32[]{:S(2)}) async-start(f32[64,1,32]{2,1,0:T(1,128)} %bitcast.5), calls=%async_computation | async-start | bytes 65536 | tf_op jit(solution)/shard_map/all_to_all | solution.py:239
  31.0 1.7 %copy-start.5 = (s32[256]{0:T(256)S(1)}, s32[256]{0:T(256)}, u32[]{:S(2)}) copy-start(s32[256]{0:T(256)} %param.12) | copy-start | bytes 3076
  31.0 1.7 %copy-start.6 = (f32[1024]{0:T(1024)S(1)}, f32[1024]{0:T(1024)}, u32[]{:S(2)}) copy-start(f32[1024]{0:T(1024)} %param.16) | copy-start | bytes 12292
  36.4 87.8 %copy-start.2 = (f32[128,256]{1,0:T(8,128)S(1)}, f32[128,256]{1,0:T(8,128)}, u32[]{:S(2)}) copy-start(f32[128,256]{1,0:T(8,128)} %moment_ref.1) | copy-start | bytes 393220
  36.4 87.8 %copy-start.4 = (f32[128]{0:T(128)S(1)}, f32[128]{0:T(128)}, u32[]{:S(2)}) copy-start(f32[128]{0:T(128)} %param.19) | copy-start | bytes 1540
  43.2 71.0 %all-to-all-start.1 = ((bf16[512,8,128]{2,1,0:T(8,128)(2,1)}), bf16[512,8,128]{2,1,0:T(8,128)(2,1)S(1)}, u32[]{:S(2)}, u32[]{:S(2)}) async-start(bf16[512,8,128]{2,1,0:T(8,128)(2,1)} %bitcast.7), calls=%async_computation.1 | async-start | bytes 2097152 | tf_op jit(solution)/shard_map/all_to_all | solution.py:245
  115.4 8.8 %collective-permute-start = (f32[128,256]{1,0:T(8,128)S(1)}, f32[128,256]{1,0:T(8,128)S(1)}, u32[]{:S(2)}, u32[]{:S(2)}) collective-permute-start(f32[128,256]{1,0:T(8,128)S(1)} %get-tuple-element.18), channel_id=1, source_target_pairs={{0,64},{64,0},{128,192},{192,128},{256,320},{320,256},{384,448},{4... | collective-permute-start | bytes 393224 | tf_op jit(solution)/shard_map/ppermute | solution.py:263
  125.0 24.3 %all-to-all-start.2 = ((bf16[16,16,256]{2,1,0:T(8,128)(2,1)}), bf16[16,16,256]{2,1,0:T(8,128)(2,1)S(1)}, u32[]{:S(2)}, u32[]{:S(2)}) async-start(bf16[16,16,256]{2,1,0:T(8,128)(2,1)} %get-tuple-element.20), calls=%async_computation.2 | async-start | bytes 262144 | tf_op jit(solution)/shard_map/all_to_all | solution.py:277

commit v5 on v4

--- a/solution.py
+++ b/solution.py
@@ -57,6 +57,7 @@
     count = feats * bag
     sums = jnp.zeros((64, 32), F32)
     locs, ys, cs, ms = [], [], [], []
+    m_here, y_here = lax.axis_index("mp"), lax.axis_index("replica") >> 1
     lane = iota((1, batch), 1).astype(F32)
     for fl in range(count):
         ids = ids_ref[fl // bag, fl % bag : fl % bag + 1, :]
@@ -71,8 +72,8 @@
         low, high = pick(0).astype(I32), pick(1).astype(I32) + 256
         loc = (low & 127).astype(F32)
         own, y, c = high >> 3, high & 7, low >> 7
-        owner = onehot(iota((64, batch), 0) == own)
-        cell = jnp.where(iota((16, batch), 0) == c * 8 + y, 1.0, 0.0)
+        owner = onehot(iota((64, batch), 0) == own ^ m_here)
+        cell = jnp.where(iota((16, batch), 0) == c * 8 + (y ^ y_here), 1.0, 0.0)
         owners[fl] = owner
         cells[fl] = cell
         terms = jnp.concatenate([cell * float(fl), cell * lane], axis=0).astype(BF)
@@ -91,9 +92,10 @@
         rank = (pair < 2.0 * (lane + float(fl * batch))).astype(I32)
         lead = cs[fl] * 2 + rank
         slot_ref[fl : fl + 1, :] = (ys[fl] * 64 + ms[fl]) * 4 + lead
-        spread = jnp.where(iota((32, batch), 0) == lead * 8 + ys[fl], locs[fl], 0.0)
+        spread = jnp.where(iota((32, batch), 0) == lead * 8 + (ys[fl] ^ y_here), locs[fl], 0.0)
         local += dot_t(owners[fl], spread.astype(BF))
-    local_ref[...] = local
+    turned = local.T
+    local_ref[...] = jnp.concatenate([turned[:16], turned[16:]], axis=1)
 
 
 def pack_body(slot_ref, grads_ref, send_ref):
@@ -117,17 +119,19 @@
         send_ref[chunk * 2 * step : (chunk + 1) * 2 * step, :] = both.reshape(2 * step, 128).astype(BF)
 
 
-def spots_body(place_ref, local_ref, spots_ref):
-    y_here, core = place_ref[0], place_ref[1]
-    n = iota((32, 512), 1)
-    pick = onehot(iota((32, 512), 0) == (n & 3) * 8 + y_here)
-    near = iota((64, 512), 0) == iota((64, 512), 1) >> 3
-    n = iota((1, 512), 1)
-    shift = ((n >> 2) & 1) * 256 + (((n >> 1) & 1) ^ core) * 128
-    for y in range(8):
-        found = dot(local_ref[y].astype(BF), pick)
-        spot = jnp.sum(jnp.where(near, found, 0.0), axis=0, keepdims=True).astype(I32)
-        spots_ref[y : y + 1, :] = spot + shift
+def spots_body(local_ref, spots_ref):
+    here = lax.axis_index("replica")
+    y_here, core = here >> 1, here & 1
+    n = iota((128, 512), 1)
+    lane = ((n >> 1) & 1) * 64 + ((n >> 3) ^ lax.axis_index("mp"))
+    found = dot(local_ref[...].astype(BF), onehot(iota((128, 512), 0) == lane)).astype(BF)
+    row = iota((8, 16), 0) ^ y_here
+    place = iota((8, 16), 1)
+    first = dot(onehot(place == row), found)
+    second = dot(onehot(place == row + 8), found)
+    n = iota((8, 512), 1)
+    spot = jnp.where((n & 1) == 0, first, second).astype(I32)
+    spots_ref[...] = spot + ((n >> 2) & 1) * 256 + (((n >> 1) & 1) ^ core) * 128
 
 
 def total_body(spots_ref, got_ref, own_ref, sib_ref):
@@ -222,12 +226,9 @@
     same_core = [[2 * y + c for y in range(8)] for c in range(2)]
     planes = [[r * 64 + m for r in group for m in range(64)] for group in same_core]
     other_core = [(i, i ^ 1) for i in range(16)]
-    core = lax.axis_index(rep) & 1
-    place = jnp.stack([lax.axis_index(rep) >> 1, core]).astype(I32)
-
     slots, local = call(
         route_body,
-        [shape((8, 256), I32), shape((64, 32), F32)],
+        [shape((8, 256), I32), shape((16, 128), F32)],
         row_ids.transpose(1, 2, 0),
         row_slot.reshape(1024, 128),
         scratch=[
@@ -235,9 +236,6 @@
             pltpu.VMEM((8, 64, 256), BF),
             pltpu.VMEM((8, 16, 256), F32),
         ],
-    )
-    local = lax.all_to_all(
-        local.reshape(64, 1, 32), mp, split_axis=0, concat_axis=0, tiled=True
     )
     grads = pooled_grads(pooled, labels, w_hidden, b_hidden, w_out)
     (send,) = call(pack_body, [shape((4096, 128), BF)], slots, grads)
@@ -250,10 +248,14 @@
         tiled=True,
         axis_index_groups=planes,
     )
-    local = lax.all_gather(
-        local.reshape(64, 32), rep, axis=0, tiled=False, axis_index_groups=same_core
-    )
-    (spots,) = call(spots_body, [shape((8, 512), I32)], place, local, smem=1)
+    rows, lanes = iota((16, 128), 0), iota((16, 128), 1)
+    for bit in (1, 2, 4):
+        other = lax.ppermute(local, rep, [(i, i ^ (2 * bit)) for i in range(16)])
+        local = jnp.where((rows & bit) != 0, other, local)
+    for bit in (1, 2, 4, 8, 16, 32):
+        other = lax.ppermute(local, mp, [(i, i ^ bit) for i in range(64)])
+        local = jnp.where((lanes & bit) != 0, other, local)
+    (spots,) = call(spots_body, [shape((8, 512), I32)], local)
     own, sib = call(
         total_body,
         [shape((128, 256), F32), shape((128, 256), F32)],

time: 152 us -> 157 us (1.033)
  starting transfers between devices: 56.2 us -> 80.8 us
  blocking collectives: 41.8 us -> 20.2 us
  Pallas kernels: 12.6 us -> 10.5 us
  waiting for transfers between devices: 34.8 us -> 36.8 us
    ppermute x0 -> x9, waiting for transfers between devices: none -> 35.8 us  [the longest x6 26.2 us: on_device(): other = lax.ppermute(local, mp, [(i, i ^ bit) for i in range(64)])]
    ppermute x0 -> x9, starting transfers between devices: none -> 31.5 us  [the longest x6 22.3 us: on_device(): other = lax.ppermute(local, mp, [(i, i ^ bit) for i in range(64)])]
    all_to_all x1, waiting for transfers between devices: 27 us -> 0.01 us  [on_device(): lax.all_to_all(send.reshape(512, 8, 128), (rep, mp), split_axis=0, concat...]
    all_to_all x1 -> x0, starting transfers between devices: 22.8 us -> none  [on_device(): lax.all_to_all(local.reshape(64, 1, 32), mp, split_axis=0, concat_axis=0,...]
    all_gather x1 -> x0, blocking collectives: 21.6 us -> none  [on_device(): lax.all_gather(local.reshape(64, 32), rep, axis=0, tiled=False, axis_inde...]
    all_to_all x1, starting transfers between devices: 21.4 us -> 36.5 us  [on_device(): lax.all_to_all(send.reshape(512, 8, 128), (rep, mp), split_axis=0, concat...]
    all_to_all x1 -> x0, waiting for transfers between devices: 6.81 us -> none  [on_device(): lax.all_to_all(local.reshape(64, 1, 32), mp, split_axis=0, concat_axis=0,...]
    all_to_all x1, starting transfers between devices: 4.12 us -> 7.12 us  [on_device(): tails = lax.all_to_all(tail, rep, split_axis=0, concat_axis=0, tiled=True)]
  transfers between devices with their start and end apart: 4 -> 12, of which waited for: 3 -> 10; matrix products, arithmetic and copies ran while one was open for 3% -> 0% of each run, Pallas kernels for 2% -> 0%
where the time goes in v5:
time: 157 us; the launch traced here: 156 us
  starting transfers between devices  80.8 us (51%)
  waiting for transfers between devices  36.8 us (23%)
  blocking collectives  20.2 us (13%)
  Pallas kernels  10.5 us (7%)
  local copies, waits for them, and re-layouts  4.06 us (3%)
  matrix products  2.61 us (2%)
    all_to_all x1, starting transfers between devices, on_device(): lax.all_to_all(send.reshape(512, 8, 128), (rep, mp), split_axis=0, concat...  36.5 us
    ppermute x6, waiting for transfers between devices, on_device(): other = lax.ppermute(local, mp, [(i, i ^ bit) for i in range(64)])  26.2 us
    ppermute x6, starting transfers between devices, on_device(): other = lax.ppermute(local, mp, [(i, i ^ bit) for i in range(64)])  22.3 us
    all_gather x1, blocking collectives, on_device(): heads = lax.all_gather(head, rep, axis=0, tiled=False)  20.2 us
    ppermute x3, waiting for transfers between devices, on_device(): other = lax.ppermute(local, rep, [(i, i ^ 2 * bit) for i in range(16)])  9.67 us
    ppermute x3, starting transfers between devices, on_device(): other = lax.ppermute(local, rep, [(i, i ^ 2 * bit) for i in range(16)])  9.27 us
    pallas_call x5, Pallas kernels, call(): pl.pallas_call(body, out_shape=outs, in_specs=specs, out_specs=[pl.BlockS...  8.05 us
    all_to_all x1, starting transfers between devices, on_device(): tails = lax.all_to_all(tail, rep, split_axis=0, concat_axis=0, tiled=True)  7.12 us
  transfers between devices with their start and end apart: 12, of which 10 were waited for; matrix products, arithmetic and copies ran while one was open for 0% of the time, Pallas kernels for 0%

profile of v5, /device:TPU:1, one launch (start us, length us, event | category | flops | bytes accessed | tf_op | source)
XLA Modules:
  0.0 156.3 jit_solution(5930410155681372685)
XLA Ops:
  0.6 1.3 copy.13
  1.9 1.0 copy-done.2
  3.7 4.0 %shard_map.121 = (s32[8,256]{1,0:T(8,128)S(1)}, f32[16,128]{1,0:T(8,128)S(1)}) custom-call(s32[4,2,256]{2,1,0:T(2,128)S(1)} %bitcast.16, s32[1024,128]{1,0:T(8,128)S(1)} %bitcast.15), custom_call_target="tpu_custom_call" | custom-call | tf_op jit(solution)/shard_map/pallas_call | solution.py:40
  7.7 1.7 %multiply_reduce_fusion = (f32[256]{0:T(256)S(1)}, f32[256,1024]{1,0:T(8,128)S(1)}) fusion(f32[1024]{0:T(1024)} %param.16, f32[1024]{0:T(1024)} %param.15, bf16[256,1024]{1,0:T(8,128)(2,1)S(1)} %bitcast.19, bf16[1024,1024]{1,0:T(8,128)(2,1)S(1)} %copy-done), kind=kOutput, calls=%fused_computation.3 | convolution fusion | flops 538705664 | bytes 3679232 | tf_op jit(solution)/shard_map/dot_general | solution.py:194
  9.4 0.9 convolution_convert_fusion.grads_ref
  10.4 1.8 %shard_map.122 = bf16[4096,128]{1,0:T(8,128)(2,1)S(1)} custom-call(s32[8,256]{1,0:T(8,128)S(1)} %get-tuple-element.13.slot_ref, bf16[256,1024]{1,0:T(8,128)(2,1)S(1)} %convolution_convert_fusion.grads_ref), custom_call_target="tpu_custom_call" | custom-call | tf_op jit(solution)/shard_map/pallas_call | solution.py:40
  12.2 1.0 copy-done.1
  13.1 36.5 %all-to-all-start = ((bf16[512,8,128]{2,1,0:T(8,128)(2,1)}), bf16[512,8,128]{2,1,0:T(8,128)(2,1)S(1)}, u32[]{:S(2)}, u32[]{:S(2)}) async-start(bf16[512,8,128]{2,1,0:T(8,128)(2,1)} %bitcast.13), calls=%async_computation | async-start | bytes 2097152 | tf_op jit(solution)/shard_map/all_to_all | solution.py:243
  49.6 1.9 %collective-permute-start = (f32[16,128]{1,0:T(8,128)S(1)}, f32[16,128]{1,0:T(8,128)S(1)}, u32[]{:S(2)}, u32[]{:S(2)}) collective-permute-start(f32[16,128]{1,0:T(8,128)S(1)} %get-tuple-element.15), channel_id=1, source_target_pairs={{0,128},{64,192},{128,0},{192,64},{256,384},{320,448},{384,256},{4... | collective-permute-start | bytes 24584 | tf_op jit(solution)/shard_map/ppermute | solution.py:253
  51.6 2.8 %collective-permute-done = f32[16,128]{1,0:T(8,128)S(1)} collective-permute-done((f32[16,128]{1,0:T(8,128)S(1)}, f32[16,128]{1,0:T(8,128)S(1)}, u32[]{:S(2)}, u32[]{:S(2)}) %collective-permute-start) | collective-permute-done | bytes 8224 | tf_op jit(solution)/shard_map/ppermute | solution.py:253
  54.4 1.9 %collective-permute-start.1 = (f32[16,128]{1,0:T(8,128)S(1)}, f32[16,128]{1,0:T(8,128)S(1)}, u32[]{:S(2)}, u32[]{:S(2)}) collective-permute-start(f32[16,128]{1,0:T(8,128)S(1)} %broadcast_select_fusion), channel_id=1, source_target_pairs={{0,256},{64,320},{128,384},{192,448},{256,0},{320,64},{384,128},{4... | collective-permute-start | bytes 24584 | tf_op jit(solution)/shard_map/ppermute | solution.py:253
  56.3 3.7 %collective-permute-done.1 = f32[16,128]{1,0:T(8,128)S(1)} collective-permute-done((f32[16,128]{1,0:T(8,128)S(1)}, f32[16,128]{1,0:T(8,128)S(1)}, u32[]{:S(2)}, u32[]{:S(2)}) %collective-permute-start.1) | collective-permute-done | bytes 8224 | tf_op jit(solution)/shard_map/ppermute | solution.py:253
  60.1 5.4 %collective-permute-start.2 = (f32[16,128]{1,0:T(8,128)S(1)}, f32[16,128]{1,0:T(8,128)S(1)}, u32[]{:S(2)}, u32[]{:S(2)}) collective-permute-start(f32[16,128]{1,0:T(8,128)S(1)} %broadcast_select_fusion.1), channel_id=1, source_target_pairs={{0,512},{64,576},{128,640},{192,704},{256,768},{320,832},{384,896}... | collective-permute-start | bytes 24584 | tf_op jit(solution)/shard_map/ppermute | solution.py:253
  65.6 3.2 %collective-permute-done.2 = f32[16,128]{1,0:T(8,128)S(1)} collective-permute-done((f32[16,128]{1,0:T(8,128)S(1)}, f32[16,128]{1,0:T(8,128)S(1)}, u32[]{:S(2)}, u32[]{:S(2)}) %collective-permute-start.2) | collective-permute-done | bytes 8224 | tf_op jit(solution)/shard_map/ppermute | solution.py:253
  68.8 1.9 %collective-permute-start.3 = (f32[16,128]{1,0:T(8,128)S(1)}, f32[16,128]{1,0:T(8,128)S(1)}, u32[]{:S(2)}, u32[]{:S(2)}) collective-permute-start(f32[16,128]{1,0:T(8,128)S(1)} %broadcast_select_fusion.2), channel_id=1, source_target_pairs={{0,1},{1,0},{2,3},{3,2},{4,5},{5,4},{6,7},{7,6},{8,9},{9,8},{10,11... | collective-permute-start | bytes 24584 | tf_op jit(solution)/shard_map/ppermute | solution.py:256
  70.8 2.8 %collective-permute-done.3 = f32[16,128]{1,0:T(8,128)S(1)} collective-permute-done((f32[16,128]{1,0:T(8,128)S(1)}, f32[16,128]{1,0:T(8,128)S(1)}, u32[]{:S(2)}, u32[]{:S(2)}) %collective-permute-start.3) | collective-permute-done | bytes 8224 | tf_op jit(solution)/shard_map/ppermute | solution.py:256
  73.5 2.7 %collective-permute-start.4 = (f32[16,128]{1,0:T(8,128)S(1)}, f32[16,128]{1,0:T(8,128)S(1)}, u32[]{:S(2)}, u32[]{:S(2)}) collective-permute-start(f32[16,128]{1,0:T(8,128)S(1)} %broadcast_select_fusion.3), channel_id=1, source_target_pairs={{0,2},{1,3},{2,0},{3,1},{4,6},{5,7},{6,4},{7,5},{8,10},{9,11},{10,... | collective-permute-start | bytes 24584 | tf_op jit(solution)/shard_map/ppermute | solution.py:256
  76.2 3.5 %collective-permute-done.4 = f32[16,128]{1,0:T(8,128)S(1)} collective-permute-done((f32[16,128]{1,0:T(8,128)S(1)}, f32[16,128]{1,0:T(8,128)S(1)}, u32[]{:S(2)}, u32[]{:S(2)}) %collective-permute-start.4) | collective-permute-done | bytes 8224 | tf_op jit(solution)/shard_map/ppermute | solution.py:256
  79.8 1.9 %collective-permute-start.5 = (f32[16,128]{1,0:T(8,128)S(1)}, f32[16,128]{1,0:T(8,128)S(1)}, u32[]{:S(2)}, u32[]{:S(2)}) collective-permute-start(f32[16,128]{1,0:T(8,128)S(1)} %broadcast_select_fusion.4), channel_id=1, source_target_pairs={{0,4},{1,5},{2,6},{3,7},{4,0},{5,1},{6,2},{7,3},{8,12},{9,13},{10,... | collective-permute-start | bytes 24584 | tf_op jit(solution)/shard_map/ppermute | solution.py:256
  81.7 8.5 %collective-permute-done.5 = f32[16,128]{1,0:T(8,128)S(1)} collective-permute-done((f32[16,128]{1,0:T(8,128)S(1)}, f32[16,128]{1,0:T(8,128)S(1)}, u32[]{:S(2)}, u32[]{:S(2)}) %collective-permute-start.5) | collective-permute-done | bytes 8224 | tf_op jit(solution)/shard_map/ppermute | solution.py:256
  90.2 1.9 %collective-permute-start.6 = (f32[16,128]{1,0:T(8,128)S(1)}, f32[16,128]{1,0:T(8,128)S(1)}, u32[]{:S(2)}, u32[]{:S(2)}) collective-permute-start(f32[16,128]{1,0:T(8,128)S(1)} %broadcast_select_fusion.5), channel_id=1, source_target_pairs={{0,8},{1,9},{2,10},{3,11},{4,12},{5,13},{6,14},{7,15},{8,0},{9,1},... | collective-permute-start | bytes 24584 | tf_op jit(solution)/shard_map/ppermute | solution.py:256
  92.1 3.6 %collective-permute-done.6 = f32[16,128]{1,0:T(8,128)S(1)} collective-permute-done((f32[16,128]{1,0:T(8,128)S(1)}, f32[16,128]{1,0:T(8,128)S(1)}, u32[]{:S(2)}, u32[]{:S(2)}) %collective-permute-start.6) | collective-permute-done | bytes 8224 | tf_op jit(solution)/shard_map/ppermute | solution.py:256
  95.8 4.3 %collective-permute-start.7 = (f32[16,128]{1,0:T(8,128)S(1)}, f32[16,128]{1,0:T(8,128)S(1)}, u32[]{:S(2)}, u32[]{:S(2)}) collective-permute-start(f32[16,128]{1,0:T(8,128)S(1)} %broadcast_select_fusion.6), channel_id=1, source_target_pairs={{0,16},{1,17},{2,18},{3,19},{4,20},{5,21},{6,22},{7,23},{8,24},{9,... | collective-permute-start | bytes 24584 | tf_op jit(solution)/shard_map/ppermute | solution.py:256
  100.1 4.2 %collective-permute-done.7 = f32[16,128]{1,0:T(8,128)S(1)} collective-permute-done((f32[16,128]{1,0:T(8,128)S(1)}, f32[16,128]{1,0:T(8,128)S(1)}, u32[]{:S(2)}, u32[]{:S(2)}) %collective-permute-start.7) | collective-permute-done | bytes 8224 | tf_op jit(solution)/shard_map/ppermute | solution.py:256
  104.3 9.6 %collective-permute-start.8 = (f32[16,128]{1,0:T(8,128)S(1)}, f32[16,128]{1,0:T(8,128)S(1)}, u32[]{:S(2)}, u32[]{:S(2)}) collective-permute-start(f32[16,128]{1,0:T(8,128)S(1)} %broadcast_select_fusion.7), channel_id=1, source_target_pairs={{0,32},{1,33},{2,34},{3,35},{4,36},{5,37},{6,38},{7,39},{8,40},{9,... | collective-permute-start | bytes 24584 | tf_op jit(solution)/shard_map/ppermute | solution.py:256
  113.9 3.5 %collective-permute-done.8 = f32[16,128]{1,0:T(8,128)S(1)} collective-permute-done((f32[16,128]{1,0:T(8,128)S(1)}, f32[16,128]{1,0:T(8,128)S(1)}, u32[]{:S(2)}, u32[]{:S(2)}) %collective-permute-start.8) | collective-permute-done | bytes 8224 | tf_op jit(solution)/shard_map/ppermute | solution.py:256
  117.7 1.2 shard_map.124
  119.0 5.6 %collective-permute-start.9 = (f32[128,256]{1,0:T(8,128)S(1)}, f32[128,256]{1,0:T(8,128)S(1)}, u32[]{:S(2)}, u32[]{:S(2)}) collective-permute-start(f32[128,256]{1,0:T(8,128)S(1)} %get-tuple-element.18), channel_id=1, source_target_pairs={{0,64},{64,0},{128,192},{192,128},{256,320},{320,256},{384,448},{4... | collective-permute-start | bytes 393224 | tf_op jit(solution)/shard_map/ppermute | solution.py:265
  124.6 1.0 collective-permute-done.9.sib_ref
  126.4 7.1 %all-to-all-start.1 = ((bf16[16,16,256]{2,1,0:T(8,128)(2,1)}), bf16[16,16,256]{2,1,0:T(8,128)(2,1)S(1)}, u32[]{:S(2)}, u32[]{:S(2)}) async-start(bf16[16,16,256]{2,1,0:T(8,128)(2,1)} %get-tuple-element.20), calls=%async_computation.1 | async-start | bytes 262144 | tf_op jit(solution)/shard_map/all_to_all | solution.py:279
  133.5 20.2 %all-gather = bf16[1792,256]{1,0:T(8,128)(2,1)S(1)} all-gather(bf16[112,256]{1,0:T(8,128)(2,1)S(1)} %get-tuple-element.19), channel_id=2, replica_groups=mesh['replica'=16,'mp'=64] {'replica'}, dimensions={0}, use_global_device_ids=true | all-gather | bytes 974848 | tf_op jit(solution)/shard_map/all_gather | solution.py:280
  153.7 2.5 %shard_map.126 = f32[2048,256]{1,0:T(8,128)} custom-call(bf16[16,112,256]{2,1,0:T(8,128)(2,1)S(1)} %bitcast.14, bf16[16,16,256]{2,1,0:T(8,128)(2,1)S(1)} %all-to-all-done.1.tail_ref, f32[2048,256]{1,0:T(8,128)} %table_ref.1), custom_call_target="tpu_custom_call" | custom-call | tf_op jit(solution)/shard_map/pallas_call | solution.py:282
  (37 shorter events, 2.2 us)
Async XLA Ops:
  0.6 7.0 %copy-start = (bf16[1024,1024]{1,0:T(8,128)(2,1)S(1)}, bf16[1024,1024]{1,0:T(8,128)(2,1)}, u32[]{:S(2)}) copy-start(bf16[1024,1024]{1,0:T(8,128)(2,1)} %param.14) | copy-start | bytes 6291460
  1.9 1.0 copy-start.2
  3.0 0.7 copy-start.4
  7.6 1.8 %copy-start.6 = (s32[256]{0:T(256)S(1)}, s32[256]{0:T(256)}, u32[]{:S(2)}) copy-start(s32[256]{0:T(256)} %param.12) | copy-start | bytes 3076
  7.6 1.8 %copy-start.7 = (f32[1024]{0:T(1024)S(1)}, f32[1024]{0:T(1024)}, u32[]{:S(2)}) copy-start(f32[1024]{0:T(1024)} %param.16) | copy-start | bytes 12292
  12.1 1.0 copy-start.1
  13.1 112.5 %copy-start.3 = (f32[128,256]{1,0:T(8,128)S(1)}, f32[128,256]{1,0:T(8,128)}, u32[]{:S(2)}) copy-start(f32[128,256]{1,0:T(8,128)} %moment_ref.1) | copy-start | bytes 393220
  13.1 112.5 %copy-start.5 = (f32[128]{0:T(128)S(1)}, f32[128]{0:T(128)}, u32[]{:S(2)}) copy-start(f32[128]{0:T(128)} %param.19) | copy-start | bytes 1540
  13.1 104.6 %all-to-all-start = ((bf16[512,8,128]{2,1,0:T(8,128)(2,1)}), bf16[512,8,128]{2,1,0:T(8,128)(2,1)S(1)}, u32[]{:S(2)}, u32[]{:S(2)}) async-start(bf16[512,8,128]{2,1,0:T(8,128)(2,1)} %bitcast.13), calls=%async_computation | async-start | bytes 2097152 | tf_op jit(solution)/shard_map/all_to_all | solution.py:243
  49.6 4.7 %collective-permute-start = (f32[16,128]{1,0:T(8,128)S(1)}, f32[16,128]{1,0:T(8,128)S(1)}, u32[]{:S(2)}, u32[]{:S(2)}) collective-permute-start(f32[16,128]{1,0:T(8,128)S(1)} %get-tuple-element.15), channel_id=1, source_target_pairs={{0,128},{64,192},{128,0},{192,64},{256,384},{320,448},{384,256},{4... | collective-permute-start | bytes 24584 | tf_op jit(solution)/shard_map/ppermute | solution.py:253
  54.4 5.6 %collective-permute-start.1 = (f32[16,128]{1,0:T(8,128)S(1)}, f32[16,128]{1,0:T(8,128)S(1)}, u32[]{:S(2)}, u32[]{:S(2)}) collective-permute-start(f32[16,128]{1,0:T(8,128)S(1)} %broadcast_select_fusion), channel_id=1, source_target_pairs={{0,256},{64,320},{128,384},{192,448},{256,0},{320,64},{384,128},{4... | collective-permute-start | bytes 24584 | tf_op jit(solution)/shard_map/ppermute | solution.py:253
  60.1 8.7 %collective-permute-start.2 = (f32[16,128]{1,0:T(8,128)S(1)}, f32[16,128]{1,0:T(8,128)S(1)}, u32[]{:S(2)}, u32[]{:S(2)}) collective-permute-start(f32[16,128]{1,0:T(8,128)S(1)} %broadcast_select_fusion.1), channel_id=1, source_target_pairs={{0,512},{64,576},{128,640},{192,704},{256,768},{320,832},{384,896}... | collective-permute-start | bytes 24584 | tf_op jit(solution)/shard_map/ppermute | solution.py:253
  68.8 4.7 %collective-permute-start.3 = (f32[16,128]{1,0:T(8,128)S(1)}, f32[16,128]{1,0:T(8,128)S(1)}, u32[]{:S(2)}, u32[]{:S(2)}) collective-permute-start(f32[16,128]{1,0:T(8,128)S(1)} %broadcast_select_fusion.2), channel_id=1, source_target_pairs={{0,1},{1,0},{2,3},{3,2},{4,5},{5,4},{6,7},{7,6},{8,9},{9,8},{10,11... | collective-permute-start | bytes 24584 | tf_op jit(solution)/shard_map/ppermute | solution.py:256
  73.5 6.2 %collective-permute-start.4 = (f32[16,128]{1,0:T(8,128)S(1)}, f32[16,128]{1,0:T(8,128)S(1)}, u32[]{:S(2)}, u32[]{:S(2)}) collective-permute-start(f32[16,128]{1,0:T(8,128)S(1)} %broadcast_select_fusion.3), channel_id=1, source_target_pairs={{0,2},{1,3},{2,0},{3,1},{4,6},{5,7},{6,4},{7,5},{8,10},{9,11},{10,... | collective-permute-start | bytes 24584 | tf_op jit(solution)/shard_map/ppermute | solution.py:256
  79.8 10.4 %collective-permute-start.5 = (f32[16,128]{1,0:T(8,128)S(1)}, f32[16,128]{1,0:T(8,128)S(1)}, u32[]{:S(2)}, u32[]{:S(2)}) collective-permute-start(f32[16,128]{1,0:T(8,128)S(1)} %broadcast_select_fusion.4), channel_id=1, source_target_pairs={{0,4},{1,5},{2,6},{3,7},{4,0},{5,1},{6,2},{7,3},{8,12},{9,13},{10,... | collective-permute-start | bytes 24584 | tf_op jit(solution)/shard_map/ppermute | solution.py:256
  90.2 5.6 %collective-permute-start.6 = (f32[16,128]{1,0:T(8,128)S(1)}, f32[16,128]{1,0:T(8,128)S(1)}, u32[]{:S(2)}, u32[]{:S(2)}) collective-permute-start(f32[16,128]{1,0:T(8,128)S(1)} %broadcast_select_fusion.5), channel_id=1, source_target_pairs={{0,8},{1,9},{2,10},{3,11},{4,12},{5,13},{6,14},{7,15},{8,0},{9,1},... | collective-permute-start | bytes 24584 | tf_op jit(solution)/shard_map/ppermute | solution.py:256
  95.8 8.5 %collective-permute-start.7 = (f32[16,128]{1,0:T(8,128)S(1)}, f32[16,128]{1,0:T(8,128)S(1)}, u32[]{:S(2)}, u32[]{:S(2)}) collective-permute-start(f32[16,128]{1,0:T(8,128)S(1)} %broadcast_select_fusion.6), channel_id=1, source_target_pairs={{0,16},{1,17},{2,18},{3,19},{4,20},{5,21},{6,22},{7,23},{8,24},{9,... | collective-permute-start | bytes 24584 | tf_op jit(solution)/shard_map/ppermute | solution.py:256
  104.3 13.1 %collective-permute-start.8 = (f32[16,128]{1,0:T(8,128)S(1)}, f32[16,128]{1,0:T(8,128)S(1)}, u32[]{:S(2)}, u32[]{:S(2)}) collective-permute-start(f32[16,128]{1,0:T(8,128)S(1)} %broadcast_select_fusion.7), channel_id=1, source_target_pairs={{0,32},{1,33},{2,34},{3,35},{4,36},{5,37},{6,38},{7,39},{8,40},{9,... | collective-permute-start | bytes 24584 | tf_op jit(solution)/shard_map/ppermute | solution.py:256
  119.0 6.6 %collective-permute-start.9 = (f32[128,256]{1,0:T(8,128)S(1)}, f32[128,256]{1,0:T(8,128)S(1)}, u32[]{:S(2)}, u32[]{:S(2)}) collective-permute-start(f32[128,256]{1,0:T(8,128)S(1)} %get-tuple-element.18), channel_id=1, source_target_pairs={{0,64},{64,0},{128,192},{192,128},{256,320},{320,256},{384,448},{4... | collective-permute-start | bytes 393224 | tf_op jit(solution)/shard_map/ppermute | solution.py:265
  126.4 27.3 %all-to-all-start.1 = ((bf16[16,16,256]{2,1,0:T(8,128)(2,1)}), bf16[16,16,256]{2,1,0:T(8,128)(2,1)S(1)}, u32[]{:S(2)}, u32[]{:S(2)}) async-start(bf16[16,16,256]{2,1,0:T(8,128)(2,1)} %get-tuple-element.20), calls=%async_computation.1 | async-start | bytes 262144 | tf_op jit(solution)/shard_map/all_to_all | solution.py:279

commit v6 on v5

--- a/solution.py
+++ b/solution.py
@@ -237,6 +237,10 @@
             pltpu.VMEM((8, 16, 256), F32),
         ],
     )
+    rows, lanes = iota((16, 128), 0), iota((16, 128), 1)
+    for bit in (1, 2, 4):
+        other = lax.ppermute(local, rep, [(i, i ^ (2 * bit)) for i in range(16)])
+        local = jnp.where((rows & bit) != 0, other, local)
     grads = pooled_grads(pooled, labels, w_hidden, b_hidden, w_out)
     (send,) = call(pack_body, [shape((4096, 128), BF)], slots, grads)
     send, local = lax.optimization_barrier((send, local))
@@ -248,10 +252,6 @@
         tiled=True,
         axis_index_groups=planes,
     )
-    rows, lanes = iota((16, 128), 0), iota((16, 128), 1)
-    for bit in (1, 2, 4):
-        other = lax.ppermute(local, rep, [(i, i ^ (2 * bit)) for i in range(16)])
-        local = jnp.where((rows & bit) != 0, other, local)
     for bit in (1, 2, 4, 8, 16, 32):
         other = lax.ppermute(local, mp, [(i, i ^ bit) for i in range(64)])
         local = jnp.where((lanes & bit) != 0, other, local)

time: 157 us -> 170 us (1.083)
  waiting for transfers between devices: 36.8 us -> 49.7 us
    ppermute x6, waiting for transfers between devices: 26.2 us -> 47.6 us  [on_device(): other = lax.ppermute(local, mp, [(i, i ^ bit) for i in range(64)])]
    ppermute x3, waiting for transfers between devices: 9.67 us -> 1.06 us  [on_device(): other = lax.ppermute(local, rep, [(i, i ^ 2 * bit) for i in range(16)])]
    ppermute x3, starting transfers between devices: 9.27 us -> 14.8 us  [on_device(): other = lax.ppermute(local, rep, [(i, i ^ 2 * bit) for i in range(16)])]
    ppermute x6, starting transfers between devices: 22.3 us -> 19.1 us  [on_device(): other = lax.ppermute(local, mp, [(i, i ^ bit) for i in range(64)])]
    all_to_all x1, starting transfers between devices: 36.5 us -> 33.6 us  [on_device(): lax.all_to_all(send.reshape(512, 8, 128), (rep, mp), split_axis=0, concat...]
    unnamed x17 -> x15, local copies, waits for them, and re-layouts: 4.06 us -> 3.05 us
  transfers between devices with their start and end apart: 12 -> 12, of which waited for: 10 -> 8; matrix products, arithmetic and copies ran while one was open for 0% -> 2% of each run, Pallas kernels for 0% -> 2%
where the time goes in v6:
time: 170 us
  starting transfers between devices  81.2 us (48%)
  waiting for transfers between devices  49.7 us (29%)
  blocking collectives  20.2 us (12%)
  Pallas kernels  11.5 us (7%)
  local copies, waits for them, and re-layouts  3.05 us (2%)
  matrix products  2.6 us (2%)
    ppermute x6, waiting for transfers between devices, on_device(): other = lax.ppermute(local, mp, [(i, i ^ bit) for i in range(64)])  47.6 us
    all_to_all x1, starting transfers between devices, on_device(): lax.all_to_all(send.reshape(512, 8, 128), (rep, mp), split_axis=0, concat...  33.6 us
    all_gather x1, blocking collectives, on_device(): heads = lax.all_gather(head, rep, axis=0, tiled=False)  20.2 us
    ppermute x6, starting transfers between devices, on_device(): other = lax.ppermute(local, mp, [(i, i ^ bit) for i in range(64)])  19.1 us
    ppermute x3, starting transfers between devices, on_device(): other = lax.ppermute(local, rep, [(i, i ^ 2 * bit) for i in range(16)])  14.8 us
    pallas_call x5, Pallas kernels, call(): pl.pallas_call(body, out_shape=outs, in_specs=specs, out_specs=[pl.BlockS...  9.02 us
    all_to_all x1, starting transfers between devices, on_device(): tails = lax.all_to_all(tail, rep, split_axis=0, concat_axis=0, tiled=True)  7.23 us
    ppermute x1, starting transfers between devices, on_device(): sib = lax.ppermute(sib, rep, other_core)  6.44 us
  transfers between devices with their start and end apart: 12, of which 8 were waited for; matrix products, arithmetic and copies ran while one was open for 2% of the time, Pallas kernels for 2%

profile of v6, /device:TPU:1, one launch (start us, length us, event | category | flops | bytes accessed | tf_op | source)
XLA Modules:
  0.0 169.6 jit_solution(15729972944172354035)
XLA Ops:
  0.7 1.2 copy-done.1
  1.8 0.7 copy-done.3
  2.5 4.0 %shard_map.121 = (s32[8,256]{1,0:T(8,128)S(1)}, f32[16,128]{1,0:T(8,128)S(1)}) custom-call(s32[4,2,256]{2,1,0:T(2,128)S(1)} %bitcast.15, s32[1024,128]{1,0:T(8,128)S(1)} %bitcast.14), custom_call_target="tpu_custom_call" | custom-call | tf_op jit(solution)/shard_map/pallas_call | solution.py:40
  6.5 4.1 %collective-permute-start = (f32[16,128]{1,0:T(8,128)S(1)}, f32[16,128]{1,0:T(8,128)S(1)}, u32[]{:S(2)}, u32[]{:S(2)}) collective-permute-start(f32[16,128]{1,0:T(8,128)S(1)} %get-tuple-element.14), channel_id=1, source_target_pairs={{0,128},{64,192},{128,0},{192,64},{256,384},{320,448},{384,256},{4... | collective-permute-start | bytes 24584 | tf_op jit(solution)/shard_map/ppermute | solution.py:242
  10.6 1.1 copy.13
  11.8 1.7 multiply_reduce_fusion
  13.5 0.9 convolution_convert_fusion.grads_ref
  14.5 4.2 %collective-permute-start.1 = (f32[16,128]{1,0:T(8,128)S(1)}, f32[16,128]{1,0:T(8,128)S(1)}, u32[]{:S(2)}, u32[]{:S(2)}) collective-permute-start(f32[16,128]{1,0:T(8,128)S(1)} %broadcast_select_fusion), channel_id=1, source_target_pairs={{0,256},{64,320},{128,384},{192,448},{256,0},{320,64},{384,128},{4... | collective-permute-start | bytes 24584 | tf_op jit(solution)/shard_map/ppermute | solution.py:242
  18.7 1.1 collective-permute-done.1
  19.9 6.5 %collective-permute-start.2 = (f32[16,128]{1,0:T(8,128)S(1)}, f32[16,128]{1,0:T(8,128)S(1)}, u32[]{:S(2)}, u32[]{:S(2)}) collective-permute-start(f32[16,128]{1,0:T(8,128)S(1)} %broadcast_select_fusion.1), channel_id=1, source_target_pairs={{0,512},{64,576},{128,640},{192,704},{256,768},{320,832},{384,896}... | collective-permute-start | bytes 24584 | tf_op jit(solution)/shard_map/ppermute | solution.py:242
  26.5 2.7 %shard_map.122 = bf16[4096,128]{1,0:T(8,128)(2,1)} custom-call(s32[8,256]{1,0:T(8,128)S(1)} %get-tuple-element.13.slot_ref, bf16[256,1024]{1,0:T(8,128)(2,1)S(1)} %convolution_convert_fusion.grads_ref), custom_call_target="tpu_custom_call" | custom-call | tf_op jit(solution)/shard_map/pallas_call | solution.py:40
  29.3 33.6 %all-to-all-start = ((bf16[512,8,128]{2,1,0:T(8,128)(2,1)}), bf16[512,8,128]{2,1,0:T(8,128)(2,1)S(1)}, u32[]{:S(2)}, u32[]{:S(2)}) async-start(bf16[512,8,128]{2,1,0:T(8,128)(2,1)} %bitcast.2), calls=%async_computation | async-start | bytes 2097152 | tf_op jit(solution)/shard_map/all_to_all | solution.py:247
  62.9 1.9 %collective-permute-start.3 = (f32[16,128]{1,0:T(8,128)S(1)}, f32[16,128]{1,0:T(8,128)S(1)}, u32[]{:S(2)}, u32[]{:S(2)}) collective-permute-start(f32[16,128]{1,0:T(8,128)S(1)} %broadcast_select_fusion.2), channel_id=1, source_target_pairs={{0,1},{1,0},{2,3},{3,2},{4,5},{5,4},{6,7},{7,6},{8,9},{9,8},{10,11... | collective-permute-start | bytes 24584 | tf_op jit(solution)/shard_map/ppermute | solution.py:256
  64.8 2.8 %collective-permute-done.3 = f32[16,128]{1,0:T(8,128)S(1)} collective-permute-done((f32[16,128]{1,0:T(8,128)S(1)}, f32[16,128]{1,0:T(8,128)S(1)}, u32[]{:S(2)}, u32[]{:S(2)}) %collective-permute-start.3) | collective-permute-done | bytes 8224 | tf_op jit(solution)/shard_map/ppermute | solution.py:256
  67.6 1.9 %collective-permute-start.4 = (f32[16,128]{1,0:T(8,128)S(1)}, f32[16,128]{1,0:T(8,128)S(1)}, u32[]{:S(2)}, u32[]{:S(2)}) collective-permute-start(f32[16,128]{1,0:T(8,128)S(1)} %broadcast_select_fusion.3), channel_id=1, source_target_pairs={{0,2},{1,3},{2,0},{3,1},{4,6},{5,7},{6,4},{7,5},{8,10},{9,11},{10,... | collective-permute-start | bytes 24584 | tf_op jit(solution)/shard_map/ppermute | solution.py:256
  69.5 4.3 %collective-permute-done.4 = f32[16,128]{1,0:T(8,128)S(1)} collective-permute-done((f32[16,128]{1,0:T(8,128)S(1)}, f32[16,128]{1,0:T(8,128)S(1)}, u32[]{:S(2)}, u32[]{:S(2)}) %collective-permute-start.4) | collective-permute-done | bytes 8224 | tf_op jit(solution)/shard_map/ppermute | solution.py:256
  73.8 1.9 %collective-permute-start.5 = (f32[16,128]{1,0:T(8,128)S(1)}, f32[16,128]{1,0:T(8,128)S(1)}, u32[]{:S(2)}, u32[]{:S(2)}) collective-permute-start(f32[16,128]{1,0:T(8,128)S(1)} %broadcast_select_fusion.4), channel_id=1, source_target_pairs={{0,4},{1,5},{2,6},{3,7},{4,0},{5,1},{6,2},{7,3},{8,12},{9,13},{10,... | collective-permute-start | bytes 24584 | tf_op jit(solution)/shard_map/ppermute | solution.py:256
  75.7 26.7 %collective-permute-done.5 = f32[16,128]{1,0:T(8,128)S(1)} collective-permute-done((f32[16,128]{1,0:T(8,128)S(1)}, f32[16,128]{1,0:T(8,128)S(1)}, u32[]{:S(2)}, u32[]{:S(2)}) %collective-permute-start.5) | collective-permute-done | bytes 8224 | tf_op jit(solution)/shard_map/ppermute | solution.py:256
  102.5 1.9 %collective-permute-start.6 = (f32[16,128]{1,0:T(8,128)S(1)}, f32[16,128]{1,0:T(8,128)S(1)}, u32[]{:S(2)}, u32[]{:S(2)}) collective-permute-start(f32[16,128]{1,0:T(8,128)S(1)} %broadcast_select_fusion.5), channel_id=1, source_target_pairs={{0,8},{1,9},{2,10},{3,11},{4,12},{5,13},{6,14},{7,15},{8,0},{9,1},... | collective-permute-start | bytes 24584 | tf_op jit(solution)/shard_map/ppermute | solution.py:256
  104.4 3.6 %collective-permute-done.6 = f32[16,128]{1,0:T(8,128)S(1)} collective-permute-done((f32[16,128]{1,0:T(8,128)S(1)}, f32[16,128]{1,0:T(8,128)S(1)}, u32[]{:S(2)}, u32[]{:S(2)}) %collective-permute-start.6) | collective-permute-done | bytes 8224 | tf_op jit(solution)/shard_map/ppermute | solution.py:256
  108.1 3.3 %collective-permute-start.7 = (f32[16,128]{1,0:T(8,128)S(1)}, f32[16,128]{1,0:T(8,128)S(1)}, u32[]{:S(2)}, u32[]{:S(2)}) collective-permute-start(f32[16,128]{1,0:T(8,128)S(1)} %broadcast_select_fusion.6), channel_id=1, source_target_pairs={{0,16},{1,17},{2,18},{3,19},{4,20},{5,21},{6,22},{7,23},{8,24},{9,... | collective-permute-start | bytes 24584 | tf_op jit(solution)/shard_map/ppermute | solution.py:256
  111.3 5.3 %collective-permute-done.7 = f32[16,128]{1,0:T(8,128)S(1)} collective-permute-done((f32[16,128]{1,0:T(8,128)S(1)}, f32[16,128]{1,0:T(8,128)S(1)}, u32[]{:S(2)}, u32[]{:S(2)}) %collective-permute-start.7) | collective-permute-done | bytes 8224 | tf_op jit(solution)/shard_map/ppermute | solution.py:256
  116.7 8.2 %collective-permute-start.8 = (f32[16,128]{1,0:T(8,128)S(1)}, f32[16,128]{1,0:T(8,128)S(1)}, u32[]{:S(2)}, u32[]{:S(2)}) collective-permute-start(f32[16,128]{1,0:T(8,128)S(1)} %broadcast_select_fusion.7), channel_id=1, source_target_pairs={{0,32},{1,33},{2,34},{3,35},{4,36},{5,37},{6,38},{7,39},{8,40},{9,... | collective-permute-start | bytes 24584 | tf_op jit(solution)/shard_map/ppermute | solution.py:256
  124.9 4.9 %collective-permute-done.8 = f32[16,128]{1,0:T(8,128)S(1)} collective-permute-done((f32[16,128]{1,0:T(8,128)S(1)}, f32[16,128]{1,0:T(8,128)S(1)}, u32[]{:S(2)}, u32[]{:S(2)}) %collective-permute-start.8) | collective-permute-done | bytes 8224 | tf_op jit(solution)/shard_map/ppermute | solution.py:256
  129.8 0.3 shard_map.123.spots_ref
  130.0 1.2 shard_map.124
  131.3 6.4 %collective-permute-start.9 = (f32[128,256]{1,0:T(8,128)S(1)}, f32[128,256]{1,0:T(8,128)S(1)}, u32[]{:S(2)}, u32[]{:S(2)}) collective-permute-start(f32[128,256]{1,0:T(8,128)S(1)} %get-tuple-element.18), channel_id=1, source_target_pairs={{0,64},{64,0},{128,192},{192,128},{256,320},{320,256},{384,448},{4... | collective-permute-start | bytes 393224 | tf_op jit(solution)/shard_map/ppermute | solution.py:265
  137.7 1.0 collective-permute-done.9.sib_ref
  138.7 0.8 shard_map.125
  139.5 7.2 %all-to-all-start.1 = ((bf16[16,16,256]{2,1,0:T(8,128)(2,1)}), bf16[16,16,256]{2,1,0:T(8,128)(2,1)S(1)}, u32[]{:S(2)}, u32[]{:S(2)}) async-start(bf16[16,16,256]{2,1,0:T(8,128)(2,1)} %get-tuple-element.20), calls=%async_computation.1 | async-start | bytes 262144 | tf_op jit(solution)/shard_map/all_to_all | solution.py:279
  146.7 20.2 %all-gather = bf16[1792,256]{1,0:T(8,128)(2,1)S(1)} all-gather(bf16[112,256]{1,0:T(8,128)(2,1)S(1)} %get-tuple-element.19), channel_id=2, replica_groups=mesh['replica'=16,'mp'=64] {'replica'}, dimensions={0}, use_global_device_ids=true | all-gather | bytes 974848 | tf_op jit(solution)/shard_map/all_gather | solution.py:280
  166.9 2.5 %shard_map.126 = f32[2048,256]{1,0:T(8,128)} custom-call(bf16[16,112,256]{2,1,0:T(8,128)(2,1)S(1)} %bitcast.13, bf16[16,16,256]{2,1,0:T(8,128)(2,1)S(1)} %all-to-all-done.1.tail_ref, f32[2048,256]{1,0:T(8,128)} %table_ref.1), custom_call_target="tpu_custom_call" | custom-call | tf_op jit(solution)/shard_map/pallas_call | solution.py:282
  (35 shorter events, 0.4 us)
Async XLA Ops:
  0.6 11.1 %copy-start = (bf16[1024,1024]{1,0:T(8,128)(2,1)S(1)}, bf16[1024,1024]{1,0:T(8,128)(2,1)}, u32[]{:S(2)}) copy-start(bf16[1024,1024]{1,0:T(8,128)(2,1)} %param.14) | copy-start | bytes 6291460
  0.6 1.2 copy-start.1
  1.8 0.7 copy-start.3
  6.5 7.9 %collective-permute-start = (f32[16,128]{1,0:T(8,128)S(1)}, f32[16,128]{1,0:T(8,128)S(1)}, u32[]{:S(2)}, u32[]{:S(2)}) collective-permute-start(f32[16,128]{1,0:T(8,128)S(1)} %get-tuple-element.14), channel_id=1, source_target_pairs={{0,128},{64,192},{128,0},{192,64},{256,384},{320,448},{384,256},{4... | collective-permute-start | bytes 24584 | tf_op jit(solution)/shard_map/ppermute | solution.py:242
  11.7 1.7 %copy-start.5 = (s32[256]{0:T(256)S(1)}, s32[256]{0:T(256)}, u32[]{:S(2)}) copy-start(s32[256]{0:T(256)} %param.12) | copy-start | bytes 3076
  11.7 1.7 %copy-start.6 = (f32[1024]{0:T(1024)S(1)}, f32[1024]{0:T(1024)}, u32[]{:S(2)}) copy-start(f32[1024]{0:T(1024)} %param.16) | copy-start | bytes 12292
  14.5 5.3 %collective-permute-start.1 = (f32[16,128]{1,0:T(8,128)S(1)}, f32[16,128]{1,0:T(8,128)S(1)}, u32[]{:S(2)}, u32[]{:S(2)}) collective-permute-start(f32[16,128]{1,0:T(8,128)S(1)} %broadcast_select_fusion), channel_id=1, source_target_pairs={{0,256},{64,320},{128,384},{192,448},{256,0},{320,64},{384,128},{4... | collective-permute-start | bytes 24584 | tf_op jit(solution)/shard_map/ppermute | solution.py:242
  19.9 9.3 %collective-permute-start.2 = (f32[16,128]{1,0:T(8,128)S(1)}, f32[16,128]{1,0:T(8,128)S(1)}, u32[]{:S(2)}, u32[]{:S(2)}) collective-permute-start(f32[16,128]{1,0:T(8,128)S(1)} %broadcast_select_fusion.1), channel_id=1, source_target_pairs={{0,512},{64,576},{128,640},{192,704},{256,768},{320,832},{384,896}... | collective-permute-start | bytes 24584 | tf_op jit(solution)/shard_map/ppermute | solution.py:242
  26.4 112.3 %copy-start.2 = (f32[128,256]{1,0:T(8,128)S(1)}, f32[128,256]{1,0:T(8,128)}, u32[]{:S(2)}) copy-start(f32[128,256]{1,0:T(8,128)} %moment_ref.1) | copy-start | bytes 393220
  26.4 112.3 %copy-start.4 = (f32[128]{0:T(128)S(1)}, f32[128]{0:T(128)}, u32[]{:S(2)}) copy-start(f32[128]{0:T(128)} %param.19) | copy-start | bytes 1540
  29.3 100.8 %all-to-all-start = ((bf16[512,8,128]{2,1,0:T(8,128)(2,1)}), bf16[512,8,128]{2,1,0:T(8,128)(2,1)S(1)}, u32[]{:S(2)}, u32[]{:S(2)}) async-start(bf16[512,8,128]{2,1,0:T(8,128)(2,1)} %bitcast.2), calls=%async_computation | async-start | bytes 2097152 | tf_op jit(solution)/shard_map/all_to_all | solution.py:247
  62.9 4.7 %collective-permute-start.3 = (f32[16,128]{1,0:T(8,128)S(1)}, f32[16,128]{1,0:T(8,128)S(1)}, u32[]{:S(2)}, u32[]{:S(2)}) collective-permute-start(f32[16,128]{1,0:T(8,128)S(1)} %broadcast_select_fusion.2), channel_id=1, source_target_pairs={{0,1},{1,0},{2,3},{3,2},{4,5},{5,4},{6,7},{7,6},{8,9},{9,8},{10,11... | collective-permute-start | bytes 24584 | tf_op jit(solution)/shard_map/ppermute | solution.py:256
  67.6 6.2 %collective-permute-start.4 = (f32[16,128]{1,0:T(8,128)S(1)}, f32[16,128]{1,0:T(8,128)S(1)}, u32[]{:S(2)}, u32[]{:S(2)}) collective-permute-start(f32[16,128]{1,0:T(8,128)S(1)} %broadcast_select_fusion.3), channel_id=1, source_target_pairs={{0,2},{1,3},{2,0},{3,1},{4,6},{5,7},{6,4},{7,5},{8,10},{9,11},{10,... | collective-permute-start | bytes 24584 | tf_op jit(solution)/shard_map/ppermute | solution.py:256
  73.8 28.7 %collective-permute-start.5 = (f32[16,128]{1,0:T(8,128)S(1)}, f32[16,128]{1,0:T(8,128)S(1)}, u32[]{:S(2)}, u32[]{:S(2)}) collective-permute-start(f32[16,128]{1,0:T(8,128)S(1)} %broadcast_select_fusion.4), channel_id=1, source_target_pairs={{0,4},{1,5},{2,6},{3,7},{4,0},{5,1},{6,2},{7,3},{8,12},{9,13},{10,... | collective-permute-start | bytes 24584 | tf_op jit(solution)/shard_map/ppermute | solution.py:256
  102.5 5.6 %collective-permute-start.6 = (f32[16,128]{1,0:T(8,128)S(1)}, f32[16,128]{1,0:T(8,128)S(1)}, u32[]{:S(2)}, u32[]{:S(2)}) collective-permute-start(f32[16,128]{1,0:T(8,128)S(1)} %broadcast_select_fusion.5), channel_id=1, source_target_pairs={{0,8},{1,9},{2,10},{3,11},{4,12},{5,13},{6,14},{7,15},{8,0},{9,1},... | collective-permute-start | bytes 24584 | tf_op jit(solution)/shard_map/ppermute | solution.py:256
  108.1 8.6 %collective-permute-start.7 = (f32[16,128]{1,0:T(8,128)S(1)}, f32[16,128]{1,0:T(8,128)S(1)}, u32[]{:S(2)}, u32[]{:S(2)}) collective-permute-start(f32[16,128]{1,0:T(8,128)S(1)} %broadcast_select_fusion.6), channel_id=1, source_target_pairs={{0,16},{1,17},{2,18},{3,19},{4,20},{5,21},{6,22},{7,23},{8,24},{9,... | collective-permute-start | bytes 24584 | tf_op jit(solution)/shard_map/ppermute | solution.py:256
  116.7 13.1 %collective-permute-start.8 = (f32[16,128]{1,0:T(8,128)S(1)}, f32[16,128]{1,0:T(8,128)S(1)}, u32[]{:S(2)}, u32[]{:S(2)}) collective-permute-start(f32[16,128]{1,0:T(8,128)S(1)} %broadcast_select_fusion.7), channel_id=1, source_target_pairs={{0,32},{1,33},{2,34},{3,35},{4,36},{5,37},{6,38},{7,39},{8,40},{9,... | collective-permute-start | bytes 24584 | tf_op jit(solution)/shard_map/ppermute | solution.py:256
  131.3 7.4 %collective-permute-start.9 = (f32[128,256]{1,0:T(8,128)S(1)}, f32[128,256]{1,0:T(8,128)S(1)}, u32[]{:S(2)}, u32[]{:S(2)}) collective-permute-start(f32[128,256]{1,0:T(8,128)S(1)} %get-tuple-element.18), channel_id=1, source_target_pairs={{0,64},{64,0},{128,192},{192,128},{256,320},{320,256},{384,448},{4... | collective-permute-start | bytes 393224 | tf_op jit(solution)/shard_map/ppermute | solution.py:265
  139.5 27.4 %all-to-all-start.1 = ((bf16[16,16,256]{2,1,0:T(8,128)(2,1)}), bf16[16,16,256]{2,1,0:T(8,128)(2,1)S(1)}, u32[]{:S(2)}, u32[]{:S(2)}) async-start(bf16[16,16,256]{2,1,0:T(8,128)(2,1)} %get-tuple-element.20), calls=%async_computation.1 | async-start | bytes 262144 | tf_op jit(solution)/shard_map/all_to_all | solution.py:279

commit v7 on v4

--- a/solution.py
+++ b/solution.py
@@ -28,6 +28,10 @@
 
 def dot_t(a, b):
     return lax.dot_general(a, b, (((1,), (1,)), ((), ())), preferred_element_type=F32)
+
+
+def turned_bits(z):
+    return ((z & 1) << 3) | ((z & 2) << 1) | ((z & 4) >> 1) | ((z & 8) >> 3)
 
 
 def onehot(cond):
@@ -90,7 +94,8 @@
         pair = jnp.sum(cells[fl] * (64.0 * seen[:16] + seen[16:]), axis=0, keepdims=True)
         rank = (pair < 2.0 * (lane + float(fl * batch))).astype(I32)
         lead = cs[fl] * 2 + rank
-        slot_ref[fl : fl + 1, :] = (ys[fl] * 64 + ms[fl]) * 4 + lead
+        peer = (ms[fl] & 3) * 128 + ys[fl] * 16 + turned_bits(ms[fl] >> 2)
+        slot_ref[fl : fl + 1, :] = peer * 4 + lead
         spread = jnp.where(iota((32, batch), 0) == lead * 8 + ys[fl], locs[fl], 0.0)
         local += dot_t(owners[fl], spread.astype(BF))
     local_ref[...] = local
@@ -121,13 +126,15 @@
     y_here, core = place_ref[0], place_ref[1]
     n = iota((32, 512), 1)
     pick = onehot(iota((32, 512), 0) == (n & 3) * 8 + y_here)
-    near = iota((64, 512), 0) == iota((64, 512), 1) >> 3
+    rows = iota((512, 512), 0)
     n = iota((1, 512), 1)
     shift = ((n >> 2) & 1) * 256 + (((n >> 1) & 1) ^ core) * 128
-    for y in range(8):
-        found = dot(local_ref[y].astype(BF), pick)
-        spot = jnp.sum(jnp.where(near, found, 0.0), axis=0, keepdims=True).astype(I32)
-        spots_ref[y : y + 1, :] = spot + shift
+    found = dot(local_ref[...].reshape(512, 32).astype(BF), pick)
+    for part in range(8):
+        y = (part & 1) * 4 + (n >> 7)
+        source = y * 64 + turned_bits((n >> 3) & 15) * 4 + (part >> 1)
+        spot = jnp.sum(jnp.where(rows == source, found, 0.0), axis=0, keepdims=True).astype(I32)
+        spots_ref[part : part + 1, :] = spot + shift
 
 
 def total_body(spots_ref, got_ref, own_ref, sib_ref):
@@ -220,7 +227,10 @@
     shape = jax.ShapeDtypeStruct
     rep, mp = "replica", "mp"
     same_core = [[2 * y + c for y in range(8)] for c in range(2)]
-    planes = [[r * 64 + m for r in group for m in range(64)] for group in same_core]
+    planes = [
+        [r * 64 + turned_bits(z) * 4 + x for x in range(4) for r in group for z in range(16)]
+        for group in same_core
+    ]
     other_core = [(i, i ^ 1) for i in range(16)]
     core = lax.axis_index(rep) & 1
     place = jnp.stack([lax.axis_index(rep) >> 1, core]).astype(I32)

time: 152 us -> 152 us (level)
  transfers between devices with their start and end apart: 4 -> 4, of which waited for: 3 -> 3; matrix products, arithmetic and copies ran while one was open for 3% -> 3% of each run, Pallas kernels for 2% -> 3%
where the time goes in v7:
time: 152 us
  starting transfers between devices  56.3 us (37%)
  blocking collectives  41.5 us (27%)
  waiting for transfers between devices  33.4 us (22%)
  Pallas kernels  13.8 us (9%)
  local copies, waits for them, and re-layouts  3.04 us (2%)
  matrix products  2.6 us (2%)
    all_to_all x1, waiting for transfers between devices, on_device(): lax.all_to_all(send.reshape(512, 8, 128), (rep, mp), split_axis=0, concat...  25.6 us
    all_to_all x1, starting transfers between devices, on_device(): lax.all_to_all(local.reshape(64, 1, 32), mp, split_axis=0, concat_axis=0,...  22.8 us
    all_to_all x1, starting transfers between devices, on_device(): lax.all_to_all(send.reshape(512, 8, 128), (rep, mp), split_axis=0, concat...  21.4 us
    all_gather x1, blocking collectives, on_device(): lax.all_gather(local.reshape(64, 32), rep, axis=0, tiled=False, axis_inde...  21.3 us
    all_gather x1, blocking collectives, on_device(): heads = lax.all_gather(head, rep, axis=0, tiled=False)  20.2 us
    pallas_call x5, Pallas kernels, call(): pl.pallas_call(body, out_shape=outs, in_specs=specs, out_specs=[pl.BlockS...  11.3 us
    all_to_all x1, waiting for transfers between devices, on_device(): lax.all_to_all(local.reshape(64, 1, 32), mp, split_axis=0, concat_axis=0,...  6.81 us
    ppermute x1, starting transfers between devices, on_device(): sib = lax.ppermute(sib, rep, other_core)  6.69 us
  transfers between devices with their start and end apart: 4, of which 3 were waited for; matrix products, arithmetic and copies ran while one was open for 3% of the time, Pallas kernels for 3%

profile of v7, /device:TPU:1, one launch (start us, length us, event | category | flops | bytes accessed | tf_op | source)
XLA Modules:
  0.0 151.6 jit_solution(1968822880853166405)
XLA Ops:
  0.6 0.0 copy-start
  0.6 0.0 copy-start.1
  0.7 1.2 copy-done.1
  1.8 0.0 copy-start.3
  1.8 0.7 copy-done.3
  2.5 4.5 %shard_map.121 = (s32[8,256]{1,0:T(8,128)S(1)}, f32[64,32]{1,0:T(8,128)}) custom-call(s32[4,2,256]{2,1,0:T(2,128)S(1)} %bitcast.22, s32[1024,128]{1,0:T(8,128)S(1)} %bitcast.21), custom_call_target="tpu_custom_call" | custom-call | tf_op jit(solution)/shard_map/pallas_call | solution.py:44
  7.0 22.8 %all-to-all-start = ((f32[64,1,32]{2,1,0:T(1,128)}), f32[64,1,32]{2,1,0:T(1,128)S(1)}, u32[]{:S(2)}, u32[]{:S(2)}) async-start(f32[64,1,32]{2,1,0:T(1,128)} %bitcast.5), calls=%async_computation | async-start | bytes 65536 | tf_op jit(solution)/shard_map/all_to_all | solution.py:249
  29.8 1.1 copy.15
  31.0 0.0 copy-done
  31.0 0.0 copy-start.5
  31.0 0.0 copy-start.6
  31.0 1.7 %multiply_reduce_fusion = (f32[256]{0:T(256)S(1)}, f32[256,1024]{1,0:T(8,128)S(1)}) fusion(f32[1024]{0:T(1024)} %param.16, f32[1024]{0:T(1024)} %param.15, bf16[256,1024]{1,0:T(8,128)(2,1)S(1)} %bitcast.25, bf16[1024,1024]{1,0:T(8,128)(2,1)S(1)} %copy-done), kind=kOutput, calls=%fused_computation.3 | convolution fusion | flops 538705664 | bytes 3679232 | tf_op jit(solution)/shard_map/dot_general | solution.py:197
  32.7 0.0 copy-done.5
  32.7 0.0 copy-done.6
  32.7 0.9 convolution_convert_fusion.grads_ref
  33.7 2.7 %shard_map.122 = bf16[4096,128]{1,0:T(8,128)(2,1)} custom-call(s32[8,256]{1,0:T(8,128)S(1)} %get-tuple-element.13.slot_ref, bf16[256,1024]{1,0:T(8,128)(2,1)S(1)} %convolution_convert_fusion.grads_ref), custom_call_target="tpu_custom_call" | custom-call | tf_op jit(solution)/shard_map/pallas_call | solution.py:44
  36.4 6.8 %all-to-all-done = f32[64,1,32]{2,1,0:T(1,128)S(1)} async-done(((f32[64,1,32]{2,1,0:T(1,128)}), f32[64,1,32]{2,1,0:T(1,128)S(1)}, u32[]{:S(2)}, u32[]{:S(2)}) %all-to-all-start) | async-done | bytes 8224 | tf_op jit(solution)/shard_map/all_to_all | solution.py:249
  43.2 21.4 %all-to-all-start.1 = ((bf16[512,8,128]{2,1,0:T(8,128)(2,1)}), bf16[512,8,128]{2,1,0:T(8,128)(2,1)S(1)}, u32[]{:S(2)}, u32[]{:S(2)}) async-start(bf16[512,8,128]{2,1,0:T(8,128)(2,1)} %bitcast.7), calls=%async_computation.1 | async-start | bytes 2097152 | tf_op jit(solution)/shard_map/all_to_all | solution.py:255
  64.7 0.1 pad_add_fusion.place_ref
  64.7 21.3 %all-gather = f32[512,1,32]{2,1,0:T(1,128)S(1)} all-gather(f32[64,1,32]{2,1,0:T(1,128)S(1)} %all-to-all-done), channel_id=2, replica_groups={{0,128,256,384,512,640,768,896},{64,192,320,448,576,704,832,960},{1,129..., dimensions={0}, use_global_device_ids=true | all-gather | bytes 73728 | tf_op jit(solution)/shard_map/all_gather | solution.py:263
  86.0 2.0 %shard_map.123.spots_ref = s32[8,512]{1,0:T(8,128)S(1)} custom-call(s32[2]{0:T(128)S(1)} %pad_add_fusion.place_ref, f32[8,64,32]{2,1,0:T(8,128)S(1)} %bitcast.20), custom_call_target="tpu_custom_call" | custom-call | tf_op jit(solution)/shard_map/pallas_call | solution.py:44
  88.1 25.6 %all-to-all-done.1 = bf16[512,8,128]{2,1,0:T(8,128)(2,1)S(1)} async-done(((bf16[512,8,128]{2,1,0:T(8,128)(2,1)}), bf16[512,8,128]{2,1,0:T(8,128)(2,1)S(1)}, u32[]{:S(2)}, u32[]{:S(2)}) %all-to-all-start.1) | async-done | bytes 1048608 | tf_op jit(solution)/shard_map/all_to_all | solution.py:255
  113.7 1.2 shard_map.124
  114.9 6.7 %collective-permute-start = (f32[128,256]{1,0:T(8,128)S(1)}, f32[128,256]{1,0:T(8,128)S(1)}, u32[]{:S(2)}, u32[]{:S(2)}) collective-permute-start(f32[128,256]{1,0:T(8,128)S(1)} %get-tuple-element.18), channel_id=1, source_target_pairs={{0,64},{64,0},{128,192},{192,128},{256,320},{320,256},{384,448},{4... | collective-permute-start | bytes 393224 | tf_op jit(solution)/shard_map/ppermute | solution.py:273
  121.6 1.0 collective-permute-done.sib_ref
  122.6 0.0 copy-done.2
  122.6 0.0 copy-done.4
  122.6 0.8 shard_map.125
  123.4 5.4 %all-to-all-start.2 = ((bf16[16,16,256]{2,1,0:T(8,128)(2,1)}), bf16[16,16,256]{2,1,0:T(8,128)(2,1)S(1)}, u32[]{:S(2)}, u32[]{:S(2)}) async-start(bf16[16,16,256]{2,1,0:T(8,128)(2,1)} %get-tuple-element.20), calls=%async_computation.2 | async-start | bytes 262144 | tf_op jit(solution)/shard_map/all_to_all | solution.py:287
  128.8 20.2 %all-gather.1 = bf16[1792,256]{1,0:T(8,128)(2,1)S(1)} all-gather(bf16[112,256]{1,0:T(8,128)(2,1)S(1)} %get-tuple-element.19), channel_id=3, replica_groups=mesh['replica'=16,'mp'=64] {'replica'}, dimensions={0}, use_global_device_ids=true | all-gather | bytes 974848 | tf_op jit(solution)/shard_map/all_gather | solution.py:288
  149.0 0.0 all-to-all-done.2.tail_ref
  149.0 2.5 %shard_map.126 = f32[2048,256]{1,0:T(8,128)} custom-call(bf16[16,112,256]{2,1,0:T(8,128)(2,1)S(1)} %bitcast.19, bf16[16,16,256]{2,1,0:T(8,128)(2,1)S(1)} %all-to-all-done.2.tail_ref, f32[2048,256]{1,0:T(8,128)} %table_ref.1), custom_call_target="tpu_custom_call" | custom-call | tf_op jit(solution)/shard_map/pallas_call | solution.py:290
  (3 shorter events, 0.0 us)
Async XLA Ops:
  0.6 30.3 %copy-start = (bf16[1024,1024]{1,0:T(8,128)(2,1)S(1)}, bf16[1024,1024]{1,0:T(8,128)(2,1)}, u32[]{:S(2)}) copy-start(bf16[1024,1024]{1,0:T(8,128)(2,1)} %param.14) | copy-start | bytes 6291460
  0.6 1.2 copy-start.1
  1.8 0.7 copy-start.3
  7.0 36.2 %all-to-all-start = ((f32[64,1,32]{2,1,0:T(1,128)}), f32[64,1,32]{2,1,0:T(1,128)S(1)}, u32[]{:S(2)}, u32[]{:S(2)}) async-start(f32[64,1,32]{2,1,0:T(1,128)} %bitcast.5), calls=%async_computation | async-start | bytes 65536 | tf_op jit(solution)/shard_map/all_to_all | solution.py:249
  31.0 1.7 %copy-start.5 = (s32[256]{0:T(256)S(1)}, s32[256]{0:T(256)}, u32[]{:S(2)}) copy-start(s32[256]{0:T(256)} %param.12) | copy-start | bytes 3076
  31.0 1.7 %copy-start.6 = (f32[1024]{0:T(1024)S(1)}, f32[1024]{0:T(1024)}, u32[]{:S(2)}) copy-start(f32[1024]{0:T(1024)} %param.16) | copy-start | bytes 12292
  36.4 86.2 %copy-start.2 = (f32[128,256]{1,0:T(8,128)S(1)}, f32[128,256]{1,0:T(8,128)}, u32[]{:S(2)}) copy-start(f32[128,256]{1,0:T(8,128)} %moment_ref.1) | copy-start | bytes 393220
  36.4 86.2 %copy-start.4 = (f32[128]{0:T(128)S(1)}, f32[128]{0:T(128)}, u32[]{:S(2)}) copy-start(f32[128]{0:T(128)} %param.19) | copy-start | bytes 1540
  43.2 70.5 %all-to-all-start.1 = ((bf16[512,8,128]{2,1,0:T(8,128)(2,1)}), bf16[512,8,128]{2,1,0:T(8,128)(2,1)S(1)}, u32[]{:S(2)}, u32[]{:S(2)}) async-start(bf16[512,8,128]{2,1,0:T(8,128)(2,1)} %bitcast.7), calls=%async_computation.1 | async-start | bytes 2097152 | tf_op jit(solution)/shard_map/all_to_all | solution.py:255
  114.9 7.7 %collective-permute-start = (f32[128,256]{1,0:T(8,128)S(1)}, f32[128,256]{1,0:T(8,128)S(1)}, u32[]{:S(2)}, u32[]{:S(2)}) collective-permute-start(f32[128,256]{1,0:T(8,128)S(1)} %get-tuple-element.18), channel_id=1, source_target_pairs={{0,64},{64,0},{128,192},{192,128},{256,320},{320,256},{384,448},{4... | collective-permute-start | bytes 393224 | tf_op jit(solution)/shard_map/ppermute | solution.py:273
  123.4 25.6 %all-to-all-start.2 = ((bf16[16,16,256]{2,1,0:T(8,128)(2,1)}), bf16[16,16,256]{2,1,0:T(8,128)(2,1)S(1)}, u32[]{:S(2)}, u32[]{:S(2)}) async-start(bf16[16,16,256]{2,1,0:T(8,128)(2,1)} %get-tuple-element.20), calls=%async_computation.2 | async-start | bytes 262144 | tf_op jit(solution)/shard_map/all_to_all | solution.py:287

commit v8 on v7

--- a/solution.py
+++ b/solution.py
@@ -61,6 +61,7 @@
     count = feats * bag
     sums = jnp.zeros((64, 32), F32)
     locs, ys, cs, ms = [], [], [], []
+    x_here = lax.axis_index("mp") & 3
     lane = iota((1, batch), 1).astype(F32)
     for fl in range(count):
         ids = ids_ref[fl // bag, fl % bag : fl % bag + 1, :]
@@ -75,7 +76,7 @@
         low, high = pick(0).astype(I32), pick(1).astype(I32) + 256
         loc = (low & 127).astype(F32)
         own, y, c = high >> 3, high & 7, low >> 7
-        owner = onehot(iota((64, batch), 0) == own)
+        owner = onehot(iota((64, batch), 0) == ((own & 3) ^ x_here) * 16 + (own >> 2))
         cell = jnp.where(iota((16, batch), 0) == c * 8 + y, 1.0, 0.0)
         owners[fl] = owner
         cells[fl] = cell
@@ -98,7 +99,8 @@
         slot_ref[fl : fl + 1, :] = peer * 4 + lead
         spread = jnp.where(iota((32, batch), 0) == lead * 8 + ys[fl], locs[fl], 0.0)
         local += dot_t(owners[fl], spread.astype(BF))
-    local_ref[...] = local
+    parts = [local[16 * x : 16 * (x + 1)] for x in range(4)]
+    local_ref[...] = jnp.concatenate(parts, axis=1)
 
 
 def pack_body(slot_ref, grads_ref, send_ref):
@@ -122,19 +124,21 @@
         send_ref[chunk * 2 * step : (chunk + 1) * 2 * step, :] = both.reshape(2 * step, 128).astype(BF)
 
 
-def spots_body(place_ref, local_ref, spots_ref):
-    y_here, core = place_ref[0], place_ref[1]
-    n = iota((32, 512), 1)
-    pick = onehot(iota((32, 512), 0) == (n & 3) * 8 + y_here)
-    rows = iota((512, 512), 0)
+def spots_body(local_ref, spots_ref):
+    here, x_here = lax.axis_index("replica"), lax.axis_index("mp") & 3
+    y_here, core = here >> 1, here & 1
+    local = local_ref[...].reshape(128, 128).astype(BF)
+    lanes, rows = iota((128, 512), 0), iota((128, 512), 0)
     n = iota((1, 512), 1)
     shift = ((n >> 2) & 1) * 256 + (((n >> 1) & 1) ^ core) * 128
-    found = dot(local_ref[...].reshape(512, 32).astype(BF), pick)
-    for part in range(8):
-        y = (part & 1) * 4 + (n >> 7)
-        source = y * 64 + turned_bits((n >> 3) & 15) * 4 + (part >> 1)
-        spot = jnp.sum(jnp.where(rows == source, found, 0.0), axis=0, keepdims=True).astype(I32)
-        spots_ref[part : part + 1, :] = spot + shift
+    for x in range(4):
+        pick = onehot(lanes == (x ^ x_here) * 32 + (n & 3) * 8 + y_here)
+        found = dot(local, pick)
+        for part in (2 * x, 2 * x + 1):
+            y = (part & 1) * 4 + (n >> 7)
+            near = rows == y * 16 + turned_bits((n >> 3) & 15)
+            spot = jnp.sum(jnp.where(near, found, 0.0), axis=0, keepdims=True).astype(I32)
+            spots_ref[part : part + 1, :] = spot + shift
 
 
 def total_body(spots_ref, got_ref, own_ref, sib_ref):
@@ -232,12 +236,9 @@
         for group in same_core
     ]
     other_core = [(i, i ^ 1) for i in range(16)]
-    core = lax.axis_index(rep) & 1
-    place = jnp.stack([lax.axis_index(rep) >> 1, core]).astype(I32)
-
     slots, local = call(
         route_body,
-        [shape((8, 256), I32), shape((64, 32), F32)],
+        [shape((8, 256), I32), shape((16, 128), F32)],
         row_ids.transpose(1, 2, 0),
         row_slot.reshape(1024, 128),
         scratch=[
@@ -247,7 +248,12 @@
         ],
     )
     local = lax.all_to_all(
-        local.reshape(64, 1, 32), mp, split_axis=0, concat_axis=0, tiled=True
+        local.reshape(16, 1, 128),
+        mp,
+        split_axis=0,
+        concat_axis=0,
+        tiled=True,
+        axis_index_groups=[[4 * z + x for z in range(16)] for x in range(4)],
     )
     grads = pooled_grads(pooled, labels, w_hidden, b_hidden, w_out)
     (send,) = call(pack_body, [shape((4096, 128), BF)], slots, grads)
@@ -260,10 +266,13 @@
         tiled=True,
         axis_index_groups=planes,
     )
-    local = lax.all_gather(
-        local.reshape(64, 32), rep, axis=0, tiled=False, axis_index_groups=same_core
-    )
-    (spots,) = call(spots_body, [shape((8, 512), I32)], place, local, smem=1)
+    local = local.reshape(16, 128)
+    lanes = iota((16, 128), 1)
+    for bit in (1, 2):
+        other = lax.ppermute(local, mp, [(i, i ^ bit) for i in range(64)])
+        local = jnp.where((lanes & (32 * bit)) != 0, other, local)
+    local = lax.all_gather(local, rep, axis=0, tiled=False, axis_index_groups=same_core)
+    (spots,) = call(spots_body, [shape((8, 512), I32)], local)
     own, sib = call(
         total_body,
         [shape((128, 256), F32), shape((128, 256), F32)],

time: 152 us -> 149 us (0.980)
  waiting for transfers between devices: 33.4 us -> 28.7 us
  starting transfers between devices: 56.3 us -> 60.5 us
    all_to_all x1, waiting for transfers between devices: 25.6 us -> 17.4 us  [on_device(): lax.all_to_all(send.reshape(512, 8, 128), (rep, mp), split_axis=0, concat...]
    ppermute x0 -> x2, waiting for transfers between devices: none -> 5.64 us  [on_device(): other = lax.ppermute(local, mp, [(i, i ^ bit) for i in range(64)])]
    ppermute x0 -> x2, starting transfers between devices: none -> 5.22 us  [on_device(): other = lax.ppermute(local, mp, [(i, i ^ bit) for i in range(64)])]
    all_to_all x1, starting transfers between devices: 22.8 us -> 19.4 us  [on_device(): lax.all_to_all(local.reshape(16, 1, 128), mp, split_axis=0, concat_axis=0...]
    all_to_all x1, starting transfers between devices: 21.4 us -> 23.8 us  [on_device(): lax.all_to_all(send.reshape(512, 8, 128), (rep, mp), split_axis=0, concat...]
    all_to_all x1, waiting for transfers between devices: 6.81 us -> 4.64 us  [on_device(): lax.all_to_all(local.reshape(16, 1, 128), mp, split_axis=0, concat_axis=0...]
  transfers between devices with their start and end apart: 4 -> 6, of which waited for: 3 -> 5; matrix products, arithmetic and copies ran while one was open for 3% -> 3% of each run, Pallas kernels for 3% -> 2%
where the time goes in v8:
time: 149 us
  starting transfers between devices  60.5 us (41%)
  blocking collectives  40.5 us (27%)
  waiting for transfers between devices  28.7 us (19%)
  Pallas kernels  12.3 us (8%)
  local copies, waits for them, and re-layouts  3.05 us (2%)
  matrix products  2.6 us (2%)
    all_to_all x1, starting transfers between devices, on_device(): lax.all_to_all(send.reshape(512, 8, 128), (rep, mp), split_axis=0, concat...  23.8 us
    all_gather x1, blocking collectives, on_device(): lax.all_gather(local, rep, axis=0, tiled=False, axis_index_groups=same_core)  20.3 us
    all_gather x1, blocking collectives, on_device(): heads = lax.all_gather(head, rep, axis=0, tiled=False)  20.2 us
    all_to_all x1, starting transfers between devices, on_device(): lax.all_to_all(local.reshape(16, 1, 128), mp, split_axis=0, concat_axis=0...  19.4 us
    all_to_all x1, waiting for transfers between devices, on_device(): lax.all_to_all(send.reshape(512, 8, 128), (rep, mp), split_axis=0, concat...  17.4 us
    pallas_call x5, Pallas kernels, call(): pl.pallas_call(body, out_shape=outs, in_specs=specs, out_specs=[pl.BlockS...  9.81 us
    ppermute x1, starting transfers between devices, on_device(): sib = lax.ppermute(sib, rep, other_core)  6.69 us
    ppermute x2, waiting for transfers between devices, on_device(): other = lax.ppermute(local, mp, [(i, i ^ bit) for i in range(64)])  5.64 us
  transfers between devices with their start and end apart: 6, of which 5 were waited for; matrix products, arithmetic and copies ran while one was open for 3% of the time, Pallas kernels for 2%

profile of v8, /device:TPU:1, one launch (start us, length us, event | category | flops | bytes accessed | tf_op | source)
XLA Modules:
  0.0 148.5 jit_solution(17572143427332999689)
XLA Ops:
  0.6 0.0 copy-start
  0.6 0.0 copy-start.1
  0.7 1.2 copy-done.1
  1.8 0.7 copy-done.3
  2.5 4.6 %shard_map.121 = (s32[8,256]{1,0:T(8,128)S(1)}, f32[16,128]{1,0:T(8,128)}) custom-call(s32[4,2,256]{2,1,0:T(2,128)S(1)} %bitcast.21, s32[1024,128]{1,0:T(8,128)S(1)} %bitcast.19), custom_call_target="tpu_custom_call" | custom-call | tf_op jit(solution)/shard_map/pallas_call | solution.py:44
  7.1 19.4 %all-to-all-start = ((f32[16,1,128]{2,1,0:T(1,128)}), f32[16,1,128]{2,1,0:T(1,128)S(1)}, u32[]{:S(2)}, u32[]{:S(2)}) async-start(f32[16,1,128]{2,1,0:T(1,128)} %bitcast.3), calls=%async_computation | async-start | bytes 16384 | tf_op jit(solution)/shard_map/all_to_all | solution.py:250
  26.5 1.1 copy.14
  27.7 0.0 copy-start.5
  27.7 0.0 copy-start.6
  27.7 1.7 %multiply_reduce_fusion = (f32[256]{0:T(256)S(1)}, f32[256,1024]{1,0:T(8,128)S(1)}) fusion(f32[1024]{0:T(1024)} %param.16, f32[1024]{0:T(1024)} %param.15, bf16[256,1024]{1,0:T(8,128)(2,1)S(1)} %bitcast.24, bf16[1024,1024]{1,0:T(8,128)(2,1)S(1)} %copy-done), kind=kOutput, calls=%fused_computation.3 | convolution fusion | flops 538705664 | bytes 3679232 | tf_op jit(solution)/shard_map/dot_general | solution.py:201
  29.4 0.9 convolution_convert_fusion.grads_ref
  30.4 0.0 copy-start.2
  30.4 0.0 copy-start.4
  30.4 2.7 %shard_map.122 = bf16[4096,128]{1,0:T(8,128)(2,1)} custom-call(s32[8,256]{1,0:T(8,128)S(1)} %get-tuple-element.13.slot_ref, bf16[256,1024]{1,0:T(8,128)(2,1)S(1)} %convolution_convert_fusion.grads_ref), custom_call_target="tpu_custom_call" | custom-call | tf_op jit(solution)/shard_map/pallas_call | solution.py:44
  33.1 4.6 %all-to-all-done = f32[16,1,128]{2,1,0:T(1,128)S(1)} async-done(((f32[16,1,128]{2,1,0:T(1,128)}), f32[16,1,128]{2,1,0:T(1,128)S(1)}, u32[]{:S(2)}, u32[]{:S(2)}) %all-to-all-start) | async-done | bytes 8224 | tf_op jit(solution)/shard_map/all_to_all | solution.py:250
  37.8 23.8 %all-to-all-start.1 = ((bf16[512,8,128]{2,1,0:T(8,128)(2,1)}), bf16[512,8,128]{2,1,0:T(8,128)(2,1)S(1)}, u32[]{:S(2)}, u32[]{:S(2)}) async-start(bf16[512,8,128]{2,1,0:T(8,128)(2,1)} %bitcast.6), calls=%async_computation.1 | async-start | bytes 2097152 | tf_op jit(solution)/shard_map/all_to_all | solution.py:261
  61.5 1.9 %collective-permute-start = (f32[16,128]{1,0:T(8,128)S(1)}, f32[16,128]{1,0:T(8,128)S(1)}, u32[]{:S(2)}, u32[]{:S(2)}) collective-permute-start(f32[16,128]{1,0:T(8,128)S(1)} %bitcast.25), channel_id=1, source_target_pairs={{0,1},{1,0},{2,3},{3,2},{4,5},{5,4},{6,7},{7,6},{8,9},{9,8},{10,11... | collective-permute-start | bytes 24584 | tf_op jit(solution)/shard_map/ppermute | solution.py:272
  63.5 2.8 %collective-permute-done = f32[16,128]{1,0:T(8,128)S(1)} collective-permute-done((f32[16,128]{1,0:T(8,128)S(1)}, f32[16,128]{1,0:T(8,128)S(1)}, u32[]{:S(2)}, u32[]{:S(2)}) %collective-permute-start) | collective-permute-done | bytes 8224 | tf_op jit(solution)/shard_map/ppermute | solution.py:272
  66.3 3.3 %collective-permute-start.1 = (f32[16,128]{1,0:T(8,128)S(1)}, f32[16,128]{1,0:T(8,128)S(1)}, u32[]{:S(2)}, u32[]{:S(2)}) collective-permute-start(f32[16,128]{1,0:T(8,128)S(1)} %broadcast_select_fusion), channel_id=1, source_target_pairs={{0,2},{1,3},{2,0},{3,1},{4,6},{5,7},{6,4},{7,5},{8,10},{9,11},{10,... | collective-permute-start | bytes 24584 | tf_op jit(solution)/shard_map/ppermute | solution.py:272
  69.6 2.9 %collective-permute-done.1 = f32[16,128]{1,0:T(8,128)S(1)} collective-permute-done((f32[16,128]{1,0:T(8,128)S(1)}, f32[16,128]{1,0:T(8,128)S(1)}, u32[]{:S(2)}, u32[]{:S(2)}) %collective-permute-start.1) | collective-permute-done | bytes 8224 | tf_op jit(solution)/shard_map/ppermute | solution.py:272
  72.5 20.3 %all-gather = f32[128,128]{1,0:T(8,128)S(1)} all-gather(f32[16,128]{1,0:T(8,128)S(1)} %broadcast_select_fusion.1), channel_id=2, replica_groups={{0,128,256,384,512,640,768,896},{64,192,320,448,576,704,832,960},{1,129..., dimensions={0}, use_global_device_ids=true | all-gather | bytes 73728 | tf_op jit(solution)/shard_map/all_gather | solution.py:274
  92.7 0.4 shard_map.123.spots_ref
  93.2 17.4 %all-to-all-done.1 = bf16[512,8,128]{2,1,0:T(8,128)(2,1)S(1)} async-done(((bf16[512,8,128]{2,1,0:T(8,128)(2,1)}), bf16[512,8,128]{2,1,0:T(8,128)(2,1)S(1)}, u32[]{:S(2)}, u32[]{:S(2)}) %all-to-all-start.1) | async-done | bytes 1048608 | tf_op jit(solution)/shard_map/all_to_all | solution.py:261
  110.6 1.2 shard_map.124
  111.8 6.7 %collective-permute-start.2 = (f32[128,256]{1,0:T(8,128)S(1)}, f32[128,256]{1,0:T(8,128)S(1)}, u32[]{:S(2)}, u32[]{:S(2)}) collective-permute-start(f32[128,256]{1,0:T(8,128)S(1)} %get-tuple-element.18), channel_id=1, source_target_pairs={{0,64},{64,0},{128,192},{192,128},{256,320},{320,256},{384,448},{4... | collective-permute-start | bytes 393224 | tf_op jit(solution)/shard_map/ppermute | solution.py:282
  118.5 1.0 collective-permute-done.2.sib_ref
  119.5 0.0 copy-done.2
  119.5 0.8 shard_map.125
  120.3 5.4 %all-to-all-start.2 = ((bf16[16,16,256]{2,1,0:T(8,128)(2,1)}), bf16[16,16,256]{2,1,0:T(8,128)(2,1)S(1)}, u32[]{:S(2)}, u32[]{:S(2)}) async-start(bf16[16,16,256]{2,1,0:T(8,128)(2,1)} %get-tuple-element.20), calls=%async_computation.2 | async-start | bytes 262144 | tf_op jit(solution)/shard_map/all_to_all | solution.py:296
  125.7 20.2 %all-gather.1 = bf16[1792,256]{1,0:T(8,128)(2,1)S(1)} all-gather(bf16[112,256]{1,0:T(8,128)(2,1)S(1)} %get-tuple-element.19), channel_id=3, replica_groups=mesh['replica'=16,'mp'=64] {'replica'}, dimensions={0}, use_global_device_ids=true | all-gather | bytes 974848 | tf_op jit(solution)/shard_map/all_gather | solution.py:297
  145.9 0.0 all-to-all-done.2.tail_ref
  145.9 2.5 %shard_map.126 = f32[2048,256]{1,0:T(8,128)} custom-call(bf16[16,112,256]{2,1,0:T(8,128)(2,1)S(1)} %bitcast.18, bf16[16,16,256]{2,1,0:T(8,128)(2,1)S(1)} %all-to-all-done.2.tail_ref, f32[2048,256]{1,0:T(8,128)} %table_ref.1), custom_call_target="tpu_custom_call" | custom-call | tf_op jit(solution)/shard_map/pallas_call | solution.py:299
  (10 shorter events, 0.0 us)
Async XLA Ops:
  0.6 27.0 %copy-start = (bf16[1024,1024]{1,0:T(8,128)(2,1)S(1)}, bf16[1024,1024]{1,0:T(8,128)(2,1)}, u32[]{:S(2)}) copy-start(bf16[1024,1024]{1,0:T(8,128)(2,1)} %param.14) | copy-start | bytes 6291460
  0.6 1.2 copy-start.1
  1.8 0.7 copy-start.3
  7.1 30.6 %all-to-all-start = ((f32[16,1,128]{2,1,0:T(1,128)}), f32[16,1,128]{2,1,0:T(1,128)S(1)}, u32[]{:S(2)}, u32[]{:S(2)}) async-start(f32[16,1,128]{2,1,0:T(1,128)} %bitcast.3), calls=%async_computation | async-start | bytes 16384 | tf_op jit(solution)/shard_map/all_to_all | solution.py:250
  27.7 1.7 %copy-start.5 = (s32[256]{0:T(256)S(1)}, s32[256]{0:T(256)}, u32[]{:S(2)}) copy-start(s32[256]{0:T(256)} %param.12) | copy-start | bytes 3076
  27.7 1.7 %copy-start.6 = (f32[1024]{0:T(1024)S(1)}, f32[1024]{0:T(1024)}, u32[]{:S(2)}) copy-start(f32[1024]{0:T(1024)} %param.16) | copy-start | bytes 12292
  30.4 89.1 %copy-start.2 = (f32[128,256]{1,0:T(8,128)S(1)}, f32[128,256]{1,0:T(8,128)}, u32[]{:S(2)}) copy-start(f32[128,256]{1,0:T(8,128)} %moment_ref.1) | copy-start | bytes 393220
  30.4 89.1 %copy-start.4 = (f32[128]{0:T(128)S(1)}, f32[128]{0:T(128)}, u32[]{:S(2)}) copy-start(f32[128]{0:T(128)} %param.19) | copy-start | bytes 1540
  37.8 72.8 %all-to-all-start.1 = ((bf16[512,8,128]{2,1,0:T(8,128)(2,1)}), bf16[512,8,128]{2,1,0:T(8,128)(2,1)S(1)}, u32[]{:S(2)}, u32[]{:S(2)}) async-start(bf16[512,8,128]{2,1,0:T(8,128)(2,1)} %bitcast.6), calls=%async_computation.1 | async-start | bytes 2097152 | tf_op jit(solution)/shard_map/all_to_all | solution.py:261
  61.5 4.7 %collective-permute-start = (f32[16,128]{1,0:T(8,128)S(1)}, f32[16,128]{1,0:T(8,128)S(1)}, u32[]{:S(2)}, u32[]{:S(2)}) collective-permute-start(f32[16,128]{1,0:T(8,128)S(1)} %bitcast.25), channel_id=1, source_target_pairs={{0,1},{1,0},{2,3},{3,2},{4,5},{5,4},{6,7},{7,6},{8,9},{9,8},{10,11... | collective-permute-start | bytes 24584 | tf_op jit(solution)/shard_map/ppermute | solution.py:272
  66.3 6.2 %collective-permute-start.1 = (f32[16,128]{1,0:T(8,128)S(1)}, f32[16,128]{1,0:T(8,128)S(1)}, u32[]{:S(2)}, u32[]{:S(2)}) collective-permute-start(f32[16,128]{1,0:T(8,128)S(1)} %broadcast_select_fusion), channel_id=1, source_target_pairs={{0,2},{1,3},{2,0},{3,1},{4,6},{5,7},{6,4},{7,5},{8,10},{9,11},{10,... | collective-permute-start | bytes 24584 | tf_op jit(solution)/shard_map/ppermute | solution.py:272
  111.8 7.7 %collective-permute-start.2 = (f32[128,256]{1,0:T(8,128)S(1)}, f32[128,256]{1,0:T(8,128)S(1)}, u32[]{:S(2)}, u32[]{:S(2)}) collective-permute-start(f32[128,256]{1,0:T(8,128)S(1)} %get-tuple-element.18), channel_id=1, source_target_pairs={{0,64},{64,0},{128,192},{192,128},{256,320},{320,256},{384,448},{4... | collective-permute-start | bytes 393224 | tf_op jit(solution)/shard_map/ppermute | solution.py:282
  120.3 25.6 %all-to-all-start.2 = ((bf16[16,16,256]{2,1,0:T(8,128)(2,1)}), bf16[16,16,256]{2,1,0:T(8,128)(2,1)S(1)}, u32[]{:S(2)}, u32[]{:S(2)}) async-start(bf16[16,16,256]{2,1,0:T(8,128)(2,1)} %get-tuple-element.20), calls=%async_computation.2 | async-start | bytes 262144 | tf_op jit(solution)/shard_map/all_to_all | solution.py:296

commit v9 on v8

--- a/solution.py
+++ b/solution.py
@@ -124,13 +124,14 @@
         send_ref[chunk * 2 * step : (chunk + 1) * 2 * step, :] = both.reshape(2 * step, 128).astype(BF)
 
 
-def spots_body(local_ref, spots_ref):
+def spots_body(local_ref, own_ref, sib_ref):
     here, x_here = lax.axis_index("replica"), lax.axis_index("mp") & 3
     y_here, core = here >> 1, here & 1
     local = local_ref[...].reshape(128, 128).astype(BF)
     lanes, rows = iota((128, 512), 0), iota((128, 512), 0)
     n = iota((1, 512), 1)
-    shift = ((n >> 2) & 1) * 256 + (((n >> 1) & 1) ^ core) * 128
+    shift = ((n >> 2) & 1) * 128
+    same = ((n >> 1) & 1) == core
     for x in range(4):
         pick = onehot(lanes == (x ^ x_here) * 32 + (n & 3) * 8 + y_here)
         found = dot(local, pick)
@@ -138,18 +139,17 @@
             y = (part & 1) * 4 + (n >> 7)
             near = rows == y * 16 + turned_bits((n >> 3) & 15)
             spot = jnp.sum(jnp.where(near, found, 0.0), axis=0, keepdims=True).astype(I32)
-            spots_ref[part : part + 1, :] = spot + shift
-
-
-def total_body(spots_ref, got_ref, own_ref, sib_ref):
-    acc = jnp.zeros((512, 128), F32)
-    for y in range(8):
-        hit = onehot(iota((512, 512), 0) == spots_ref[y : y + 1, :])
-        acc += dot(hit, got_ref[y * 512 : (y + 1) * 512, :])
-    own_ref[:, :128] = acc[0:128]
-    own_ref[:, 128:] = acc[256:384]
-    sib_ref[:, :128] = acc[128:256]
-    sib_ref[:, 128:] = acc[384:512]
+            own_ref[part : part + 1, :] = jnp.where(same, spot + shift, -1)
+            sib_ref[part : part + 1, :] = jnp.where(same, -1, spot + shift)
+
+
+def total_body(spots_ref, got_ref, out_ref):
+    acc = jnp.zeros((256, 128), F32)
+    for part in range(8):
+        hit = onehot(iota((256, 512), 0) == spots_ref[part : part + 1, :])
+        acc += dot(hit, got_ref[part * 512 : (part + 1) * 512, :])
+    out_ref[:, :128] = acc[:128]
+    out_ref[:, 128:] = acc[128:]
 
 
 def adam_body(own_ref, sib_ref, moment_ref, second_ref, new_moment_ref, new_second_ref, head_ref, tail_ref):
@@ -272,13 +272,10 @@
         other = lax.ppermute(local, mp, [(i, i ^ bit) for i in range(64)])
         local = jnp.where((lanes & (32 * bit)) != 0, other, local)
     local = lax.all_gather(local, rep, axis=0, tiled=False, axis_index_groups=same_core)
-    (spots,) = call(spots_body, [shape((8, 512), I32)], local)
-    own, sib = call(
-        total_body,
-        [shape((128, 256), F32), shape((128, 256), F32)],
-        spots,
-        got.reshape(4096, 128),
-    )
+    spots = call(spots_body, [shape((8, 512), I32)] * 2, local)
+    got = got.reshape(4096, 128)
+    (sib,) = call(total_body, [shape((128, 256), F32)], spots[1], got)
+    (own,) = call(total_body, [shape((128, 256), F32)], spots[0], got)
     sib = lax.ppermute(sib, rep, other_core)
     new_moment, new_second, head, tail = call(
         adam_body,

time: 149 us -> 149 us (level)
    unnamed x15 -> x17, local copies, waits for them, and re-layouts: 3.05 us -> 4.01 us
    pallas_call x5 -> x6, Pallas kernels: 9.81 us -> 9.01 us  [call(): pl.pallas_call(body, out_shape=outs, in_specs=specs, out_specs=[pl.BlockS...]
where the time goes in v9:
time: 149 us; the launch traced here: 148 us
  starting transfers between devices  60.6 us (41%)
  blocking collectives  40.5 us (27%)
  waiting for transfers between devices  27.9 us (19%)
  Pallas kernels  11.5 us (8%)
  local copies, waits for them, and re-layouts  4.01 us (3%)
  matrix products  2.6 us (2%)
    all_to_all x1, starting transfers between devices, on_device(): lax.all_to_all(send.reshape(512, 8, 128), (rep, mp), split_axis=0, concat...  23.9 us
    all_gather x1, blocking collectives, on_device(): lax.all_gather(local, rep, axis=0, tiled=False, axis_index_groups=same_core)  20.3 us
    all_gather x1, blocking collectives, on_device(): heads = lax.all_gather(head, rep, axis=0, tiled=False)  20.2 us
    all_to_all x1, starting transfers between devices, on_device(): lax.all_to_all(local.reshape(16, 1, 128), mp, split_axis=0, concat_axis=0...  19.4 us
    all_to_all x1, waiting for transfers between devices, on_device(): lax.all_to_all(send.reshape(512, 8, 128), (rep, mp), split_axis=0, concat...  17.4 us
    pallas_call x6, Pallas kernels, call(): pl.pallas_call(body, out_shape=outs, in_specs=specs, out_specs=[pl.BlockS...  9.01 us
    ppermute x1, starting transfers between devices, on_device(): sib = lax.ppermute(sib, rep, other_core)  6.7 us
    ppermute x2, waiting for transfers between devices, on_device(): other = lax.ppermute(local, mp, [(i, i ^ bit) for i in range(64)])  5.64 us
  transfers between devices with their start and end apart: 6, of which 5 were waited for; matrix products, arithmetic and copies ran while one was open for 3% of the time, Pallas kernels for 2%

profile of v9, /device:TPU:1, one launch (start us, length us, event | category | flops | bytes accessed | tf_op | source)
XLA Modules:
  0.0 148.1 jit_solution(14639954401281422067)
XLA Ops:
  0.6 0.0 copy-start
  0.6 0.0 copy-start.2
  0.7 1.2 copy-done.2
  1.8 0.7 copy-done.4
  2.5 4.6 %shard_map.121 = (s32[8,256]{1,0:T(8,128)S(1)}, f32[16,128]{1,0:T(8,128)}) custom-call(s32[4,2,256]{2,1,0:T(2,128)S(1)} %bitcast.23, s32[1024,128]{1,0:T(8,128)S(1)} %bitcast.21), custom_call_target="tpu_custom_call" | custom-call | tf_op jit(solution)/shard_map/pallas_call | solution.py:44
  7.1 19.4 %all-to-all-start = ((f32[16,1,128]{2,1,0:T(1,128)}), f32[16,1,128]{2,1,0:T(1,128)S(1)}, u32[]{:S(2)}, u32[]{:S(2)}) async-start(f32[16,1,128]{2,1,0:T(1,128)} %bitcast.3), calls=%async_computation | async-start | bytes 16384 | tf_op jit(solution)/shard_map/all_to_all | solution.py:250
  26.5 1.1 copy.14
  27.7 0.0 copy-start.6
  27.7 0.0 copy-start.7
  27.7 1.7 %multiply_reduce_fusion = (f32[256]{0:T(256)S(1)}, f32[256,1024]{1,0:T(8,128)S(1)}) fusion(f32[1024]{0:T(1024)} %param.16, f32[1024]{0:T(1024)} %param.15, bf16[256,1024]{1,0:T(8,128)(2,1)S(1)} %bitcast.26, bf16[1024,1024]{1,0:T(8,128)(2,1)S(1)} %copy-done), kind=kOutput, calls=%fused_computation.3 | convolution fusion | flops 538705664 | bytes 3679232 | tf_op jit(solution)/shard_map/dot_general | solution.py:201
  29.4 0.9 convolution_convert_fusion.grads_ref
  30.4 1.8 %shard_map.122 = bf16[4096,128]{1,0:T(8,128)(2,1)S(1)} custom-call(s32[8,256]{1,0:T(8,128)S(1)} %get-tuple-element.13.slot_ref, bf16[256,1024]{1,0:T(8,128)(2,1)S(1)} %convolution_convert_fusion.grads_ref), custom_call_target="tpu_custom_call" | custom-call | tf_op jit(solution)/shard_map/pallas_call | solution.py:44
  32.1 0.0 copy-start.1
  32.1 1.0 copy-done.1
  33.1 4.7 %all-to-all-done = f32[16,1,128]{2,1,0:T(1,128)S(1)} async-done(((f32[16,1,128]{2,1,0:T(1,128)}), f32[16,1,128]{2,1,0:T(1,128)S(1)}, u32[]{:S(2)}, u32[]{:S(2)}) %all-to-all-start) | async-done | bytes 8224 | tf_op jit(solution)/shard_map/all_to_all | solution.py:250
  37.8 23.9 %all-to-all-start.1 = ((bf16[512,8,128]{2,1,0:T(8,128)(2,1)}), bf16[512,8,128]{2,1,0:T(8,128)(2,1)S(1)}, u32[]{:S(2)}, u32[]{:S(2)}) async-start(bf16[512,8,128]{2,1,0:T(8,128)(2,1)} %bitcast.19), calls=%async_computation.1 | async-start | bytes 2097152 | tf_op jit(solution)/shard_map/all_to_all | solution.py:261
  61.7 1.9 %collective-permute-start = (f32[16,128]{1,0:T(8,128)S(1)}, f32[16,128]{1,0:T(8,128)S(1)}, u32[]{:S(2)}, u32[]{:S(2)}) collective-permute-start(f32[16,128]{1,0:T(8,128)S(1)} %bitcast.27), channel_id=1, source_target_pairs={{0,1},{1,0},{2,3},{3,2},{4,5},{5,4},{6,7},{7,6},{8,9},{9,8},{10,11... | collective-permute-start | bytes 24584 | tf_op jit(solution)/shard_map/ppermute | solution.py:272
  63.6 2.8 %collective-permute-done = f32[16,128]{1,0:T(8,128)S(1)} collective-permute-done((f32[16,128]{1,0:T(8,128)S(1)}, f32[16,128]{1,0:T(8,128)S(1)}, u32[]{:S(2)}, u32[]{:S(2)}) %collective-permute-start) | collective-permute-done | bytes 8224 | tf_op jit(solution)/shard_map/ppermute | solution.py:272
  66.4 3.3 %collective-permute-start.1 = (f32[16,128]{1,0:T(8,128)S(1)}, f32[16,128]{1,0:T(8,128)S(1)}, u32[]{:S(2)}, u32[]{:S(2)}) collective-permute-start(f32[16,128]{1,0:T(8,128)S(1)} %broadcast_select_fusion), channel_id=1, source_target_pairs={{0,2},{1,3},{2,0},{3,1},{4,6},{5,7},{6,4},{7,5},{8,10},{9,11},{10,... | collective-permute-start | bytes 24584 | tf_op jit(solution)/shard_map/ppermute | solution.py:272
  69.7 2.9 %collective-permute-done.1 = f32[16,128]{1,0:T(8,128)S(1)} collective-permute-done((f32[16,128]{1,0:T(8,128)S(1)}, f32[16,128]{1,0:T(8,128)S(1)}, u32[]{:S(2)}, u32[]{:S(2)}) %collective-permute-start.1) | collective-permute-done | bytes 8224 | tf_op jit(solution)/shard_map/ppermute | solution.py:272
  72.6 20.3 %all-gather = f32[128,128]{1,0:T(8,128)S(1)} all-gather(f32[16,128]{1,0:T(8,128)S(1)} %broadcast_select_fusion.1), channel_id=2, replica_groups={{0,128,256,384,512,640,768,896},{64,192,320,448,576,704,832,960},{1,129..., dimensions={0}, use_global_device_ids=true | all-gather | bytes 73728 | tf_op jit(solution)/shard_map/all_gather | solution.py:274
  92.8 0.5 shard_map.123
  93.3 17.4 %all-to-all-done.1 = bf16[512,8,128]{2,1,0:T(8,128)(2,1)S(1)} async-done(((bf16[512,8,128]{2,1,0:T(8,128)(2,1)}), bf16[512,8,128]{2,1,0:T(8,128)(2,1)S(1)}, u32[]{:S(2)}, u32[]{:S(2)}) %all-to-all-start.1) | async-done | bytes 1048608 | tf_op jit(solution)/shard_map/all_to_all | solution.py:261
  110.7 0.7 shard_map.125
  111.4 6.7 %collective-permute-start.2 = (f32[128,256]{1,0:T(8,128)S(1)}, f32[128,256]{1,0:T(8,128)S(1)}, u32[]{:S(2)}, u32[]{:S(2)}) collective-permute-start(f32[128,256]{1,0:T(8,128)S(1)} %shard_map.125), channel_id=1, source_target_pairs={{0,64},{64,0},{128,192},{192,128},{256,320},{320,256},{384,448},{4... | collective-permute-start | bytes 393224 | tf_op jit(solution)/shard_map/ppermute | solution.py:279
  118.1 0.7 shard_map.124.own_ref
  118.8 0.3 collective-permute-done.2.sib_ref
  119.1 0.8 shard_map.126
  119.9 5.4 %all-to-all-start.2 = ((bf16[16,16,256]{2,1,0:T(8,128)(2,1)}), bf16[16,16,256]{2,1,0:T(8,128)(2,1)S(1)}, u32[]{:S(2)}, u32[]{:S(2)}) async-start(bf16[16,16,256]{2,1,0:T(8,128)(2,1)} %get-tuple-element.20), calls=%async_computation.2 | async-start | bytes 262144 | tf_op jit(solution)/shard_map/all_to_all | solution.py:293
  125.3 20.2 %all-gather.1 = bf16[1792,256]{1,0:T(8,128)(2,1)S(1)} all-gather(bf16[112,256]{1,0:T(8,128)(2,1)S(1)} %get-tuple-element.19), channel_id=3, replica_groups=mesh['replica'=16,'mp'=64] {'replica'}, dimensions={0}, use_global_device_ids=true | all-gather | bytes 974848 | tf_op jit(solution)/shard_map/all_gather | solution.py:294
  145.5 0.0 all-to-all-done.2.tail_ref
  145.5 2.5 %shard_map.127 = f32[2048,256]{1,0:T(8,128)} custom-call(bf16[16,112,256]{2,1,0:T(8,128)(2,1)S(1)} %bitcast.20, bf16[16,16,256]{2,1,0:T(8,128)(2,1)S(1)} %all-to-all-done.2.tail_ref, f32[2048,256]{1,0:T(8,128)} %table_ref.1), custom_call_target="tpu_custom_call" | custom-call | tf_op jit(solution)/shard_map/pallas_call | solution.py:296
  (13 shorter events, 0.0 us)
Async XLA Ops:
  0.6 27.0 %copy-start = (bf16[1024,1024]{1,0:T(8,128)(2,1)S(1)}, bf16[1024,1024]{1,0:T(8,128)(2,1)}, u32[]{:S(2)}) copy-start(bf16[1024,1024]{1,0:T(8,128)(2,1)} %param.14) | copy-start | bytes 6291460
  0.6 1.2 copy-start.2
  1.8 0.7 copy-start.4
  7.1 30.6 %all-to-all-start = ((f32[16,1,128]{2,1,0:T(1,128)}), f32[16,1,128]{2,1,0:T(1,128)S(1)}, u32[]{:S(2)}, u32[]{:S(2)}) async-start(f32[16,1,128]{2,1,0:T(1,128)} %bitcast.3), calls=%async_computation | async-start | bytes 16384 | tf_op jit(solution)/shard_map/all_to_all | solution.py:250
  27.7 1.7 %copy-start.6 = (s32[256]{0:T(256)S(1)}, s32[256]{0:T(256)}, u32[]{:S(2)}) copy-start(s32[256]{0:T(256)} %param.12) | copy-start | bytes 3076
  27.7 1.7 %copy-start.7 = (f32[1024]{0:T(1024)S(1)}, f32[1024]{0:T(1024)}, u32[]{:S(2)}) copy-start(f32[1024]{0:T(1024)} %param.16) | copy-start | bytes 12292
  32.1 1.0 copy-start.1
  37.8 81.3 %copy-start.3 = (f32[128,256]{1,0:T(8,128)S(1)}, f32[128,256]{1,0:T(8,128)}, u32[]{:S(2)}) copy-start(f32[128,256]{1,0:T(8,128)} %moment_ref.1) | copy-start | bytes 393220
  37.8 81.3 %copy-start.5 = (f32[128]{0:T(128)S(1)}, f32[128]{0:T(128)}, u32[]{:S(2)}) copy-start(f32[128]{0:T(128)} %param.19) | copy-start | bytes 1540
  37.8 72.9 %all-to-all-start.1 = ((bf16[512,8,128]{2,1,0:T(8,128)(2,1)}), bf16[512,8,128]{2,1,0:T(8,128)(2,1)S(1)}, u32[]{:S(2)}, u32[]{:S(2)}) async-start(bf16[512,8,128]{2,1,0:T(8,128)(2,1)} %bitcast.19), calls=%async_computation.1 | async-start | bytes 2097152 | tf_op jit(solution)/shard_map/all_to_all | solution.py:261
  61.7 4.7 %collective-permute-start = (f32[16,128]{1,0:T(8,128)S(1)}, f32[16,128]{1,0:T(8,128)S(1)}, u32[]{:S(2)}, u32[]{:S(2)}) collective-permute-start(f32[16,128]{1,0:T(8,128)S(1)} %bitcast.27), channel_id=1, source_target_pairs={{0,1},{1,0},{2,3},{3,2},{4,5},{5,4},{6,7},{7,6},{8,9},{9,8},{10,11... | collective-permute-start | bytes 24584 | tf_op jit(solution)/shard_map/ppermute | solution.py:272
  66.4 6.2 %collective-permute-start.1 = (f32[16,128]{1,0:T(8,128)S(1)}, f32[16,128]{1,0:T(8,128)S(1)}, u32[]{:S(2)}, u32[]{:S(2)}) collective-permute-start(f32[16,128]{1,0:T(8,128)S(1)} %broadcast_select_fusion), channel_id=1, source_target_pairs={{0,2},{1,3},{2,0},{3,1},{4,6},{5,7},{6,4},{7,5},{8,10},{9,11},{10,... | collective-permute-start | bytes 24584 | tf_op jit(solution)/shard_map/ppermute | solution.py:272
  111.4 7.7 %collective-permute-start.2 = (f32[128,256]{1,0:T(8,128)S(1)}, f32[128,256]{1,0:T(8,128)S(1)}, u32[]{:S(2)}, u32[]{:S(2)}) collective-permute-start(f32[128,256]{1,0:T(8,128)S(1)} %shard_map.125), channel_id=1, source_target_pairs={{0,64},{64,0},{128,192},{192,128},{256,320},{320,256},{384,448},{4... | collective-permute-start | bytes 393224 | tf_op jit(solution)/shard_map/ppermute | solution.py:279
  119.9 25.6 %all-to-all-start.2 = ((bf16[16,16,256]{2,1,0:T(8,128)(2,1)}), bf16[16,16,256]{2,1,0:T(8,128)(2,1)S(1)}, u32[]{:S(2)}, u32[]{:S(2)}) async-start(bf16[16,16,256]{2,1,0:T(8,128)(2,1)} %get-tuple-element.20), calls=%async_computation.2 | async-start | bytes 262144 | tf_op jit(solution)/shard_map/all_to_all | solution.py:293
